TPU v7x, 512 devices: a whole 4x4x16 slice. The times are simulated.
512 devices in a mesh: ens: 8 (over z_hi, y), space: 64 (over x, z_lo, core).
Axes of the slice: x: 4, y: 4, z: 16 (z_hi: 2, z_lo: 8; z = z_hi * 8 + z_lo), core: 2. Of those that a mesh axis runs over, the one named last changes fastest.
Arguments:
- node_states: bfloat16 [8, 8192, 1024], P('ens', 'space'), may hold values from -6 to 6
- query: bfloat16 [8, 8192, 512], P('ens', 'space'), may hold values from -240 to 240
- key: bfloat16 [8, 8192, 512], P('ens', 'space'), may hold values from -6 to 6
- value: bfloat16 [8, 8192, 512], P('ens', 'space'), may hold values from -6 to 6
- out_weight: bfloat16 [512, 1024], replicated, may hold values from -0.25 to 0.25
- dec_weight: bfloat16 [100, 1024], replicated, may hold values from -0.1875 to 0.1875
- target: float32 [100, 65536], P(None, 'space'), may hold values from -6 to 6
- area_weight: float32 [65536], P('space'), may hold values from 0.25 to 2.5
- var_weight: float32 [100], replicated, may hold values from 0.5 to 5
- edges: int32 [3, 65536], P(None, 'space'), may hold values from 0 to 8191, as said below
- edge_weight: float32 [3, 65536], P(None, 'space'), may hold values from 0.1 to 0.6
- windows: int32 [2, 64], P(None, 'space'), may hold values from 0 to 8192, as said below
Outputs:
- grad_states: bfloat16 [8, 8192, 1024], P('ens', 'space')
- grad_query: bfloat16 [8, 8192, 512], P('ens', 'space')
- grad_key: bfloat16 [8, 8192, 512], P('ens', 'space')
- grad_value: bfloat16 [8, 8192, 512], P('ens', 'space')
- grad_wo: float32 [512, 1024], P('space')
- grad_dec: float32 [100, 1024], replicated
Inputs may be any that keep to these rules, and one draw needn't show every extreme that they name: The edges of a point among the 1024 points p with p // 1024 = d name nodes from d * 128 - 128 to d * 128 + 2 * 128 - 1; both ends are named in every draw. For the block b of nodes s = b * 128 to s + 127: max(0, s - 128) <= windows[0, b] <= s and s + 128 <= windows[1, b] <= min(8192, s + 256); the outer ends s - 128 and s + 256 are reached by some block in every draw.
All inputs are finite; a program needn't handle non-finite values.
Results may differ from a plain program's by a relative error of at most 0.017.
Values may be sent and summed in bfloat16 or wider, within the bound.
No kernel may reach another device: no remote copies, remote signals or barrier semaphores. Data moves between devices by JAX's collectives and lax.ppermute only.
A program may use at most 64 MiB of HBM per device.

v0:
```python
import math

import jax
import jax.numpy as jnp
from jax import lax
from jax.sharding import PartitionSpec as P

HEADS = 8
HEAD_DIM = 64
BLOCK = 128


SMOOTH_SQUARE = 0.0625
MASKED_SCORE = -1e30


def extended(block, sides, width):
    for axis, dim in sides:
        count = lax.axis_size(axis)
        forward = [(i, i + 1) for i in range(count - 1)]
        backward = [(target, source) for source, target in forward]
        low = lax.ppermute(
            lax.slice_in_dim(block, block.shape[dim] - width, None, axis=dim), axis, forward
        )
        high = lax.ppermute(lax.slice_in_dim(block, 0, width, axis=dim), axis, backward)
        block = jnp.concatenate([low, block, high], axis=dim)
    return block


def shifted(block, axis, distance):
    devices = range(lax.axis_size(axis))
    route = [(i - distance, i) for i in devices if i - distance in devices]
    return lax.ppermute(block, axis, route)


def together(arrays, axis):
    flat, at, outs = (jnp.concatenate([a.reshape(-1) for a in arrays]), 0, [])
    total = lax.psum(flat, axis)
    for a in arrays:
        outs.append(total[at : at + a.size].reshape(a.shape))
        at += a.size
    return tuple(outs)


def smooth_slope(diff_value):
    return diff_value * lax.rsqrt(diff_value * diff_value + SMOOTH_SQUARE)


def per_device(
    node_states,
    query,
    key,
    value,
    out_weight,
    dec_weight,
    target,
    area_weight,
    var_weight,
    edges,
    edge_weight,
    windows,
):
    states = node_states[0]
    node_count = states.shape[0]
    width = states.shape[1]
    point_count = target.shape[1]
    members = lax.axis_size("ens")
    band_index = lax.axis_index("space")
    first_node = band_index * node_count
    states_ext = extended(states, (("space", 0),), node_count)
    local_edges = edges - (first_node - node_count)
    latent_sum = jnp.zeros((point_count, width), jnp.float32)
    for edge_slot in range(edges.shape[0]):
        latent_sum = latent_sum + edge_weight[edge_slot][:, None] * jnp.take(
            states_ext, local_edges[edge_slot], axis=0
        ).astype(jnp.float32)
    latent = latent_sum.astype(jnp.bfloat16)
    prediction = lax.dot_general(
        dec_weight, latent, (((1,), (1,)), ((), ())), preferred_element_type=jnp.float32
    ).astype(jnp.bfloat16)
    weights = area_weight[None, :] * var_weight[:, None]
    sub_points = point_count // members
    member_values = lax.all_to_all(
        prediction[None], "ens", split_axis=2, concat_axis=0, tiled=True
    ).astype(jnp.float32)
    offset_start = lax.axis_index("ens") * sub_points
    part_target = lax.dynamic_slice_in_dim(target, offset_start, sub_points, 1)
    part_weights = lax.dynamic_slice_in_dim(weights, offset_start, sub_points, 1)
    pair_sum = jnp.sum(smooth_slope(member_values[:, None] - member_values[None, :]), axis=1)
    slopes = smooth_slope(member_values - part_target[None]) - pair_sum / (members - 1)
    grad_slices = (part_weights[None] * slopes).astype(jnp.bfloat16)
    grad_prediction = lax.all_to_all(grad_slices, "ens", split_axis=0, concat_axis=2, tiled=True)[0]
    grad_latent = lax.dot_general(
        grad_prediction, dec_weight, (((0,), (0,)), ((), ())), preferred_element_type=jnp.float32
    )
    dec_term = lax.dot_general(
        grad_prediction, latent, (((1,), (0,)), ((), ())), preferred_element_type=jnp.float32
    )
    node_sum = jnp.zeros((3 * node_count, width), jnp.float32)
    for edge_slot in range(edges.shape[0]):
        node_sum = node_sum.at[local_edges[edge_slot]].add(
            edge_weight[edge_slot][:, None] * grad_latent
        )
    owned = node_sum[node_count : 2 * node_count]
    for step_by, border in ((1, node_sum[2 * node_count :]), (-1, node_sum[:node_count])):
        owned = owned + shifted(border, "space", step_by)
    grad_states = owned.astype(jnp.bfloat16)
    paired = jnp.stack([key[0], value[0]])
    paired_ext = extended(paired, (("space", 1),), node_count)
    score_scale = 1.0 / math.sqrt(HEAD_DIM)
    query_heads = query[0].reshape(node_count, HEADS, HEAD_DIM)
    key_heads = paired_ext[0].reshape(3 * node_count, HEADS, HEAD_DIM)
    value_heads = paired_ext[1].reshape(3 * node_count, HEADS, HEAD_DIM)
    block_count = windows.shape[1]
    lower_rows = jnp.broadcast_to(windows[0][:, None], (block_count, BLOCK)).reshape(-1)
    upper_rows = jnp.broadcast_to(windows[1][:, None], (block_count, BLOCK)).reshape(-1)
    key_place = first_node - node_count + jnp.arange(3 * node_count, dtype=jnp.int32)
    inside = (key_place[None, :] >= lower_rows[:, None]) & (
        key_place[None, :] < upper_rows[:, None]
    )
    scores = (
        jnp.einsum("qhc,khc->hqk", query_heads, key_heads, preferred_element_type=jnp.float32)
        * score_scale
    )
    scores = jnp.where(inside[None], scores, MASKED_SCORE)
    row_max = jnp.max(scores, axis=-1, keepdims=True)
    exponent = jnp.exp(scores - row_max)
    attn_prob = exponent / jnp.sum(exponent, axis=-1, keepdims=True)
    prob_low = attn_prob.astype(jnp.bfloat16)
    attn_out = (
        jnp.einsum("hqk,khc->qhc", prob_low, value_heads, preferred_element_type=jnp.float32)
        .reshape(node_count, -1)
        .astype(jnp.bfloat16)
    )
    grad_out = lax.dot_general(
        grad_states, out_weight, (((1,), (1,)), ((), ())), preferred_element_type=jnp.float32
    ).astype(jnp.bfloat16)
    grad_heads = grad_out.reshape(node_count, HEADS, HEAD_DIM)
    value_term = jnp.einsum(
        "hqk,qhc->khc", prob_low, grad_heads, preferred_element_type=jnp.float32
    ).reshape(3 * node_count, -1)
    grad_prob = jnp.einsum(
        "qhc,khc->hqk", grad_heads, value_heads, preferred_element_type=jnp.float32
    )
    row_delta = jnp.sum(attn_prob * grad_prob, axis=-1, keepdims=True)
    grad_scores = (attn_prob * (grad_prob - row_delta)).astype(jnp.bfloat16)
    grad_query = (
        (
            jnp.einsum("hqk,khc->qhc", grad_scores, key_heads, preferred_element_type=jnp.float32)
            * score_scale
        )
        .reshape(node_count, -1)
        .astype(jnp.bfloat16)
    )
    key_term = (
        jnp.einsum("hqk,qhc->khc", grad_scores, query_heads, preferred_element_type=jnp.float32)
        * score_scale
    ).reshape(3 * node_count, -1)
    both_terms = jnp.stack([key_term, value_term])
    owned_terms = both_terms[:, node_count : 2 * node_count]
    for step_by, border in ((1, both_terms[:, 2 * node_count :]), (-1, both_terms[:, :node_count])):
        owned_terms = owned_terms + shifted(border.astype(jnp.bfloat16), "space", step_by).astype(
            border.dtype
        )
    grad_key = owned_terms[0].astype(jnp.bfloat16)
    grad_value = owned_terms[1].astype(jnp.bfloat16)
    row_count = attn_out.shape[1] // lax.axis_size("space")
    wo_term = lax.dot_general(
        attn_out, grad_states, (((0,), (0,)), ((), ())), preferred_element_type=jnp.float32
    )
    wo_total, grad_dec = together((wo_term, dec_term), ("ens", "space"))
    grad_wo = lax.dynamic_slice_in_dim(wo_total, band_index * row_count, row_count, 0)
    return (
        grad_states[None],
        grad_query[None],
        grad_key[None],
        grad_value[None],
        grad_wo,
        grad_dec,
    )


def solution(mesh):
    in_specs = (
        P("ens", "space", None),
        P("ens", "space", None),
        P("ens", "space", None),
        P("ens", "space", None),
        P(),
        P(),
        P(None, "space"),
        P("space"),
        P(),
        P(None, "space"),
        P(None, "space"),
        P(None, "space"),
    )
    out_specs = (
        P("ens", "space", None),
        P("ens", "space", None),
        P("ens", "space", None),
        P("ens", "space", None),
        P("space", None),
        P(),
    )
    return jax.shard_map(
        per_device, mesh=mesh, in_specs=in_specs, out_specs=out_specs, check_vma=False
    )
```

profile of v0, /device:TPU:1, one launch (start us, length us, event | category | flops | bytes accessed | tf_op | source)
XLA Modules:
  0.0 687.1 jit_solution(11359500251764939703)
XLA Ops:
  7.2 5.1 collective-permute-start
  12.3 5.2 collective-permute-start.1
  21.2 5.4 gather_fusion
  26.6 5.4 gather_fusion.1
  31.9 5.4 gather_fusion.2
  37.3 4.5 add_convert_fusion
  44.2 3.1 reduce
  48.8 16.5 %all-to-all-start = ((bf16[8,2,6400]{2,1,0:T(2,128)(2,1)}), bf16[8,2,6400]{2,1,0:T(2,128)(2,1)S(1)}, u32[]{:S(2)}, u32[]{:S(2)}) async-start(bf16[8,2,6400]{2,1,0:T(2,128)(2,1)} %reshape.258), calls=%async_computation | async-start | bytes 409600 | tf_op jit(solution)/shard_map/all_to_all | solution.py:83
  69.7 2.9 collective-permute-start.5
  76.9 5.3 all-to-all-done
  89.1 8.6 %all-to-all-start.1 = ((bf16[8,100,128]{2,1,0:T(8,128)(2,1)}), bf16[8,100,128]{2,1,0:T(8,128)(2,1)}, u32[]{:S(2)}, u32[]{:S(2)}) async-start(bf16[8,100,128]{2,1,0:T(8,128)(2,1)} %multiply_convert_fusion.1), calls=%async_computation.1 | async-start | bytes 425984 | tf_op jit(solution)/shard_map/all_to_all | solution.py:92
  105.3 2.8 fusion.54
  108.1 7.0 %all-to-all-done.1 = bf16[8,100,128]{2,1,0:T(8,128)(2,1)} async-done(((bf16[8,100,128]{2,1,0:T(8,128)(2,1)}), bf16[8,100,128]{2,1,0:T(8,128)(2,1)}, u32[]{:S(2)}, u32[]{:S(2)}) %all-to-all-start.1) | async-done | bytes 204832 | tf_op jit(solution)/shard_map/all_to_all | solution.py:92
  116.2 3.7 fusion.55
  119.9 11.5 %scatter_custom_fusion = f32[384,1024]{1,0:T(8,128)} fusion(s32[1024]{0:T(1024)} %bitcast.148, f32[1024,1024]{1,0:T(8,128)} %fusion.55, f32[1024]{0:T(1024)S(1)} %bitcast.145, f32[]{:T(128)} %constant.24.clone.1), kind=kCustom, calls=%fused_computation.13 | custom fusion | flops 2097152 | bytes 5771776 | tf_op jit(solution)/shard_map/scatter-add | solution.py:101
  131.4 12.8 %scatter_custom_fusion.1 = f32[384,1024]{1,0:T(8,128)} fusion(f32[384,1024]{1,0:T(8,128)} %scatter_custom_fusion, s32[1024]{0:T(1024)} %bitcast.147, f32[1024,1024]{1,0:T(8,128)} %fusion.55, f32[1024]{0:T(1024)S(1)} %bitcast.137), kind=kCustom, calls=%fused_computation.11 | custom fusion | flops 2097152 | bytes 5771264 | tf_op jit(solution)/shard_map/scatter-add | solution.py:101
  144.3 12.8 %scatter_custom_fusion.2 = f32[384,1024]{1,0:T(8,128)} fusion(f32[384,1024]{1,0:T(8,128)} %scatter_custom_fusion.1, s32[1024]{0:T(1024)} %bitcast.146, f32[1024,1024]{1,0:T(8,128)} %fusion.55, f32[1024]{0:T(1024)S(1)} %bitcast.135), kind=kCustom, calls=%fused_computation.9 | custom fusion | flops 2097152 | bytes 5771264 | tf_op jit(solution)/shard_map/scatter-add | solution.py:101
  159.4 6.0 collective-permute-start.2
  167.6 2.7 convolution_convert_fusion.1
  172.7 3.8 collective-permute-done.3
  181.2 3.0 fusion.29
  193.1 3.1 collective-permute-start.7
  198.3 2.8 collective-permute-done.7
  202.9 472.0 %all-reduce.2.cloned.1.call-done = f32[626688]{0:T(1024)} async-done(((f32[626688]{0:T(1024)}), f32[626688]{0:T(1024)}) %all-reduce.2.cloned.1.call-update) | async-done | bytes 2506768 | tf_op jit(solution)/shard_map/psum | solution.py:38
  (109 shorter events, 61.2 us)
Async XLA Ops:
  7.2 173.4 %copy-start = (bf16[512,1024]{1,0:T(8,128)(2,1)S(1)}, bf16[512,1024]{1,0:T(8,128)(2,1)}, u32[]{:S(2)}) copy-start(bf16[512,1024]{1,0:T(8,128)(2,1)} %param.18) | copy-start | bytes 3145732
  7.2 11.9 %collective-permute-start = (bf16[128,1024]{1,0:T(8,128)(2,1)}, bf16[128,1024]{1,0:T(8,128)(2,1)S(1)}, u32[]{:S(2)}, u32[]{:S(2)}) collective-permute-start(bf16[128,1024]{1,0:T(8,128)(2,1)} %bitcast.128), channel_id=1, source_target_pairs={{0,1},{1,2},{2,3},{3,4},{4,5},{5,6},{6,7},{7,8},{8,9},{9,10},{10,1... | collective-permute-start | bytes 786440 | tf_op jit(solution)/shard_map/ppermute | solution.py:22
  12.3 7.9 %collective-permute-start.1 = (bf16[128,1024]{1,0:T(8,128)(2,1)}, bf16[128,1024]{1,0:T(8,128)(2,1)S(1)}, u32[]{:S(2)}, u32[]{:S(2)}) collective-permute-start(bf16[128,1024]{1,0:T(8,128)(2,1)} %bitcast.129), channel_id=1, source_target_pairs={{1,0},{2,1},{3,2},{4,3},{5,4},{6,5},{7,6},{8,7},{9,8},{10,9},{11,1... | collective-permute-start | bytes 786440 | tf_op jit(solution)/shard_map/ppermute | solution.py:25
  19.1 18.2 %copy-start.13 = (f32[1,1024]{1,0:T(1,128)}, f32[1,1024]{1,0:T(1,128)S(1)}, u32[]{:S(2)}) copy-start(f32[1,1024]{1,0:T(1,128)S(1)} %get-tuple-element.55) | copy-start | bytes 12292
  19.1 18.2 %copy-start.15 = (f32[1,1024]{1,0:T(1,128)}, f32[1,1024]{1,0:T(1,128)S(1)}, u32[]{:S(2)}) copy-start(f32[1,1024]{1,0:T(1,128)S(1)} %get-tuple-element.56) | copy-start | bytes 12292
  19.1 18.2 %copy-start.17 = (f32[1,1024]{1,0:T(1,128)}, f32[1,1024]{1,0:T(1,128)S(1)}, u32[]{:S(2)}) copy-start(f32[1,1024]{1,0:T(1,128)S(1)} %get-tuple-element.54) | copy-start | bytes 12292
  37.3 4.5 copy-start.5
  41.8 23.5 %copy-start.10 = (bf16[1,128,512]{2,1,0:T(8,128)(2,1)S(1)}, bf16[1,128,512]{2,1,0:T(8,128)(2,1)}, u32[]{:S(2)}) copy-start(bf16[1,128,512]{2,1,0:T(8,128)(2,1)} %param.16) | copy-start | bytes 393220
  48.8 33.4 %all-to-all-start = ((bf16[8,2,6400]{2,1,0:T(2,128)(2,1)}), bf16[8,2,6400]{2,1,0:T(2,128)(2,1)S(1)}, u32[]{:S(2)}, u32[]{:S(2)}) async-start(bf16[8,2,6400]{2,1,0:T(2,128)(2,1)} %reshape.258), calls=%async_computation | async-start | bytes 409600 | tf_op jit(solution)/shard_map/all_to_all | solution.py:83
  67.6 32.4 %collective-permute-start.4 = (bf16[2,128,512]{2,1,0:T(8,128)(2,1)}, bf16[2,128,512]{2,1,0:T(8,128)(2,1)}, u32[]{:S(2)}, u32[]{:S(2)}) collective-permute-start(bf16[2,128,512]{2,1,0:T(8,128)(2,1)} %constant_dynamic-update-slice_fusion), channel_id=1, source_target_pairs={{0,1},{1,2},{2,3},{3,4},{4,5},{5,6},{6,7},{7,8},{8,9},{9,10},{10,1... | collective-permute-start | bytes 786440 | tf_op jit(solution)/shard_map/ppermute | solution.py:22
  69.7 30.3 %collective-permute-start.5 = (bf16[2,128,512]{2,1,0:T(8,128)(2,1)}, bf16[2,128,512]{2,1,0:T(8,128)(2,1)}, u32[]{:S(2)}, u32[]{:S(2)}) collective-permute-start(bf16[2,128,512]{2,1,0:T(8,128)(2,1)} %constant_dynamic-update-slice_fusion), channel_id=1, source_target_pairs={{1,0},{2,1},{3,2},{4,3},{5,4},{6,5},{7,6},{8,7},{9,8},{10,9},{11,1... | collective-permute-start | bytes 786440 | tf_op jit(solution)/shard_map/ppermute | solution.py:25
  86.8 12.4 %copy-start.11 = (bf16[1,128,512]{2,1,0:T(8,128)(2,1)S(1)}, bf16[1,128,512]{2,1,0:T(8,128)(2,1)}, u32[]{:S(2)}) copy-start(bf16[1,128,512]{2,1,0:T(8,128)(2,1)} %param.15) | copy-start | bytes 393220
  89.1 26.0 %all-to-all-start.1 = ((bf16[8,100,128]{2,1,0:T(8,128)(2,1)}), bf16[8,100,128]{2,1,0:T(8,128)(2,1)}, u32[]{:S(2)}, u32[]{:S(2)}) async-start(bf16[8,100,128]{2,1,0:T(8,128)(2,1)} %multiply_convert_fusion.1), calls=%async_computation.1 | async-start | bytes 425984 | tf_op jit(solution)/shard_map/all_to_all | solution.py:92
  97.7 577.3 %all-reduce.2.cloned.1.call-start = ((), (), s32[]{:S(2)}) async-start(), calls=%async_computation.2 | async-start | bytes 5013504 | tf_op jit(solution)/shard_map/psum | solution.py:38
  103.3 12.9 %copy-start.2 = (bf16[1,384,512]{1,2,0:T(8,128)(2,1)}, bf16[1,384,512]{1,2,0:T(8,128)(2,1)S(1)}, u32[]{:S(2)}) copy-start(bf16[1,384,512]{1,2,0:T(8,128)(2,1)S(1)} %copy.110) | copy-start | bytes 1179652
  119.9 11.5 %copy-start.16 = (f32[1,1024]{1,0:T(1,128)S(1)}, f32[1,1024]{1,0:T(1,128)}, u32[]{:S(2)}) copy-start(f32[1,1024]{1,0:T(1,128)} %copy-done.15) | copy-start | bytes 12292
  131.4 12.8 %copy-start.14 = (f32[1,1024]{1,0:T(1,128)S(1)}, f32[1,1024]{1,0:T(1,128)}, u32[]{:S(2)}) copy-start(f32[1,1024]{1,0:T(1,128)} %copy-done.13) | copy-start | bytes 12292
  157.1 10.5 %copy-start.6 = (bf16[1,128,512]{1,2,0:T(8,128)(2,1)S(1)}, bf16[1,128,512]{1,2,0:T(8,128)(2,1)}, u32[]{:S(2)}) copy-start(bf16[1,128,512]{1,2,0:T(8,128)(2,1)} %copy.111) | copy-start | bytes 393220
  159.4 13.2 %collective-permute-start.2 = (f32[128,1024]{1,0:T(8,128)}, f32[128,1024]{1,0:T(8,128)}, u32[]{:S(2)}, u32[]{:S(2)}) collective-permute-start(f32[128,1024]{1,0:T(8,128)} %get-tuple-element.43), channel_id=1, source_target_pairs={{0,1},{1,2},{2,3},{3,4},{4,5},{5,6},{6,7},{7,8},{8,9},{9,10},{10,1... | collective-permute-start | bytes 1572872 | tf_op jit(solution)/shard_map/ppermute | solution.py:33
  165.4 11.0 %collective-permute-start.3 = (f32[128,1024]{1,0:T(8,128)}, f32[128,1024]{1,0:T(8,128)}, u32[]{:S(2)}, u32[]{:S(2)}) collective-permute-start(f32[128,1024]{1,0:T(8,128)} %get-tuple-element.44), channel_id=1, source_target_pairs={{1,0},{2,1},{3,2},{4,3},{5,4},{6,5},{7,6},{8,7},{9,8},{10,9},{11,1... | collective-permute-start | bytes 1572872 | tf_op jit(solution)/shard_map/ppermute | solution.py:33
  171.5 6.4 copy-start.9
  181.2 4.4 copy-start.3
  191.2 7.1 %collective-permute-start.6 = (bf16[2,128,512]{2,1,0:T(8,128)(2,1)}, bf16[2,128,512]{2,1,0:T(8,128)(2,1)}, u32[]{:S(2)}, u32[]{:S(2)}) collective-permute-start(bf16[2,128,512]{2,1,0:T(8,128)(2,1)} %get-tuple-element.45), channel_id=1, source_target_pairs={{0,1},{1,2},{2,3},{3,4},{4,5},{5,6},{6,7},{7,8},{8,9},{9,10},{10,1... | collective-permute-start | bytes 786440 | tf_op jit(solution)/shard_map/ppermute | solution.py:33
  193.1 8.0 %collective-permute-start.7 = (bf16[2,128,512]{2,1,0:T(8,128)(2,1)}, bf16[2,128,512]{2,1,0:T(8,128)(2,1)}, u32[]{:S(2)}, u32[]{:S(2)}) collective-permute-start(bf16[2,128,512]{2,1,0:T(8,128)(2,1)} %get-tuple-element.46), channel_id=1, source_target_pairs={{1,0},{2,1},{3,2},{4,3},{5,4},{6,5},{7,6},{8,7},{9,8},{10,9},{11,1... | collective-permute-start | bytes 786440 | tf_op jit(solution)/shard_map/ppermute | solution.py:33
  (8 other events, 17.8 us)
Sparse Core Ops, SparseCore 0:
  180.7 494.2 all-reduce.1
where the time goes:
time: 689 us; the launch traced here: 687 us
  waiting for transfers between devices  492 us (71%)
  other arithmetic  58.3 us (8%)
  starting transfers between devices  53.7 us (8%)
  local copies, waits for them, and re-layouts  49.1 us (7%)
  matrix products  19.3 us (3%)
  between operations  14.6 us (2%)
    psum x1, waiting for transfers between devices, together(): total = lax.psum(flat, axis)  472 us
    scatter-add x3, other arithmetic, per_device(): node_sum.at[local_edges[edge_slot]]  37.2 us
    all_to_all x1, starting transfers between devices, per_device(): lax.all_to_all(prediction[None], 'ens', split_axis=2, concat_axis=0, tile...  16.5 us
    gather x3, local copies, waits for them, and re-layouts, per_device(): jnp.take(states_ext, local_edges[edge_slot], axis=0).astype(jnp.float32)  16.1 us
  transfers between devices with their start and end apart: 11, of which 6 were waited for; matrix products, arithmetic and copies ran while one was open for 6% of the time, Pallas kernels for 0%

commit v1 on v0

v1 whole, which is shorter than its diff:
```python
import functools
import math

import jax
import jax.numpy as jnp
from jax import lax
from jax.experimental import pallas as pl
from jax.experimental.pallas import tpu as pltpu
from jax.sharding import Mesh
from jax.sharding import PartitionSpec as P

HEADS = 8
HEAD_DIM = 64
PAIR = 2 * HEAD_DIM
VARS = 100
VARS_SUB = 112
VARS_LANE = 128
MEMBERS = 8
NODES = 128
POINTS = 1024
SPAN = 3 * NODES
WIDTH = 1024
ATT = 512
SMOOTH_SQUARE = 0.0625
MASKED_SCORE = -1e30
SCALE = 1.0 / math.sqrt(HEAD_DIM)

AXES = ("zh", "y", "x", "zl", "c")
SIZES = (2, 4, 4, 8, 2)
ENS = ("zh", "y")
SPACE = ("x", "zl", "c")
NEAR = ("y", "x", "c")
NEAR_SIZE = 32
FAR = ("zh", "zl")
FAR_SIZE = 16
DEC_ROWS = WIDTH // NEAR_SIZE
WO_ROWS = ATT // NEAR_SIZE
ROWS = DEC_ROWS + WO_ROWS

F32 = jnp.float32
BF16 = jnp.bfloat16
NN = (((1,), (0,)), ((), ()))
NT = (((1,), (1,)), ((), ()))
TN = (((0,), (0,)), ((), ()))


def dot(a, b, dims):
    return lax.dot_general(a, b, dims, preferred_element_type=F32)


def call(body, out_shape, scratch=(), smem=(), flops=10**8, moved=10**6, exps=0, n_in=0):
    specs = [
        pl.BlockSpec(memory_space=pltpu.SMEM if i in smem else pltpu.VMEM) for i in range(n_in)
    ]
    return pl.pallas_call(
        body,
        out_shape=out_shape,
        in_specs=specs,
        scratch_shapes=list(scratch),
        compiler_params=pltpu.CompilerParams(vmem_limit_bytes=40 * 2**20),
        cost_estimate=pl.CostEstimate(flops=flops, bytes_accessed=moved, transcendentals=exps),
    )


def shape(dims, dtype):
    return jax.ShapeDtypeStruct(dims, dtype)


def smooth_slope(t):
    return t * lax.rsqrt(t * t + SMOOTH_SQUARE)


def split(x):
    high = x.astype(BF16)
    return high, (x - high.astype(F32)).astype(BF16)


def project_body(states_ref, dec_ref, key_ref, value_ref, proj_ref, kv_ref, dec_s):
    dec_s[...] = jnp.zeros(dec_s.shape, BF16)
    dec_s[0:VARS, :] = dec_ref[...]
    proj = dot(dec_s[...], states_ref[0], NT).astype(BF16)
    for member in range(MEMBERS):
        proj_ref[member] = proj
    kv_ref[:, 0:ATT] = key_ref[0]
    kv_ref[:, ATT : 2 * ATT] = value_ref[0]


def weights_body(band_ref, edges_ref, edge_weight_ref, area_ref, var_ref, mix_ref, weight_ref):
    base = (band_ref[0] - 1) * NODES
    local = edges_ref[...] - base
    for part in range(SPAN // NODES):
        place = lax.broadcasted_iota(jnp.int32, (NODES, POINTS), 0) + part * NODES
        mix = jnp.zeros((NODES, POINTS), F32)
        for slot in range(3):
            mix = mix + jnp.where(
                local[slot : slot + 1, :] == place, edge_weight_ref[slot : slot + 1, :], 0.0
            )
        mix_ref[part * NODES : (part + 1) * NODES, :] = mix.astype(BF16)
    row = jnp.concatenate([var_ref[...], jnp.zeros((1, VARS_LANE - VARS), F32)], axis=1)
    column = jnp.transpose(jnp.broadcast_to(row, (VARS_LANE, VARS_LANE)))[0:VARS_SUB, 0:1]
    weight_ref[...] = column * area_ref[...]


def crps_body(
    member_ref,
    low_ref,
    mid_ref,
    high_ref,
    mix_ref,
    weight_ref,
    target_ref,
    own_ref,
    below_ref,
    above_ref,
    pred_s,
    grad_s,
):
    mix = mix_ref[...]
    for member in range(MEMBERS):
        proj = jnp.concatenate([low_ref[member], mid_ref[member], high_ref[member]], axis=1)
        pred_s[member] = dot(proj, mix, NN)
    grad_s[...] = jnp.zeros(grad_s.shape, BF16)
    me = member_ref[0]
    for first in range(0, VARS, 16):
        rows = min(16, VARS - first)
        mine = pred_s[me, first : first + rows, :]
        total = jnp.zeros_like(mine)
        for member in range(MEMBERS):
            total = total + smooth_slope(mine - pred_s[member, first : first + rows, :])
        slopes = smooth_slope(mine - target_ref[first : first + rows, :]) - total * (
            1.0 / (MEMBERS - 1)
        )
        grad_s[first : first + rows, :] = (weight_ref[first : first + rows, :] * slopes).astype(
            BF16
        )
    sums = dot(mix, grad_s[...], NT)
    below_ref[...] = sums[0:NODES]
    own_ref[...] = sums[NODES : 2 * NODES]
    above_ref[...] = sums[2 * NODES : SPAN]


def terms_body(own_ref, low_ref, high_ref, states_ref, attn_ref, total_ref, out_ref):
    total = own_ref[...] + low_ref[...] + high_ref[...]
    total_ref[...] = total
    parts = jnp.concatenate(split(total), axis=0)
    states = states_ref[0]
    dec = dot(jnp.concatenate([states, states], axis=0), parts, TN)
    out_ref[:, 0:DEC_ROWS, :] = dec.astype(BF16).reshape(NEAR_SIZE, DEC_ROWS, VARS_LANE)
    attn = attn_ref[...]
    wo = dot(jnp.concatenate([attn, attn], axis=0), parts, TN)
    out_ref[:, DEC_ROWS:ROWS, :] = wo.astype(BF16).reshape(NEAR_SIZE, WO_ROWS, VARS_LANE)


def sum_body(copies, in_ref, out_ref):
    total = in_ref[0].astype(F32)
    for i in range(1, in_ref.shape[0]):
        total = total + in_ref[i].astype(F32)
    total = total.astype(BF16)
    for i in range(copies):
        out_ref[i] = total


def final_body(band_ref, all_ref, dec_ref, wo_ref, grad_dec_ref, dec_s, wo_s):
    dec_s[...] = jnp.zeros(dec_s.shape, BF16)
    dec_s[0:VARS, :] = dec_ref[...]
    band = band_ref[0]
    rows = all_ref[lax.div(band, 2), DEC_ROWS:ROWS, :]
    wo_s[...] = dot(rows, dec_s[...], NN)
    wo_ref[...] = wo_s[pl.ds(pl.multiple_of(lax.rem(band, 2) * 8, 8), 8), :]
    dec = all_ref[:, 0:DEC_ROWS, :].astype(F32).reshape(WIDTH, VARS_LANE)
    grad_dec_ref[...] = jnp.transpose(dec)[0:VARS, :]


def pair_masks(dtype):
    lane = lax.broadcasted_iota(jnp.int32, (1, PAIR), 1)
    return (lane < HEAD_DIM).astype(dtype), (lane >= HEAD_DIM).astype(dtype)


def forward_body(
    band_ref, windows_ref, query_ref, low_ref, mid_ref, high_ref, prob_ref, attn_ref
):
    base = (band_ref[0] - 1) * NODES
    place = lax.broadcasted_iota(jnp.int32, (1, SPAN), 1) + base
    inside = (place >= windows_ref[0, 0]) & (place < windows_ref[1, 0])
    masks = pair_masks(BF16)
    lane = lax.broadcasted_iota(jnp.int32, (1, PAIR), 1)
    for pair in range(HEADS // 2):
        cols = slice(pair * PAIR, (pair + 1) * PAIR)
        vcols = slice(ATT + pair * PAIR, ATT + (pair + 1) * PAIR)
        query = query_ref[0, :, cols]
        keys = jnp.concatenate([r[:, cols] for r in (low_ref, mid_ref, high_ref)], axis=0)
        values = jnp.concatenate([r[:, vcols] for r in (low_ref, mid_ref, high_ref)], axis=0)
        outs = []
        for half in range(2):
            scores = dot(query * masks[half], keys, NT) * SCALE
            scores = jnp.where(inside, scores, MASKED_SCORE)
            exponent = jnp.exp(scores - jnp.max(scores, axis=-1, keepdims=True))
            prob = exponent / jnp.sum(exponent, axis=-1, keepdims=True)
            prob_ref[2 * pair + half] = prob
            outs.append(dot(prob.astype(BF16), values, NN))
        attn_ref[:, cols] = jnp.where(lane < HEAD_DIM, outs[0], outs[1]).astype(BF16)


def backward_body(
    total_ref,
    dec_ref,
    out_weight_ref,
    query_ref,
    low_ref,
    mid_ref,
    high_ref,
    prob_ref,
    states_ref,
    grad_query_ref,
    own_ref,
    below_ref,
    above_ref,
    dec_s,
):
    dec_s[...] = jnp.zeros(dec_s.shape, BF16)
    dec_s[0:VARS, :] = dec_ref[...]
    dec = dec_s[...]
    grad_states = dot(
        jnp.concatenate(split(total_ref[...]), axis=1), jnp.concatenate([dec, dec], axis=0), NN
    ).astype(BF16)
    states_ref[0] = grad_states
    grad_out = dot(grad_states, out_weight_ref[...], NT).astype(BF16)
    masks = pair_masks(BF16)
    lane = lax.broadcasted_iota(jnp.int32, (1, PAIR), 1)
    first = lane < HEAD_DIM
    for pair in range(HEADS // 2):
        cols = slice(pair * PAIR, (pair + 1) * PAIR)
        vcols = slice(ATT + pair * PAIR, ATT + (pair + 1) * PAIR)
        query = query_ref[0, :, cols]
        keys = jnp.concatenate([r[:, cols] for r in (low_ref, mid_ref, high_ref)], axis=0)
        values = jnp.concatenate([r[:, vcols] for r in (low_ref, mid_ref, high_ref)], axis=0)
        grads = grad_out[:, cols]
        key_terms, value_terms, query_terms = [], [], []
        for half in range(2):
            prob = prob_ref[2 * pair + half]
            grad_prob = dot(grads * masks[half], values, NT)
            delta = jnp.sum(prob * grad_prob, axis=-1, keepdims=True)
            grad_scores = (prob * (grad_prob - delta)).astype(BF16)
            value_terms.append(dot(prob.astype(BF16), grads, TN))
            query_terms.append(dot(grad_scores, keys, NN))
            key_terms.append(dot(grad_scores, query, TN))
        grad_query_ref[0, :, cols] = (
            jnp.where(first, query_terms[0], query_terms[1]) * SCALE
        ).astype(BF16)
        key_term = jnp.where(first, key_terms[0], key_terms[1]) * SCALE
        value_term = jnp.where(first, value_terms[0], value_terms[1])
        for term, where in ((key_term, cols), (value_term, vcols)):
            below_ref[:, where] = term[0:NODES].astype(BF16)
            own_ref[:, where] = term[NODES : 2 * NODES]
            above_ref[:, where] = term[2 * NODES : SPAN].astype(BF16)


def join_body(own_ref, low_ref, high_ref, key_ref, value_ref):
    key_ref[0] = (
        own_ref[:, 0:ATT] + low_ref[:, 0:ATT].astype(F32) + high_ref[:, 0:ATT].astype(F32)
    ).astype(BF16)
    value_ref[0] = (
        own_ref[:, ATT : 2 * ATT]
        + low_ref[:, ATT : 2 * ATT].astype(F32)
        + high_ref[:, ATT : 2 * ATT].astype(F32)
    ).astype(BF16)


def up(x):
    count = 64
    return lax.ppermute(x, SPACE, [(i, i + 1) for i in range(count - 1)])


def down(x):
    count = 64
    return lax.ppermute(x, SPACE, [(i + 1, i) for i in range(count - 1)])


def exchange(x, axes):
    return lax.all_to_all(x, axes, split_axis=0, concat_axis=0, tiled=True)


def per_device(
    node_states,
    query,
    key,
    value,
    out_weight,
    dec_weight,
    target,
    area_weight,
    var_weight,
    edges,
    edge_weight,
    windows,
):
    band = lax.axis_index(SPACE).astype(jnp.int32).reshape(1)
    member = lax.axis_index(ENS).astype(jnp.int32).reshape(1)
    proj, kv = call(
        project_body,
        (shape((MEMBERS, VARS_SUB, NODES), BF16), shape((NODES, 2 * ATT), BF16)),
        scratch=[pltpu.VMEM((VARS_SUB, WIDTH), BF16)],
        n_in=4,
    )(node_states, dec_weight, key, value)
    proj_mid = exchange(proj, ENS)
    kv_low, kv_high = up(kv), down(kv)
    proj_low, proj_high = up(proj_mid), down(proj_mid)
    mix, weight = call(
        weights_body,
        (shape((SPAN, POINTS), BF16), shape((VARS_SUB, POINTS), F32)),
        smem=(0,),
        n_in=5,
    )(band, edges, edge_weight, area_weight.reshape(1, -1), var_weight.reshape(1, -1))
    prob, attn = call(
        forward_body,
        (shape((HEADS, NODES, SPAN), F32), shape((NODES, ATT), BF16)),
        smem=(0, 1),
        n_in=6,
        exps=10**6,
    )(band, windows, query, kv_low, kv, kv_high)
    block = shape((NODES, VARS_LANE), F32)
    own, below, above = call(
        crps_body,
        (block, block, block),
        scratch=[
            pltpu.VMEM((MEMBERS, VARS_SUB, POINTS), F32),
            pltpu.VMEM((VARS_LANE, POINTS), BF16),
        ],
        smem=(0,),
        n_in=7,
    )(member, proj_low, proj_mid, proj_high, mix, weight, target)
    total, terms = call(
        terms_body,
        (block, shape((NEAR_SIZE, ROWS, VARS_LANE), BF16)),
        n_in=5,
    )(own, up(above), down(below), node_states, attn)
    near = exchange(terms, NEAR)
    copies = call(
        functools.partial(sum_body, FAR_SIZE), shape((FAR_SIZE, ROWS, VARS_LANE), BF16), n_in=1
    )(near)
    far = exchange(copies, FAR)
    copies = call(
        functools.partial(sum_body, NEAR_SIZE), shape((NEAR_SIZE, ROWS, VARS_LANE), BF16), n_in=1
    )(far)
    everything = exchange(copies, NEAR)
    grad_wo, grad_dec = call(
        final_body,
        (shape((8, WIDTH), F32), shape((VARS, WIDTH), F32)),
        scratch=[pltpu.VMEM((VARS_LANE, WIDTH), BF16), pltpu.VMEM((WO_ROWS, WIDTH), F32)],
        smem=(0,),
        n_in=3,
    )(band, everything, dec_weight)
    wide = (NODES, 2 * ATT)
    grad_states, grad_query, kv_own, kv_below, kv_above = call(
        backward_body,
        (
            shape((1, NODES, WIDTH), BF16),
            shape((1, NODES, ATT), BF16),
            shape(wide, F32),
            shape(wide, BF16),
            shape(wide, BF16),
        ),
        scratch=[pltpu.VMEM((VARS_LANE, WIDTH), BF16)],
        n_in=8,
        flops=10**9,
        moved=10**7,
    )(total, dec_weight, out_weight, query, kv_low, kv, kv_high, prob)
    grad_key, grad_value = call(
        join_body, (shape((1, NODES, ATT), BF16), shape((1, NODES, ATT), BF16)), n_in=3
    )(kv_own, up(kv_above), down(kv_below))
    return grad_states, grad_query, grad_key, grad_value, grad_wo, grad_dec


def solution(mesh):
    fine = Mesh(mesh.devices.reshape(SIZES), AXES)
    in_specs = (
        P(ENS, SPACE, None),
        P(ENS, SPACE, None),
        P(ENS, SPACE, None),
        P(ENS, SPACE, None),
        P(),
        P(),
        P(None, SPACE),
        P(SPACE),
        P(),
        P(None, SPACE),
        P(None, SPACE),
        P(None, SPACE),
    )
    out_specs = (
        P(ENS, SPACE, None),
        P(ENS, SPACE, None),
        P(ENS, SPACE, None),
        P(ENS, SPACE, None),
        P(SPACE, None),
        P(),
    )
    return jax.shard_map(
        per_device, mesh=fine, in_specs=in_specs, out_specs=out_specs, check_vma=False
    )
```

time: 689 us -> 153 us (0.22)
  the two profiles are of different devices: /device:TPU:1 before, /device:TPU:2 now
where the time goes in v1:
time: 153 us; the launch traced here: 152 us
  blocking collectives  72.6 us (47%)
  starting transfers between devices  49.6 us (32%)
  Pallas kernels  14.2 us (9%)
  local copies, waits for them, and re-layouts  10.4 us (7%)
  waiting for transfers between devices  3.89 us (3%)
    all_to_all x3, blocking collectives, exchange(): return lax.all_to_all(x, axes, split_axis=0, concat_axis=0, tiled=True)  72.6 us
    ppermute x4, starting transfers between devices, down(): return lax.ppermute(x, SPACE, [(i + 1, i) for i in range(count - 1)])  36.3 us
    unnamed x39, local copies, waits for them, and re-layouts  10.4 us
    ppermute x4, starting transfers between devices, up(): return lax.ppermute(x, SPACE, [(i, i + 1) for i in range(count - 1)])  7.79 us
    all_to_all x1, starting transfers between devices, exchange(): return lax.all_to_all(x, axes, split_axis=0, concat_axis=0, tiled=True)  5.5 us
    pallas_call x1, Pallas kernels, per_device(): call(backward_body, (shape((1, NODES, WIDTH), BF16), shape((1, NODES, ATT...  3.96 us
    ppermute x4, waiting for transfers between devices, up(): return lax.ppermute(x, SPACE, [(i, i + 1) for i in range(count - 1)])  3.41 us
    pallas_call x1, Pallas kernels, per_device(): call(forward_body, (shape((HEADS, NODES, SPAN), F32), shape((NODES, ATT),...  3.4 us
  transfers between devices with their start and end apart: 9, of which 2 were waited for; matrix products, arithmetic and copies ran while one was open for 0% of the time, Pallas kernels for 8%

profile of v1, /device:TPU:2, one launch (start us, length us, event | category | flops | bytes accessed | tf_op | source)
XLA Modules:
  0.0 151.7 jit_solution(4518138851680101907)
XLA Ops:
  0.6 0.9 copy-done
  1.6 0.9 copy-done.2
  2.5 0.9 copy-done.10
  4.6 34.4 %all_to_all.20.mid_ref = bf16[8,112,128]{2,1,0:T(8,128)(2,1)S(1)} all-to-all(bf16[8,112,128]{2,1,0:T(8,128)(2,1)S(1)} %get-tuple-element.26), channel_id=1, replica_groups=mesh['zh'=2,'y'=4,'x'=4,'zl'=8,'c'=2] {'zh','y'}, dimensions={0} | all-to-all | bytes 458752 | tf_op jit(solution)/shard_map/all_to_all | solution.py:280
  39.0 3.0 %collective-permute-start.1 = (bf16[8,112,128]{2,1,0:T(8,128)(2,1)S(1)}, bf16[8,112,128]{2,1,0:T(8,128)(2,1)S(1)}, u32[]{:S(2)}, u32[]{:S(2)}) collective-permute-start(bf16[8,112,128]{2,1,0:T(8,128)(2,1)S(1)} %all_to_all.20.mid_ref), channel_id=1, source_target_pairs={{1,0},{2,1},{3,2},{4,3},{5,4},{6,5},{7,6},{8,7},{9,8},{10,9},{11,1... | collective-permute-start | bytes 688136 | tf_op jit(solution)/shard_map/ppermute | solution.py:276
  42.0 1.9 %collective-permute-start = (bf16[8,112,128]{2,1,0:T(8,128)(2,1)S(1)}, bf16[8,112,128]{2,1,0:T(8,128)(2,1)S(1)}, u32[]{:S(2)}, u32[]{:S(2)}) collective-permute-start(bf16[8,112,128]{2,1,0:T(8,128)(2,1)S(1)} %all_to_all.20.mid_ref), channel_id=1, source_target_pairs={{0,1},{1,2},{2,3},{3,4},{4,5},{5,6},{6,7},{7,8},{8,9},{9,10},{10,1... | collective-permute-start | bytes 688136 | tf_op jit(solution)/shard_map/ppermute | solution.py:271
  44.0 11.1 %collective-permute-start.5 = (bf16[128,1024]{1,0:T(8,128)(2,1)S(1)}, bf16[128,1024]{1,0:T(8,128)(2,1)S(1)}, u32[]{:S(2)}, u32[]{:S(2)}) collective-permute-start(bf16[128,1024]{1,0:T(8,128)(2,1)S(1)} %get-tuple-element.32.mid_ref), channel_id=1, source_target_pairs={{1,0},{2,1},{3,2},{4,3},{5,4},{6,5},{7,6},{8,7},{9,8},{10,9},{11,1... | collective-permute-start | bytes 786440 | tf_op jit(solution)/shard_map/ppermute | solution.py:276
  55.1 1.9 %collective-permute-start.4 = (bf16[128,1024]{1,0:T(8,128)(2,1)S(1)}, bf16[128,1024]{1,0:T(8,128)(2,1)S(1)}, u32[]{:S(2)}, u32[]{:S(2)}) collective-permute-start(bf16[128,1024]{1,0:T(8,128)(2,1)S(1)} %get-tuple-element.32.mid_ref), channel_id=1, source_target_pairs={{0,1},{1,2},{2,3},{3,4},{4,5},{5,6},{6,7},{7,8},{8,9},{9,10},{10,1... | collective-permute-start | bytes 786440 | tf_op jit(solution)/shard_map/ppermute | solution.py:271
  60.8 2.9 %shard_map.165 = (f32[128,128]{1,0:T(8,128)S(1)}, f32[128,128]{1,0:T(8,128)S(1)}, f32[128,128]{1,0:T(8,128)}) custom-call(s32[1]{0:T(128)} %bitcast.member_ref, bf16[8,112,128]{2,1,0:T(8,128)(2,1)S(1)} %collective-permute-done.low_ref, bf16[8,112,128]{2,1,0:T(8,128)(2,1)S(1)} %all_to_all.20.mid_ref, ...), custom_call_target="tpu_custom_call" | custom-call | flops 100000000 | bytes 1000000 | tf_op jit(solution)/shard_map/pallas_call | solution.py:322
  63.6 1.9 %collective-permute-start.2 = (f32[128,128]{1,0:T(8,128)}, f32[128,128]{1,0:T(8,128)S(1)}, u32[]{:S(2)}, u32[]{:S(2)}) collective-permute-start(f32[128,128]{1,0:T(8,128)} %get-tuple-element.30), channel_id=1, source_target_pairs={{0,1},{1,2},{2,3},{3,4},{4,5},{5,6},{6,7},{7,8},{8,9},{9,10},{10,1... | collective-permute-start | bytes 196616 | tf_op jit(solution)/shard_map/ppermute | solution.py:271
  65.6 11.1 %collective-permute-start.3 = (f32[128,128]{1,0:T(8,128)S(1)}, f32[128,128]{1,0:T(8,128)S(1)}, u32[]{:S(2)}, u32[]{:S(2)}) collective-permute-start(f32[128,128]{1,0:T(8,128)S(1)} %get-tuple-element.31), channel_id=1, source_target_pairs={{1,0},{2,1},{3,2},{4,3},{5,4},{6,5},{7,6},{8,7},{9,8},{10,9},{11,1... | collective-permute-start | bytes 196616 | tf_op jit(solution)/shard_map/ppermute | solution.py:276
  76.8 1.0 copy-done.12
  77.8 3.4 %shard_map.166 = (f32[8,128,384]{2,1,0:T(8,128)S(1)}, bf16[128,512]{1,0:T(8,128)(2,1)S(1)}) custom-call(s32[1]{0:T(128)} %bitcast.1.band_ref, s32[2,1]{1,0:T(2,128)S(1)} %copy.18.windows_ref, bf16[1,128,512]{2,1,0:T(8,128)(2,1)S(1)} %copy-done.12, bf16[128,1024]{1,0:T(8,128)(2,1)S(1)} %collective-permute-done.4.low_ref, ...), custom_call_target="tpu_custom_call" | custom-call | flops 100000000 | bytes 1000000 | tf_op jit(solution)/shard_map/pallas_call | solution.py:314
  81.7 14.6 %all_to_all.21.in_ref = bf16[32,48,128]{2,1,0:T(8,128)(2,1)S(1)} all-to-all(bf16[32,48,128]{2,1,0:T(8,128)(2,1)S(1)} %get-tuple-element.43), channel_id=1, replica_groups=mesh['zh'=2,'y'=4,'x'=4,'zl'=8,'c'=2] {'y','x','c'}, dimensions={0} | all-to-all | bytes 786432 | tf_op jit(solution)/shard_map/all_to_all | solution.py:280
  96.3 23.6 %all_to_all.22.in_ref = bf16[16,48,128]{2,1,0:T(8,128)(2,1)S(1)} all-to-all(bf16[16,48,128]{2,1,0:T(8,128)(2,1)S(1)} %shard_map.170), channel_id=1, replica_groups=mesh['zh'=2,'y'=4,'x'=4,'zl'=8,'c'=2] {'zh','zl'}, dimensions={0} | all-to-all | bytes 393216 | tf_op jit(solution)/shard_map/all_to_all | solution.py:280
  120.8 5.5 %all-to-all-start.3 = ((bf16[32,48,128]{2,1,0:T(8,128)(2,1)}), bf16[32,48,128]{2,1,0:T(8,128)(2,1)S(1)}, u32[]{:S(2)}, u32[]{:S(2)}) async-start(bf16[32,48,128]{2,1,0:T(8,128)(2,1)} %shard_map.171), calls=%async_computation.3 | async-start | bytes 786432 | tf_op jit(solution)/shard_map/all_to_all | solution.py:280
  126.3 0.9 copy-done.7
  127.3 0.9 copy-done.9
  128.2 0.9 copy-done.13
  129.1 4.0 %shard_map.168 = (bf16[1,128,1024]{2,1,0:T(8,128)(2,1)}, bf16[1,128,512]{2,1,0:T(8,128)(2,1)}, f32[128,1024]{1,0:T(8,128)S(1)}, bf16[128,1024]{1,0:T(8,128)(2,1)S(1)}, bf16[128,1024]{1,0:T(8,128)(2,1)S(1)}) custom-call(f32[128,128]{1,0:T(8,128)S(1)} %get-tuple-element.34.total_ref, bf16[100,1024]{1,0:T(8,128)(2,1)S(1)} %copy-done.1, ...), custom_call_target="tpu_custom_call" | custom-call | flops 1000000000 | bytes 10000000 | tf_op jit(solution)/shard_map/pallas_call | solution.py:354
  133.1 2.0 %collective-permute-start.6 = (bf16[128,1024]{1,0:T(8,128)(2,1)S(1)}, bf16[128,1024]{1,0:T(8,128)(2,1)S(1)}, u32[]{:S(2)}, u32[]{:S(2)}) collective-permute-start(bf16[128,1024]{1,0:T(8,128)(2,1)S(1)} %get-tuple-element.39), channel_id=1, source_target_pairs={{0,1},{1,2},{2,3},{3,4},{4,5},{5,6},{6,7},{7,8},{8,9},{9,10},{10,1... | collective-permute-start | bytes 786440 | tf_op jit(solution)/shard_map/ppermute | solution.py:271
  135.1 11.0 %collective-permute-start.7 = (bf16[128,1024]{1,0:T(8,128)(2,1)S(1)}, bf16[128,1024]{1,0:T(8,128)(2,1)S(1)}, u32[]{:S(2)}, u32[]{:S(2)}) collective-permute-start(bf16[128,1024]{1,0:T(8,128)(2,1)S(1)} %get-tuple-element.40), channel_id=1, source_target_pairs={{1,0},{2,1},{3,2},{4,3},{5,4},{6,5},{7,6},{8,7},{9,8},{10,9},{11,1... | collective-permute-start | bytes 786440 | tf_op jit(solution)/shard_map/ppermute | solution.py:276
  146.1 3.4 %collective-permute-done.6.low_ref = bf16[128,1024]{1,0:T(8,128)(2,1)S(1)} collective-permute-done((bf16[128,1024]{1,0:T(8,128)(2,1)S(1)}, bf16[128,1024]{1,0:T(8,128)(2,1)S(1)}, u32[]{:S(2)}, u32[]{:S(2)}) %collective-permute-start.6) | collective-permute-done | bytes 262176 | tf_op jit(solution)/shard_map/ppermute | solution.py:271
  150.8 0.9 shard_map.172
  (46 shorter events, 7.4 us)
Async XLA Ops:
  0.6 0.9 copy-start
  1.6 0.9 copy-start.2
  2.5 0.9 copy-start.10
  3.4 0.9 copy-start.11
  4.3 56.4 %copy-start.5 = (f32[100,1024]{1,0:T(8,128)S(1)}, f32[100,1024]{1,0:T(8,128)}, u32[]{:S(2)}) copy-start(f32[100,1024]{1,0:T(8,128)} %target_ref.1) | copy-start | bytes 1228804
  4.6 72.1 %copy-start.18 = (s32[2,1]{0,1:T(1,128)S(1)}, s32[2,1]{0,1:T(1,128)}, u32[]{:S(2)}) copy-start(s32[2,1]{0,1:T(1,128)} %param.23) | copy-start | bytes 28
  39.0 21.7 %collective-permute-start.1 = (bf16[8,112,128]{2,1,0:T(8,128)(2,1)S(1)}, bf16[8,112,128]{2,1,0:T(8,128)(2,1)S(1)}, u32[]{:S(2)}, u32[]{:S(2)}) collective-permute-start(bf16[8,112,128]{2,1,0:T(8,128)(2,1)S(1)} %all_to_all.20.mid_ref), channel_id=1, source_target_pairs={{1,0},{2,1},{3,2},{4,3},{5,4},{6,5},{7,6},{8,7},{9,8},{10,9},{11,1... | collective-permute-start | bytes 688136 | tf_op jit(solution)/shard_map/ppermute | solution.py:276
  42.0 18.7 %collective-permute-start = (bf16[8,112,128]{2,1,0:T(8,128)(2,1)S(1)}, bf16[8,112,128]{2,1,0:T(8,128)(2,1)S(1)}, u32[]{:S(2)}, u32[]{:S(2)}) collective-permute-start(bf16[8,112,128]{2,1,0:T(8,128)(2,1)S(1)} %all_to_all.20.mid_ref), channel_id=1, source_target_pairs={{0,1},{1,2},{2,3},{3,4},{4,5},{5,6},{6,7},{7,8},{8,9},{9,10},{10,1... | collective-permute-start | bytes 688136 | tf_op jit(solution)/shard_map/ppermute | solution.py:271
  44.0 32.9 %collective-permute-start.5 = (bf16[128,1024]{1,0:T(8,128)(2,1)S(1)}, bf16[128,1024]{1,0:T(8,128)(2,1)S(1)}, u32[]{:S(2)}, u32[]{:S(2)}) collective-permute-start(bf16[128,1024]{1,0:T(8,128)(2,1)S(1)} %get-tuple-element.32.mid_ref), channel_id=1, source_target_pairs={{1,0},{2,1},{3,2},{4,3},{5,4},{6,5},{7,6},{8,7},{9,8},{10,9},{11,1... | collective-permute-start | bytes 786440 | tf_op jit(solution)/shard_map/ppermute | solution.py:276
  55.1 21.7 %collective-permute-start.4 = (bf16[128,1024]{1,0:T(8,128)(2,1)S(1)}, bf16[128,1024]{1,0:T(8,128)(2,1)S(1)}, u32[]{:S(2)}, u32[]{:S(2)}) collective-permute-start(bf16[128,1024]{1,0:T(8,128)(2,1)S(1)} %get-tuple-element.32.mid_ref), channel_id=1, source_target_pairs={{0,1},{1,2},{2,3},{3,4},{4,5},{5,6},{6,7},{7,8},{8,9},{9,10},{10,1... | collective-permute-start | bytes 786440 | tf_op jit(solution)/shard_map/ppermute | solution.py:271
  60.8 20.5 %copy-start.3 = (bf16[1,128,1024]{2,1,0:T(8,128)(2,1)S(1)}, bf16[1,128,1024]{2,1,0:T(8,128)(2,1)}, u32[]{:S(2)}) copy-start(bf16[1,128,1024]{2,1,0:T(8,128)(2,1)} %states_ref.3) | copy-start | bytes 786436
  63.6 17.6 %collective-permute-start.2 = (f32[128,128]{1,0:T(8,128)}, f32[128,128]{1,0:T(8,128)S(1)}, u32[]{:S(2)}, u32[]{:S(2)}) collective-permute-start(f32[128,128]{1,0:T(8,128)} %get-tuple-element.30), channel_id=1, source_target_pairs={{0,1},{1,2},{2,3},{3,4},{4,5},{5,6},{6,7},{7,8},{8,9},{9,10},{10,1... | collective-permute-start | bytes 196616 | tf_op jit(solution)/shard_map/ppermute | solution.py:271
  65.6 15.7 %collective-permute-start.3 = (f32[128,128]{1,0:T(8,128)S(1)}, f32[128,128]{1,0:T(8,128)S(1)}, u32[]{:S(2)}, u32[]{:S(2)}) collective-permute-start(f32[128,128]{1,0:T(8,128)S(1)} %get-tuple-element.31), channel_id=1, source_target_pairs={{1,0},{2,1},{3,2},{4,3},{5,4},{6,5},{7,6},{8,7},{9,8},{10,9},{11,1... | collective-permute-start | bytes 196616 | tf_op jit(solution)/shard_map/ppermute | solution.py:276
  76.8 4.8 %copy-start.6 = (bf16[128,1024]{1,0:T(8,128)(2,1)}, bf16[128,1024]{1,0:T(8,128)(2,1)S(1)}, u32[]{:S(2)}) copy-start(bf16[128,1024]{1,0:T(8,128)(2,1)S(1)} %collective-permute-done.5.high_ref) | copy-start | bytes 786436
  76.8 1.0 copy-start.12
  77.8 3.8 %copy-start.8 = (bf16[128,1024]{1,0:T(8,128)(2,1)}, bf16[128,1024]{1,0:T(8,128)(2,1)S(1)}, u32[]{:S(2)}) copy-start(bf16[128,1024]{1,0:T(8,128)(2,1)S(1)} %collective-permute-done.4.low_ref) | copy-start | bytes 786436
  81.7 44.6 %copy-start.1 = (bf16[100,1024]{1,0:T(8,128)(2,1)S(1)}, bf16[100,1024]{1,0:T(8,128)(2,1)}, u32[]{:S(2)}) copy-start(bf16[100,1024]{1,0:T(8,128)(2,1)} %dec_ref.5) | copy-start | bytes 614404
  81.7 44.6 %copy-start.4 = (bf16[512,1024]{1,0:T(8,128)(2,1)S(1)}, bf16[512,1024]{1,0:T(8,128)(2,1)}, u32[]{:S(2)}) copy-start(bf16[512,1024]{1,0:T(8,128)(2,1)} %out_weight_ref.1) | copy-start | bytes 3145732
  120.8 30.0 %all-to-all-start.3 = ((bf16[32,48,128]{2,1,0:T(8,128)(2,1)}), bf16[32,48,128]{2,1,0:T(8,128)(2,1)S(1)}, u32[]{:S(2)}, u32[]{:S(2)}) async-start(bf16[32,48,128]{2,1,0:T(8,128)(2,1)} %shard_map.171), calls=%async_computation.3 | async-start | bytes 786432 | tf_op jit(solution)/shard_map/all_to_all | solution.py:280
  126.3 1.0 copy-start.7
  127.3 0.9 copy-start.9
  128.2 0.9 copy-start.13
  133.1 16.5 %collective-permute-start.6 = (bf16[128,1024]{1,0:T(8,128)(2,1)S(1)}, bf16[128,1024]{1,0:T(8,128)(2,1)S(1)}, u32[]{:S(2)}, u32[]{:S(2)}) collective-permute-start(bf16[128,1024]{1,0:T(8,128)(2,1)S(1)} %get-tuple-element.39), channel_id=1, source_target_pairs={{0,1},{1,2},{2,3},{3,4},{4,5},{5,6},{6,7},{7,8},{8,9},{9,10},{10,1... | collective-permute-start | bytes 786440 | tf_op jit(solution)/shard_map/ppermute | solution.py:271
  135.1 14.9 %collective-permute-start.7 = (bf16[128,1024]{1,0:T(8,128)(2,1)S(1)}, bf16[128,1024]{1,0:T(8,128)(2,1)S(1)}, u32[]{:S(2)}, u32[]{:S(2)}) collective-permute-start(bf16[128,1024]{1,0:T(8,128)(2,1)S(1)} %get-tuple-element.40), channel_id=1, source_target_pairs={{1,0},{2,1},{3,2},{4,3},{5,4},{6,5},{7,6},{8,7},{9,8},{10,9},{11,1... | collective-permute-start | bytes 786440 | tf_op jit(solution)/shard_map/ppermute | solution.py:276
  (4 other events, 2.8 us)

commit v2 on v1

--- a/solution.py
+++ b/solution.py
@@ -48,17 +48,21 @@
     return lax.dot_general(a, b, dims, preferred_element_type=F32)
 
 
-def call(body, out_shape, scratch=(), smem=(), flops=10**8, moved=10**6, exps=0, n_in=0):
-    specs = [
-        pl.BlockSpec(memory_space=pltpu.SMEM if i in smem else pltpu.VMEM) for i in range(n_in)
-    ]
+def call(body, out_shape, spaces, scratch=(), limit=24 * 2**20, exps=0):
+    kinds = {
+        "s": pl.BlockSpec(memory_space=pltpu.SMEM),
+        "v": pl.BlockSpec(memory_space=pltpu.VMEM),
+        "a": pl.BlockSpec(memory_space=pl.ANY),
+        "h": pl.BlockSpec(memory_space=pltpu.HBM),
+    }
+    specs = [kinds[space] for space in spaces]
     return pl.pallas_call(
         body,
         out_shape=out_shape,
         in_specs=specs,
         scratch_shapes=list(scratch),
-        compiler_params=pltpu.CompilerParams(vmem_limit_bytes=40 * 2**20),
-        cost_estimate=pl.CostEstimate(flops=flops, bytes_accessed=moved, transcendentals=exps),
+        compiler_params=pltpu.CompilerParams(vmem_limit_bytes=limit),
+        cost_estimate=pl.CostEstimate(flops=10**8, bytes_accessed=10**6, transcendentals=exps),
     )
 
 
@@ -75,14 +79,32 @@
     return high, (x - high.astype(F32)).astype(BF16)
 
 
-def project_body(states_ref, dec_ref, key_ref, value_ref, proj_ref, kv_ref, dec_s):
-    dec_s[...] = jnp.zeros(dec_s.shape, BF16)
-    dec_s[0:VARS, :] = dec_ref[...]
-    proj = dot(dec_s[...], states_ref[0], NT).astype(BF16)
+def project_body(
+    states_hbm, dec_hbm, key_hbm, value_hbm, proj_ref, kv_ref, states_s, dec_s, pad_s, sems
+):
+    copies = [
+        pltpu.make_async_copy(states_hbm.at[0], states_s, sems.at[0]),
+        pltpu.make_async_copy(dec_hbm, dec_s, sems.at[1]),
+    ]
+    for block in range(ATT // PAIR):
+        cols = pl.ds(block * PAIR, PAIR)
+        for source, first in ((key_hbm, 0), (value_hbm, ATT // PAIR)):
+            copies.append(
+                pltpu.make_async_copy(
+                    source.at[0, :, cols], kv_ref.at[first + block], sems.at[len(copies)]
+                )
+            )
+    for copy in copies:
+        copy.start()
+    pad_s[...] = jnp.zeros(pad_s.shape, BF16)
+    copies[1].wait()
+    pad_s[0:VARS, :] = dec_s[...]
+    copies[0].wait()
+    proj = dot(pad_s[...], states_s[...], NT).astype(BF16)
     for member in range(MEMBERS):
         proj_ref[member] = proj
-    kv_ref[:, 0:ATT] = key_ref[0]
-    kv_ref[:, ATT : 2 * ATT] = value_ref[0]
+    for copy in copies[2:]:
+        copy.wait()
 
 
 def weights_body(band_ref, edges_ref, edge_weight_ref, area_ref, var_ref, mix_ref, weight_ref):
@@ -117,7 +139,8 @@
 ):
     mix = mix_ref[...]
     for member in range(MEMBERS):
-        proj = jnp.concatenate([low_ref[member], mid_ref[member], high_ref[member]], axis=1)
+        rows = slice(member * VARS_SUB, (member + 1) * VARS_SUB)
+        proj = jnp.concatenate([low_ref[rows], mid_ref[member], high_ref[rows]], axis=1)
         pred_s[member] = dot(proj, mix, NN)
     grad_s[...] = jnp.zeros(grad_s.shape, BF16)
     me = member_ref[0]
@@ -151,7 +174,8 @@
     out_ref[:, DEC_ROWS:ROWS, :] = wo.astype(BF16).reshape(NEAR_SIZE, WO_ROWS, VARS_LANE)
 
 
-def sum_body(copies, in_ref, out_ref):
+def sum_body(copies, in_ref, *rest):
+    out_ref = rest[-1]
     total = in_ref[0].astype(F32)
     for i in range(1, in_ref.shape[0]):
         total = total + in_ref[i].astype(F32)
@@ -174,6 +198,12 @@
 def pair_masks(dtype):
     lane = lax.broadcasted_iota(jnp.int32, (1, PAIR), 1)
     return (lane < HEAD_DIM).astype(dtype), (lane >= HEAD_DIM).astype(dtype)
+
+
+def band_blocks(low_ref, mid_ref, high_ref, block):
+    first = MEMBERS * VARS_SUB + block * NODES
+    rows = slice(first, first + NODES)
+    return jnp.concatenate([low_ref[rows], mid_ref[block], high_ref[rows]], axis=0)
 
 
 def forward_body(
@@ -186,10 +216,9 @@
     lane = lax.broadcasted_iota(jnp.int32, (1, PAIR), 1)
     for pair in range(HEADS // 2):
         cols = slice(pair * PAIR, (pair + 1) * PAIR)
-        vcols = slice(ATT + pair * PAIR, ATT + (pair + 1) * PAIR)
         query = query_ref[0, :, cols]
-        keys = jnp.concatenate([r[:, cols] for r in (low_ref, mid_ref, high_ref)], axis=0)
-        values = jnp.concatenate([r[:, vcols] for r in (low_ref, mid_ref, high_ref)], axis=0)
+        keys = band_blocks(low_ref, mid_ref, high_ref, pair)
+        values = band_blocks(low_ref, mid_ref, high_ref, HEADS // 2 + pair)
         outs = []
         for half in range(2):
             scores = dot(query * masks[half], keys, NT) * SCALE
@@ -210,6 +239,7 @@
     mid_ref,
     high_ref,
     prob_ref,
+    after_ref,
     states_ref,
     grad_query_ref,
     own_ref,
@@ -232,8 +262,8 @@
         cols = slice(pair * PAIR, (pair + 1) * PAIR)
         vcols = slice(ATT + pair * PAIR, ATT + (pair + 1) * PAIR)
         query = query_ref[0, :, cols]
-        keys = jnp.concatenate([r[:, cols] for r in (low_ref, mid_ref, high_ref)], axis=0)
-        values = jnp.concatenate([r[:, vcols] for r in (low_ref, mid_ref, high_ref)], axis=0)
+        keys = band_blocks(low_ref, mid_ref, high_ref, pair)
+        values = band_blocks(low_ref, mid_ref, high_ref, HEADS // 2 + pair)
         grads = grad_out[:, cols]
         key_terms, value_terms, query_terms = [], [], []
         for half in range(2):
@@ -255,7 +285,8 @@
             above_ref[:, where] = term[2 * NODES : SPAN].astype(BF16)
 
 
-def join_body(own_ref, low_ref, high_ref, key_ref, value_ref):
+def join_body(own_ref, low_ref, high_ref, key_ref, value_ref, done_ref):
+    done_ref[...] = jnp.zeros(done_ref.shape, F32)
     key_ref[0] = (
         own_ref[:, 0:ATT] + low_ref[:, 0:ATT].astype(F32) + high_ref[:, 0:ATT].astype(F32)
     ).astype(BF16)
@@ -296,60 +327,53 @@
 ):
     band = lax.axis_index(SPACE).astype(jnp.int32).reshape(1)
     member = lax.axis_index(ENS).astype(jnp.int32).reshape(1)
+    blocks = 2 * ATT // PAIR
     proj, kv = call(
         project_body,
-        (shape((MEMBERS, VARS_SUB, NODES), BF16), shape((NODES, 2 * ATT), BF16)),
-        scratch=[pltpu.VMEM((VARS_SUB, WIDTH), BF16)],
-        n_in=4,
+        (shape((MEMBERS, VARS_SUB, NODES), BF16), shape((blocks, NODES, PAIR), BF16)),
+        "hhhh",
+        scratch=[
+            pltpu.VMEM((NODES, WIDTH), BF16),
+            pltpu.VMEM((VARS, WIDTH), BF16),
+            pltpu.VMEM((VARS_SUB, WIDTH), BF16),
+            pltpu.SemaphoreType.DMA((2 + blocks,)),
+        ],
+        limit=None,
     )(node_states, dec_weight, key, value)
-    proj_mid = exchange(proj, ENS)
-    kv_low, kv_high = up(kv), down(kv)
-    proj_low, proj_high = up(proj_mid), down(proj_mid)
+    mid = exchange(proj, ENS)
+    packed = jnp.concatenate([mid.reshape(-1, NODES), kv.reshape(-1, PAIR)], axis=0)
+    low, high = up(packed), down(packed)
     mix, weight = call(
         weights_body,
         (shape((SPAN, POINTS), BF16), shape((VARS_SUB, POINTS), F32)),
-        smem=(0,),
-        n_in=5,
+        "svvvv",
     )(band, edges, edge_weight, area_weight.reshape(1, -1), var_weight.reshape(1, -1))
     prob, attn = call(
         forward_body,
         (shape((HEADS, NODES, SPAN), F32), shape((NODES, ATT), BF16)),
-        smem=(0, 1),
-        n_in=6,
+        "ssvvvv",
         exps=10**6,
-    )(band, windows, query, kv_low, kv, kv_high)
+    )(band, windows, query, low, kv, high)
     block = shape((NODES, VARS_LANE), F32)
     own, below, above = call(
         crps_body,
         (block, block, block),
+        "svvvvvv",
         scratch=[
             pltpu.VMEM((MEMBERS, VARS_SUB, POINTS), F32),
             pltpu.VMEM((VARS_LANE, POINTS), BF16),
         ],
-        smem=(0,),
-        n_in=7,
-    )(member, proj_low, proj_mid, proj_high, mix, weight, target)
+    )(member, low, mid, high, mix, weight, target)
     total, terms = call(
         terms_body,
         (block, shape((NEAR_SIZE, ROWS, VARS_LANE), BF16)),
-        n_in=5,
+        "vvvvv",
     )(own, up(above), down(below), node_states, attn)
     near = exchange(terms, NEAR)
-    copies = call(
-        functools.partial(sum_body, FAR_SIZE), shape((FAR_SIZE, ROWS, VARS_LANE), BF16), n_in=1
+    near_sums = call(
+        functools.partial(sum_body, FAR_SIZE), shape((FAR_SIZE, ROWS, VARS_LANE), BF16), "v"
     )(near)
-    far = exchange(copies, FAR)
-    copies = call(
-        functools.partial(sum_body, NEAR_SIZE), shape((NEAR_SIZE, ROWS, VARS_LANE), BF16), n_in=1
-    )(far)
-    everything = exchange(copies, NEAR)
-    grad_wo, grad_dec = call(
-        final_body,
-        (shape((8, WIDTH), F32), shape((VARS, WIDTH), F32)),
-        scratch=[pltpu.VMEM((VARS_LANE, WIDTH), BF16), pltpu.VMEM((WO_ROWS, WIDTH), F32)],
-        smem=(0,),
-        n_in=3,
-    )(band, everything, dec_weight)
+    far = exchange(near_sums, FAR)
     wide = (NODES, 2 * ATT)
     grad_states, grad_query, kv_own, kv_below, kv_above = call(
         backward_body,
@@ -360,14 +384,26 @@
             shape(wide, BF16),
             shape(wide, BF16),
         ),
+        "vvvvvvvva",
         scratch=[pltpu.VMEM((VARS_LANE, WIDTH), BF16)],
-        n_in=8,
-        flops=10**9,
-        moved=10**7,
-    )(total, dec_weight, out_weight, query, kv_low, kv, kv_high, prob)
-    grad_key, grad_value = call(
-        join_body, (shape((1, NODES, ATT), BF16), shape((1, NODES, ATT), BF16)), n_in=3
+    )(total, dec_weight, out_weight, query, low, kv, high, prob, near_sums)
+    grad_key, grad_value, joined = call(
+        join_body,
+        (shape((1, NODES, ATT), BF16), shape((1, NODES, ATT), BF16), shape((8, 128), F32)),
+        "vvv",
     )(kv_own, up(kv_above), down(kv_below))
+    far_sums = call(
+        functools.partial(sum_body, NEAR_SIZE),
+        shape((NEAR_SIZE, ROWS, VARS_LANE), BF16),
+        "vv",
+    )(far, joined)
+    everything = exchange(far_sums, NEAR)
+    grad_wo, grad_dec = call(
+        final_body,
+        (shape((8, WIDTH), F32), shape((VARS, WIDTH), F32)),
+        "svv",
+        scratch=[pltpu.VMEM((VARS_LANE, WIDTH), BF16), pltpu.VMEM((WO_ROWS, WIDTH), F32)],
+    )(band, everything, dec_weight)
     return grad_states, grad_query, grad_key, grad_value, grad_wo, grad_dec
 
 

time: 153 us -> 151 us (0.987)
  the two profiles are of different devices: /device:TPU:2 before, /device:TPU:1 now
where the time goes in v2:
time: 151 us
  blocking collectives  83.5 us (55%)
  starting transfers between devices  34.3 us (23%)
  Pallas kernels  16.9 us (11%)
  waiting for transfers between devices  10.6 us (7%)
  local copies, waits for them, and re-layouts  3.45 us (2%)
    all_to_all x3, blocking collectives, exchange(): return lax.all_to_all(x, axes, split_axis=0, concat_axis=0, tiled=True)  83.5 us
    ppermute x3, starting transfers between devices, up(): return lax.ppermute(x, SPACE, [(i, i + 1) for i in range(count - 1)])  17.2 us
    ppermute x3, starting transfers between devices, down(): return lax.ppermute(x, SPACE, [(i + 1, i) for i in range(count - 1)])  8.66 us
    all_to_all x1, starting transfers between devices, exchange(): return lax.all_to_all(x, axes, split_axis=0, concat_axis=0, tiled=True)  8.41 us
    ppermute x3, waiting for transfers between devices, down(): return lax.ppermute(x, SPACE, [(i + 1, i) for i in range(count - 1)])  7.56 us
    pallas_call x1, Pallas kernels, per_device(): call(backward_body, (shape((1, NODES, WIDTH), BF16), shape((1, NODES, ATT...  3.94 us
    unnamed x31, local copies, waits for them, and re-layouts  3.45 us
    pallas_call x1, Pallas kernels, per_device(): call(forward_body, (shape((HEADS, NODES, SPAN), F32), shape((NODES, ATT),...  3.4 us
  transfers between devices with their start and end apart: 7, of which 4 were waited for; matrix products, arithmetic and copies ran while one was open for 0% of the time, Pallas kernels for 6%

profile of v2, /device:TPU:1, one launch (start us, length us, event | category | flops | bytes accessed | tf_op | source)
XLA Modules:
  0.0 150.7 jit_solution(2130481157594819583)
XLA Ops:
  0.7 2.2 %shard_map.163 = (bf16[8,112,128]{2,1,0:T(8,128)(2,1)}, bf16[8,128,128]{2,1,0:T(8,128)(2,1)}) custom-call(bf16[1,128,1024]{2,1,0:T(8,128)(2,1)} %states_ref.1, bf16[100,1024]{1,0:T(8,128)(2,1)} %dec_ref.3, bf16[1,128,512]{2,1,0:T(8,128)(2,1)} %key_hbm.1, bf16[1,128,512]{2,1,0:T(8,128)(2,1)} %value_hbm.1), custom_call_target="tpu_custom_call" | custom-call | flops 100000000 | bytes 1000000 | tf_op jit(solution)/shard_map/pallas_call | solution.py:331
  2.9 33.2 %all_to_all.20.mid_ref = bf16[8,112,128]{2,1,0:T(8,128)(2,1)S(1)} all-to-all(bf16[8,112,128]{2,1,0:T(8,128)(2,1)} %get-tuple-element.27), channel_id=1, replica_groups=mesh['zh'=2,'y'=4,'x'=4,'zl'=8,'c'=2] {'zh','y'}, dimensions={0} | all-to-all | bytes 458752 | tf_op jit(solution)/shard_map/all_to_all | solution.py:311
  36.1 1.0 pad_maximum_fusion
  37.1 4.8 %collective-permute-start.1 = (bf16[1920,128]{1,0:T(8,128)(2,1)S(1)}, bf16[1920,128]{1,0:T(8,128)(2,1)S(1)}, u32[]{:S(2)}, u32[]{:S(2)}) collective-permute-start(bf16[1920,128]{1,0:T(8,128)(2,1)S(1)} %pad_maximum_fusion), channel_id=1, source_target_pairs={{1,0},{2,1},{3,2},{4,3},{5,4},{6,5},{7,6},{8,7},{9,8},{10,9},{11,1... | collective-permute-start | bytes 1474568 | tf_op jit(solution)/shard_map/ppermute | solution.py:307
  41.9 8.6 %collective-permute-start = (bf16[1920,128]{1,0:T(8,128)(2,1)S(1)}, bf16[1920,128]{1,0:T(8,128)(2,1)S(1)}, u32[]{:S(2)}, u32[]{:S(2)}) collective-permute-start(bf16[1920,128]{1,0:T(8,128)(2,1)S(1)} %pad_maximum_fusion), channel_id=1, source_target_pairs={{0,1},{1,2},{2,3},{3,4},{4,5},{5,6},{6,7},{7,8},{8,9},{9,10},{10,1... | collective-permute-start | bytes 1474568 | tf_op jit(solution)/shard_map/ppermute | solution.py:302
  50.6 0.9 shard_map.164
  51.6 3.8 %collective-permute-done.1.high_ref = bf16[1920,128]{1,0:T(8,128)(2,1)S(1)} collective-permute-done((bf16[1920,128]{1,0:T(8,128)(2,1)S(1)}, bf16[1920,128]{1,0:T(8,128)(2,1)S(1)}, u32[]{:S(2)}, u32[]{:S(2)}) %collective-permute-start.1) | collective-permute-done | bytes 491552 | tf_op jit(solution)/shard_map/ppermute | solution.py:307
  55.4 0.9 collective-permute-done.low_ref
  56.3 2.9 %shard_map.165 = (f32[128,128]{1,0:T(8,128)S(1)}, f32[128,128]{1,0:T(8,128)}, f32[128,128]{1,0:T(8,128)}) custom-call(s32[1]{0:T(128)} %bitcast.member_ref, bf16[1920,128]{1,0:T(8,128)(2,1)S(1)} %collective-permute-done.low_ref, bf16[8,112,128]{2,1,0:T(8,128)(2,1)S(1)} %all_to_all.20.mid_ref, bf16[1920,128]{1,0:T(8,128)(2,1)S(1)} %collective-permute-done.1.high_ref, ...), custom_call_target="tpu_custom_call" | custom-call | flops 100000000 | bytes 1000000 | tf_op jit(solution)/shard_map/pallas_call | solution.py:358
  59.8 4.5 %collective-permute-start.2 = (f32[128,128]{1,0:T(8,128)}, f32[128,128]{1,0:T(8,128)S(1)}, u32[]{:S(2)}, u32[]{:S(2)}) collective-permute-start(f32[128,128]{1,0:T(8,128)} %get-tuple-element.32), channel_id=1, source_target_pairs={{0,1},{1,2},{2,3},{3,4},{4,5},{5,6},{6,7},{7,8},{8,9},{9,10},{10,1... | collective-permute-start | bytes 196616 | tf_op jit(solution)/shard_map/ppermute | solution.py:302
  64.3 1.9 %collective-permute-start.3 = (f32[128,128]{1,0:T(8,128)}, f32[128,128]{1,0:T(8,128)}, u32[]{:S(2)}, u32[]{:S(2)}) collective-permute-start(f32[128,128]{1,0:T(8,128)} %get-tuple-element.33), channel_id=1, source_target_pairs={{1,0},{2,1},{3,2},{4,3},{5,4},{6,5},{7,6},{8,7},{9,8},{10,9},{11,1... | collective-permute-start | bytes 196616 | tf_op jit(solution)/shard_map/ppermute | solution.py:307
  66.4 3.4 %shard_map.166 = (f32[8,128,384]{2,1,0:T(8,128)S(1)}, bf16[128,512]{1,0:T(8,128)(2,1)S(1)}) custom-call(s32[1]{0:T(128)} %bitcast.3.band_ref, s32[2,1]{1,0:T(2,128)S(1)} %copy.18.windows_ref, bf16[1,128,512]{2,1,0:T(8,128)(2,1)S(1)} %copy-done.5, bf16[1920,128]{1,0:T(8,128)(2,1)S(1)} %collective-permute-done.low_ref, bf16[8,128,128]{2,1,0:T(8,128)(2,1)S(1)} %copy-done.3, ...), custom_call_target="tpu_custom_call" | custom-call | flops 100000000 | bytes 1000000 | tf_op jit(solution)/shard_map/pallas_call | solution.py:351
  70.4 0.8 copy-done.9
  71.3 1.2 shard_map.167
  72.5 28.7 %all_to_all.21.in_ref = bf16[32,48,128]{2,1,0:T(8,128)(2,1)S(1)} all-to-all(bf16[32,48,128]{2,1,0:T(8,128)(2,1)S(1)} %get-tuple-element.37), channel_id=1, replica_groups=mesh['zh'=2,'y'=4,'x'=4,'zl'=8,'c'=2] {'y','x','c'}, dimensions={0} | all-to-all | bytes 786432 | tf_op jit(solution)/shard_map/all_to_all | solution.py:311
  101.9 8.4 %all-to-all-start.2 = ((bf16[16,48,128]{2,1,0:T(8,128)(2,1)}), bf16[16,48,128]{2,1,0:T(8,128)(2,1)S(1)}, u32[]{:S(2)}, u32[]{:S(2)}) async-start(bf16[16,48,128]{2,1,0:T(8,128)(2,1)} %shard_map.168.after_ref), calls=%async_computation.2 | async-start | bytes 393216 | tf_op jit(solution)/shard_map/all_to_all | solution.py:311
  110.4 1.2 copy-done.1
  111.6 3.9 %shard_map.169 = (bf16[1,128,1024]{2,1,0:T(8,128)(2,1)}, bf16[1,128,512]{2,1,0:T(8,128)(2,1)}, f32[128,1024]{1,0:T(8,128)S(1)}, bf16[128,1024]{1,0:T(8,128)(2,1)S(1)}, bf16[128,1024]{1,0:T(8,128)(2,1)S(1)}) custom-call(f32[128,128]{1,0:T(8,128)S(1)} %get-tuple-element.35.total_ref, bf16[100,1024]{1,0:T(8,128)(2,1)S(1)} %copy-done, ...), custom_call_target="tpu_custom_call" | custom-call | flops 100000000 | bytes 1000000 | tf_op jit(solution)/shard_map/pallas_call | solution.py:378
  115.5 4.1 %collective-permute-start.4 = (bf16[128,1024]{1,0:T(8,128)(2,1)S(1)}, bf16[128,1024]{1,0:T(8,128)(2,1)S(1)}, u32[]{:S(2)}, u32[]{:S(2)}) collective-permute-start(bf16[128,1024]{1,0:T(8,128)(2,1)S(1)} %get-tuple-element.41), channel_id=1, source_target_pairs={{0,1},{1,2},{2,3},{3,4},{4,5},{5,6},{6,7},{7,8},{8,9},{9,10},{10,1... | collective-permute-start | bytes 786440 | tf_op jit(solution)/shard_map/ppermute | solution.py:302
  119.6 1.9 %collective-permute-start.5 = (bf16[128,1024]{1,0:T(8,128)(2,1)S(1)}, bf16[128,1024]{1,0:T(8,128)(2,1)S(1)}, u32[]{:S(2)}, u32[]{:S(2)}) collective-permute-start(bf16[128,1024]{1,0:T(8,128)(2,1)S(1)} %get-tuple-element.42), channel_id=1, source_target_pairs={{1,0},{2,1},{3,2},{4,3},{5,4},{6,5},{7,6},{8,7},{9,8},{10,9},{11,1... | collective-permute-start | bytes 786440 | tf_op jit(solution)/shard_map/ppermute | solution.py:307
  121.5 2.1 %collective-permute-done.4.low_ref = bf16[128,1024]{1,0:T(8,128)(2,1)S(1)} collective-permute-done((bf16[128,1024]{1,0:T(8,128)(2,1)S(1)}, bf16[128,1024]{1,0:T(8,128)(2,1)S(1)}, u32[]{:S(2)}, u32[]{:S(2)}) %collective-permute-start.4) | collective-permute-done | bytes 262176 | tf_op jit(solution)/shard_map/ppermute | solution.py:302
  123.6 3.7 %collective-permute-done.5.high_ref = bf16[128,1024]{1,0:T(8,128)(2,1)S(1)} collective-permute-done((bf16[128,1024]{1,0:T(8,128)(2,1)S(1)}, bf16[128,1024]{1,0:T(8,128)(2,1)S(1)}, u32[]{:S(2)}, u32[]{:S(2)}) %collective-permute-start.5) | collective-permute-done | bytes 262176 | tf_op jit(solution)/shard_map/ppermute | solution.py:307
  128.1 21.6 %all_to_all.22.all_ref = bf16[32,48,128]{2,1,0:T(8,128)(2,1)S(1)} all-to-all(bf16[32,48,128]{2,1,0:T(8,128)(2,1)S(1)} %shard_map.171), channel_id=1, replica_groups=mesh['zh'=2,'y'=4,'x'=4,'zl'=8,'c'=2] {'y','x','c'}, dimensions={0} | all-to-all | bytes 786432 | tf_op jit(solution)/shard_map/all_to_all | solution.py:311
  149.8 0.9 shard_map.172
  (35 shorter events, 2.9 us)
Async XLA Ops:
  0.6 49.9 %copy-start.11 = (f32[3,1024]{1,0:T(4,128)S(1)}, f32[3,1024]{1,0:T(4,128)}, u32[]{:S(2)}) copy-start(f32[3,1024]{1,0:T(4,128)} %edge_weight_ref.1) | copy-start | bytes 36868
  0.6 49.9 %copy-start.10 = (s32[3,1024]{1,0:T(4,128)S(1)}, s32[3,1024]{1,0:T(4,128)}, u32[]{:S(2)}) copy-start(s32[3,1024]{1,0:T(4,128)} %edges_ref.1) | copy-start | bytes 36868
  0.7 49.9 %copy-start.13 = (f32[100]{0:T(128)S(1)}, f32[100]{0:T(128)}, u32[]{:S(2)}) copy-start(f32[100]{0:T(128)} %param.20) | copy-start | bytes 1204
  0.7 49.9 %copy-start.12 = (f32[1024]{0:T(1024)S(1)}, f32[1024]{0:T(1024)}, u32[]{:S(2)}) copy-start(f32[1024]{0:T(1024)} %param.19) | copy-start | bytes 12292
  0.7 55.6 %copy-start.4 = (f32[100,1024]{1,0:T(8,128)S(1)}, f32[100,1024]{1,0:T(8,128)}, u32[]{:S(2)}) copy-start(f32[100,1024]{1,0:T(8,128)} %target_ref.1) | copy-start | bytes 1228804
  37.1 18.3 %collective-permute-start.1 = (bf16[1920,128]{1,0:T(8,128)(2,1)S(1)}, bf16[1920,128]{1,0:T(8,128)(2,1)S(1)}, u32[]{:S(2)}, u32[]{:S(2)}) collective-permute-start(bf16[1920,128]{1,0:T(8,128)(2,1)S(1)} %pad_maximum_fusion), channel_id=1, source_target_pairs={{1,0},{2,1},{3,2},{4,3},{5,4},{6,5},{7,6},{8,7},{9,8},{10,9},{11,1... | collective-permute-start | bytes 1474568 | tf_op jit(solution)/shard_map/ppermute | solution.py:307
  41.9 14.4 %collective-permute-start = (bf16[1920,128]{1,0:T(8,128)(2,1)S(1)}, bf16[1920,128]{1,0:T(8,128)(2,1)S(1)}, u32[]{:S(2)}, u32[]{:S(2)}) collective-permute-start(bf16[1920,128]{1,0:T(8,128)(2,1)S(1)} %pad_maximum_fusion), channel_id=1, source_target_pairs={{0,1},{1,2},{2,3},{3,4},{4,5},{5,6},{6,7},{7,8},{8,9},{9,10},{10,1... | collective-permute-start | bytes 1474568 | tf_op jit(solution)/shard_map/ppermute | solution.py:302
  50.6 15.6 %copy-start.14 = (s32[2,1]{0,1:T(1,128)S(1)}, s32[2,1]{0,1:T(1,128)}, u32[]{:S(2)}) copy-start(s32[2,1]{0,1:T(1,128)} %param.23) | copy-start | bytes 28
  50.6 15.7 %copy-start.3 = (bf16[8,128,128]{2,1,0:T(8,128)(2,1)S(1)}, bf16[8,128,128]{2,1,0:T(8,128)(2,1)}, u32[]{:S(2)}) copy-start(bf16[8,128,128]{2,1,0:T(8,128)(2,1)} %get-tuple-element.28.mid_ref) | copy-start | bytes 786436
  50.6 15.7 %copy-start.5 = (bf16[1,128,512]{2,1,0:T(8,128)(2,1)S(1)}, bf16[1,128,512]{2,1,0:T(8,128)(2,1)}, u32[]{:S(2)}) copy-start(bf16[1,128,512]{2,1,0:T(8,128)(2,1)} %query_ref.3) | copy-start | bytes 393220
  59.2 0.6 copy-start.6
  59.8 10.6 %copy-start.2 = (bf16[1,128,1024]{2,1,0:T(8,128)(2,1)S(1)}, bf16[1,128,1024]{2,1,0:T(8,128)(2,1)}, u32[]{:S(2)}) copy-start(bf16[1,128,1024]{2,1,0:T(8,128)(2,1)} %states_ref.1) | copy-start | bytes 786436
  59.8 10.0 %collective-permute-start.2 = (f32[128,128]{1,0:T(8,128)}, f32[128,128]{1,0:T(8,128)S(1)}, u32[]{:S(2)}, u32[]{:S(2)}) collective-permute-start(f32[128,128]{1,0:T(8,128)} %get-tuple-element.32), channel_id=1, source_target_pairs={{0,1},{1,2},{2,3},{3,4},{4,5},{5,6},{6,7},{7,8},{8,9},{9,10},{10,1... | collective-permute-start | bytes 196616 | tf_op jit(solution)/shard_map/ppermute | solution.py:302
  64.3 6.1 %collective-permute-start.3 = (f32[128,128]{1,0:T(8,128)}, f32[128,128]{1,0:T(8,128)}, u32[]{:S(2)}, u32[]{:S(2)}) collective-permute-start(f32[128,128]{1,0:T(8,128)} %get-tuple-element.33), channel_id=1, source_target_pairs={{1,0},{2,1},{3,2},{4,3},{5,4},{6,5},{7,6},{8,7},{9,8},{10,9},{11,1... | collective-permute-start | bytes 196616 | tf_op jit(solution)/shard_map/ppermute | solution.py:307
  66.4 4.1 %copy-start.7 = (f32[128,128]{1,0:T(8,128)S(1)}, f32[128,128]{1,0:T(8,128)}, u32[]{:S(2)}) copy-start(f32[128,128]{1,0:T(8,128)} %copy-done.6) | copy-start | bytes 196612
  69.8 40.6 %copy-start = (bf16[100,1024]{1,0:T(8,128)(2,1)S(1)}, bf16[100,1024]{1,0:T(8,128)(2,1)}, u32[]{:S(2)}) copy-start(bf16[100,1024]{1,0:T(8,128)(2,1)} %dec_ref.3) | copy-start | bytes 614404
  69.8 0.6 copy-start.8
  70.4 0.8 copy-start.9
  101.9 26.2 %all-to-all-start.2 = ((bf16[16,48,128]{2,1,0:T(8,128)(2,1)}), bf16[16,48,128]{2,1,0:T(8,128)(2,1)S(1)}, u32[]{:S(2)}, u32[]{:S(2)}) async-start(bf16[16,48,128]{2,1,0:T(8,128)(2,1)} %shard_map.168.after_ref), calls=%async_computation.2 | async-start | bytes 393216 | tf_op jit(solution)/shard_map/all_to_all | solution.py:311
  110.3 1.2 copy-start.1
  115.5 8.1 %collective-permute-start.4 = (bf16[128,1024]{1,0:T(8,128)(2,1)S(1)}, bf16[128,1024]{1,0:T(8,128)(2,1)S(1)}, u32[]{:S(2)}, u32[]{:S(2)}) collective-permute-start(bf16[128,1024]{1,0:T(8,128)(2,1)S(1)} %get-tuple-element.41), channel_id=1, source_target_pairs={{0,1},{1,2},{2,3},{3,4},{4,5},{5,6},{6,7},{7,8},{8,9},{9,10},{10,1... | collective-permute-start | bytes 786440 | tf_op jit(solution)/shard_map/ppermute | solution.py:302
  119.6 7.7 %collective-permute-start.5 = (bf16[128,1024]{1,0:T(8,128)(2,1)S(1)}, bf16[128,1024]{1,0:T(8,128)(2,1)S(1)}, u32[]{:S(2)}, u32[]{:S(2)}) collective-permute-start(bf16[128,1024]{1,0:T(8,128)(2,1)S(1)} %get-tuple-element.42), channel_id=1, source_target_pairs={{1,0},{2,1},{3,2},{4,3},{5,4},{6,5},{7,6},{8,7},{9,8},{10,9},{11,1... | collective-permute-start | bytes 786440 | tf_op jit(solution)/shard_map/ppermute | solution.py:307

commit v3 on v2

--- a/solution.py
+++ b/solution.py
@@ -48,22 +48,52 @@
     return lax.dot_general(a, b, dims, preferred_element_type=F32)
 
 
-def call(body, out_shape, spaces, scratch=(), limit=24 * 2**20, exps=0):
+class Landing:
+    def __init__(self, source, target, sem):
+        self.target = target
+        self.copy = pltpu.make_async_copy(source, target, sem)
+        self.copy.start()
+
+    def ready(self):
+        self.copy.wait()
+        return self.target
+
+
+def call(body, out_shape, spaces, args, scratch=(), limit=24 * 2**20, exps=0):
     kinds = {
         "s": pl.BlockSpec(memory_space=pltpu.SMEM),
         "v": pl.BlockSpec(memory_space=pltpu.VMEM),
         "a": pl.BlockSpec(memory_space=pl.ANY),
-        "h": pl.BlockSpec(memory_space=pltpu.HBM),
+        "l": pl.BlockSpec(memory_space=pl.ANY),
     }
     specs = [kinds[space] for space in spaces]
+    landed = [i for i, space in enumerate(spaces) if space == "l"]
+    outs = len(out_shape) if isinstance(out_shape, tuple) else 1
+    if landed:
+        targets = [pltpu.VMEM(args[i].shape, args[i].dtype) for i in landed]
+        scratch = [*targets, pltpu.SemaphoreType.DMA((len(landed),)), *scratch]
+
+    def kernel(*refs):
+        inputs, results, rest = (
+            list(refs[: len(args)]),
+            refs[len(args) : len(args) + outs],
+            refs[len(args) + outs :],
+        )
+        if landed:
+            count = len(landed)
+            for k, i in enumerate(landed):
+                inputs[i] = Landing(inputs[i], rest[k], rest[count].at[k])
+            rest = rest[count + 1 :]
+        body(*inputs, *results, *rest)
+
     return pl.pallas_call(
-        body,
+        kernel,
         out_shape=out_shape,
         in_specs=specs,
         scratch_shapes=list(scratch),
         compiler_params=pltpu.CompilerParams(vmem_limit_bytes=limit),
         cost_estimate=pl.CostEstimate(flops=10**8, bytes_accessed=10**6, transcendentals=exps),
-    )
+    )(*args)
 
 
 def shape(dims, dtype):
@@ -107,15 +137,19 @@
         copy.wait()
 
 
+def bases(band):
+    side = 2 * lax.rem(band, 2) - 1
+    return (band + side) * NODES, band * NODES, (band - side) * NODES
+
+
 def weights_body(band_ref, edges_ref, edge_weight_ref, area_ref, var_ref, mix_ref, weight_ref):
-    base = (band_ref[0] - 1) * NODES
-    local = edges_ref[...] - base
-    for part in range(SPAN // NODES):
-        place = lax.broadcasted_iota(jnp.int32, (NODES, POINTS), 0) + part * NODES
+    edges = edges_ref[...]
+    for part, base in enumerate(bases(band_ref[0])):
+        place = lax.broadcasted_iota(jnp.int32, (NODES, POINTS), 0) + base
         mix = jnp.zeros((NODES, POINTS), F32)
         for slot in range(3):
             mix = mix + jnp.where(
-                local[slot : slot + 1, :] == place, edge_weight_ref[slot : slot + 1, :], 0.0
+                edges[slot : slot + 1, :] == place, edge_weight_ref[slot : slot + 1, :], 0.0
             )
         mix_ref[part * NODES : (part + 1) * NODES, :] = mix.astype(BF16)
     row = jnp.concatenate([var_ref[...], jnp.zeros((1, VARS_LANE - VARS), F32)], axis=1)
@@ -125,22 +159,22 @@
 
 def crps_body(
     member_ref,
-    low_ref,
+    far_ref,
     mid_ref,
-    high_ref,
+    mate_ref,
     mix_ref,
     weight_ref,
     target_ref,
+    to_far_ref,
     own_ref,
-    below_ref,
-    above_ref,
+    to_mate_ref,
     pred_s,
     grad_s,
 ):
     mix = mix_ref[...]
     for member in range(MEMBERS):
         rows = slice(member * VARS_SUB, (member + 1) * VARS_SUB)
-        proj = jnp.concatenate([low_ref[rows], mid_ref[member], high_ref[rows]], axis=1)
+        proj = jnp.concatenate([far_ref[rows], mid_ref[member], mate_ref[rows]], axis=1)
         pred_s[member] = dot(proj, mix, NN)
     grad_s[...] = jnp.zeros(grad_s.shape, BF16)
     me = member_ref[0]
@@ -157,19 +191,19 @@
             BF16
         )
     sums = dot(mix, grad_s[...], NT)
-    below_ref[...] = sums[0:NODES]
+    to_far_ref[...] = sums[0:NODES]
     own_ref[...] = sums[NODES : 2 * NODES]
-    above_ref[...] = sums[2 * NODES : SPAN]
-
-
-def terms_body(own_ref, low_ref, high_ref, states_ref, attn_ref, total_ref, out_ref):
-    total = own_ref[...] + low_ref[...] + high_ref[...]
+    to_mate_ref[...] = sums[2 * NODES : SPAN]
+
+
+def terms_body(own_ref, far_ref, mate_ref, states_ref, attn_ref, total_ref, out_ref):
+    total = own_ref.ready()[...] + far_ref.ready()[...] + mate_ref.ready()[...]
     total_ref[...] = total
     parts = jnp.concatenate(split(total), axis=0)
-    states = states_ref[0]
+    states = states_ref.ready()[0]
     dec = dot(jnp.concatenate([states, states], axis=0), parts, TN)
     out_ref[:, 0:DEC_ROWS, :] = dec.astype(BF16).reshape(NEAR_SIZE, DEC_ROWS, VARS_LANE)
-    attn = attn_ref[...]
+    attn = attn_ref.ready()[...]
     wo = dot(jnp.concatenate([attn, attn], axis=0), parts, TN)
     out_ref[:, DEC_ROWS:ROWS, :] = wo.astype(BF16).reshape(NEAR_SIZE, WO_ROWS, VARS_LANE)
 
@@ -200,25 +234,25 @@
     return (lane < HEAD_DIM).astype(dtype), (lane >= HEAD_DIM).astype(dtype)
 
 
-def band_blocks(low_ref, mid_ref, high_ref, block):
+def band_blocks(far_ref, mid_ref, mate_ref, block):
     first = MEMBERS * VARS_SUB + block * NODES
     rows = slice(first, first + NODES)
-    return jnp.concatenate([low_ref[rows], mid_ref[block], high_ref[rows]], axis=0)
+    return jnp.concatenate([far_ref[rows], mid_ref[block], mate_ref[rows]], axis=0)
 
 
 def forward_body(
-    band_ref, windows_ref, query_ref, low_ref, mid_ref, high_ref, prob_ref, attn_ref
+    band_ref, windows_ref, query_ref, far_ref, mid_ref, mate_ref, prob_ref, attn_ref
 ):
-    base = (band_ref[0] - 1) * NODES
-    place = lax.broadcasted_iota(jnp.int32, (1, SPAN), 1) + base
+    lanes = lax.broadcasted_iota(jnp.int32, (1, NODES), 1)
+    place = jnp.concatenate([lanes + base for base in bases(band_ref[0])], axis=1)
     inside = (place >= windows_ref[0, 0]) & (place < windows_ref[1, 0])
     masks = pair_masks(BF16)
     lane = lax.broadcasted_iota(jnp.int32, (1, PAIR), 1)
     for pair in range(HEADS // 2):
         cols = slice(pair * PAIR, (pair + 1) * PAIR)
         query = query_ref[0, :, cols]
-        keys = band_blocks(low_ref, mid_ref, high_ref, pair)
-        values = band_blocks(low_ref, mid_ref, high_ref, HEADS // 2 + pair)
+        keys = band_blocks(far_ref, mid_ref, mate_ref, pair)
+        values = band_blocks(far_ref, mid_ref, mate_ref, HEADS // 2 + pair)
         outs = []
         for half in range(2):
             scores = dot(query * masks[half], keys, NT) * SCALE
@@ -235,26 +269,29 @@
     dec_ref,
     out_weight_ref,
     query_ref,
-    low_ref,
+    far_ref,
     mid_ref,
-    high_ref,
+    mate_ref,
     prob_ref,
-    after_ref,
     states_ref,
     grad_query_ref,
+    to_far_ref,
     own_ref,
-    below_ref,
-    above_ref,
+    to_mate_ref,
+    done_ref,
     dec_s,
 ):
+    done_ref[...] = jnp.zeros(done_ref.shape, F32)
     dec_s[...] = jnp.zeros(dec_s.shape, BF16)
-    dec_s[0:VARS, :] = dec_ref[...]
+    dec_s[0:VARS, :] = dec_ref.ready()[...]
     dec = dec_s[...]
     grad_states = dot(
-        jnp.concatenate(split(total_ref[...]), axis=1), jnp.concatenate([dec, dec], axis=0), NN
+        jnp.concatenate(split(total_ref.ready()[...]), axis=1), jnp.concatenate([dec, dec], axis=0), NN
     ).astype(BF16)
     states_ref[0] = grad_states
-    grad_out = dot(grad_states, out_weight_ref[...], NT).astype(BF16)
+    grad_out = dot(grad_states, out_weight_ref.ready()[...], NT).astype(BF16)
+    query_ref, prob_ref = query_ref.ready(), prob_ref.ready()
+    far_ref, mid_ref, mate_ref = far_ref.ready(), mid_ref.ready(), mate_ref.ready()
     masks = pair_masks(BF16)
     lane = lax.broadcasted_iota(jnp.int32, (1, PAIR), 1)
     first = lane < HEAD_DIM
@@ -262,8 +299,8 @@
         cols = slice(pair * PAIR, (pair + 1) * PAIR)
         vcols = slice(ATT + pair * PAIR, ATT + (pair + 1) * PAIR)
         query = query_ref[0, :, cols]
-        keys = band_blocks(low_ref, mid_ref, high_ref, pair)
-        values = band_blocks(low_ref, mid_ref, high_ref, HEADS // 2 + pair)
+        keys = band_blocks(far_ref, mid_ref, mate_ref, pair)
+        values = band_blocks(far_ref, mid_ref, mate_ref, HEADS // 2 + pair)
         grads = grad_out[:, cols]
         key_terms, value_terms, query_terms = [], [], []
         for half in range(2):
@@ -280,31 +317,30 @@
         key_term = jnp.where(first, key_terms[0], key_terms[1]) * SCALE
         value_term = jnp.where(first, value_terms[0], value_terms[1])
         for term, where in ((key_term, cols), (value_term, vcols)):
-            below_ref[:, where] = term[0:NODES].astype(BF16)
+            to_far_ref[:, where] = term[0:NODES].astype(BF16)
             own_ref[:, where] = term[NODES : 2 * NODES]
-            above_ref[:, where] = term[2 * NODES : SPAN].astype(BF16)
-
-
-def join_body(own_ref, low_ref, high_ref, key_ref, value_ref, done_ref):
+            to_mate_ref[:, where] = term[2 * NODES : SPAN].astype(BF16)
+
+
+def join_body(own_ref, far_ref, mate_ref, key_ref, value_ref, done_ref):
     done_ref[...] = jnp.zeros(done_ref.shape, F32)
     key_ref[0] = (
-        own_ref[:, 0:ATT] + low_ref[:, 0:ATT].astype(F32) + high_ref[:, 0:ATT].astype(F32)
+        own_ref[:, 0:ATT] + far_ref[:, 0:ATT].astype(F32) + mate_ref[:, 0:ATT].astype(F32)
     ).astype(BF16)
     value_ref[0] = (
         own_ref[:, ATT : 2 * ATT]
-        + low_ref[:, ATT : 2 * ATT].astype(F32)
-        + high_ref[:, ATT : 2 * ATT].astype(F32)
+        + far_ref[:, ATT : 2 * ATT].astype(F32)
+        + mate_ref[:, ATT : 2 * ATT].astype(F32)
     ).astype(BF16)
 
 
-def up(x):
-    count = 64
-    return lax.ppermute(x, SPACE, [(i, i + 1) for i in range(count - 1)])
-
-
-def down(x):
-    count = 64
-    return lax.ppermute(x, SPACE, [(i + 1, i) for i in range(count - 1)])
+def swap_far(x):
+    pairs = [(i, i + 1) for i in range(1, 63, 2)]
+    return lax.ppermute(x, SPACE, pairs + [(target, source) for source, target in pairs])
+
+
+def swap_mate(x):
+    return lax.ppermute(x, "c", [(0, 1), (1, 0)])
 
 
 def exchange(x, axes):
@@ -331,7 +367,7 @@
     proj, kv = call(
         project_body,
         (shape((MEMBERS, VARS_SUB, NODES), BF16), shape((blocks, NODES, PAIR), BF16)),
-        "hhhh",
+        "aaaa", (node_states, dec_weight, key, value,),
         scratch=[
             pltpu.VMEM((NODES, WIDTH), BF16),
             pltpu.VMEM((VARS, WIDTH), BF16),
@@ -339,71 +375,72 @@
             pltpu.SemaphoreType.DMA((2 + blocks,)),
         ],
         limit=None,
-    )(node_states, dec_weight, key, value)
+    )
     mid = exchange(proj, ENS)
     packed = jnp.concatenate([mid.reshape(-1, NODES), kv.reshape(-1, PAIR)], axis=0)
-    low, high = up(packed), down(packed)
+    far, mate = swap_far(packed), swap_mate(packed)
     mix, weight = call(
         weights_body,
         (shape((SPAN, POINTS), BF16), shape((VARS_SUB, POINTS), F32)),
-        "svvvv",
-    )(band, edges, edge_weight, area_weight.reshape(1, -1), var_weight.reshape(1, -1))
+        "svvvv", (band, edges, edge_weight, area_weight.reshape(1, -1), var_weight.reshape(1, -1),),
+    )
     prob, attn = call(
         forward_body,
         (shape((HEADS, NODES, SPAN), F32), shape((NODES, ATT), BF16)),
-        "ssvvvv",
+        "ssvvvv", (band, windows, query, far, kv, mate,),
         exps=10**6,
-    )(band, windows, query, low, kv, high)
+    )
     block = shape((NODES, VARS_LANE), F32)
-    own, below, above = call(
+    to_far, own, to_mate = call(
         crps_body,
         (block, block, block),
-        "svvvvvv",
+        "svvvvvv", (member, far, mid, mate, mix, weight, target,),
         scratch=[
             pltpu.VMEM((MEMBERS, VARS_SUB, POINTS), F32),
             pltpu.VMEM((VARS_LANE, POINTS), BF16),
         ],
-    )(member, low, mid, high, mix, weight, target)
+    )
     total, terms = call(
         terms_body,
         (block, shape((NEAR_SIZE, ROWS, VARS_LANE), BF16)),
-        "vvvvv",
-    )(own, up(above), down(below), node_states, attn)
+        "lllll", (own, swap_far(to_far), swap_mate(to_mate), node_states, attn,),
+    )
     near = exchange(terms, NEAR)
-    near_sums = call(
-        functools.partial(sum_body, FAR_SIZE), shape((FAR_SIZE, ROWS, VARS_LANE), BF16), "v"
-    )(near)
-    far = exchange(near_sums, FAR)
     wide = (NODES, 2 * ATT)
-    grad_states, grad_query, kv_own, kv_below, kv_above = call(
+    grad_states, grad_query, kv_far, kv_own, kv_mate, done = call(
         backward_body,
         (
             shape((1, NODES, WIDTH), BF16),
             shape((1, NODES, ATT), BF16),
+            shape(wide, BF16),
             shape(wide, F32),
             shape(wide, BF16),
-            shape(wide, BF16),
+            shape((8, 128), F32),
         ),
-        "vvvvvvvva",
+        "llllllll", (total, dec_weight, out_weight, query, far, kv, mate, prob,),
         scratch=[pltpu.VMEM((VARS_LANE, WIDTH), BF16)],
-    )(total, dec_weight, out_weight, query, low, kv, high, prob, near_sums)
+    )
+    near_sums = call(
+        functools.partial(sum_body, FAR_SIZE), shape((FAR_SIZE, ROWS, VARS_LANE), BF16), "vv", (near, done,)
+    )
+    along = exchange(near_sums, FAR)
     grad_key, grad_value, joined = call(
         join_body,
         (shape((1, NODES, ATT), BF16), shape((1, NODES, ATT), BF16), shape((8, 128), F32)),
-        "vvv",
-    )(kv_own, up(kv_above), down(kv_below))
+        "vvv", (kv_own, swap_far(kv_far), swap_mate(kv_mate),),
+    )
     far_sums = call(
         functools.partial(sum_body, NEAR_SIZE),
         shape((NEAR_SIZE, ROWS, VARS_LANE), BF16),
-        "vv",
-    )(far, joined)
+        "vv", (along, joined),
+    )
     everything = exchange(far_sums, NEAR)
     grad_wo, grad_dec = call(
         final_body,
         (shape((8, WIDTH), F32), shape((VARS, WIDTH), F32)),
-        "svv",
+        "svv", (band, everything, dec_weight,),
         scratch=[pltpu.VMEM((VARS_LANE, WIDTH), BF16), pltpu.VMEM((WO_ROWS, WIDTH), F32)],
-    )(band, everything, dec_weight)
+    )
     return grad_states, grad_query, grad_key, grad_value, grad_wo, grad_dec
 
 

time: 151 us -> 150 us (level)
  blocking collectives: 83.5 us -> 59.8 us
  waiting for transfers between devices: 10.6 us -> 19.3 us
  starting transfers between devices: 34.3 us -> 40.4 us
  local copies, waits for them, and re-layouts: 3.45 us -> 9.23 us
  Pallas kernels: 16.9 us -> 18.9 us
    all_to_all x3 -> x2, blocking collectives: 83.5 us -> 59.8 us  [exchange(): return lax.all_to_all(x, axes, split_axis=0, concat_axis=0, tiled=True)]
    all_to_all x1 -> x2, starting transfers between devices: 8.41 us -> 17 us  [exchange(): return lax.all_to_all(x, axes, split_axis=0, concat_axis=0, tiled=True)]
    ppermute x6, waiting for transfers between devices: 10.6 us -> 19.1 us  [the longest x3 19 us: swap_far(): lax.ppermute(x, SPACE, pairs + [(target, source) for source, target in pa...]
    unnamed x31 -> x43, local copies, waits for them, and re-layouts: 3.45 us -> 9.23 us
    ppermute x6, starting transfers between devices: 25.9 us -> 23.4 us  [the longest x3 14.7 us: swap_far(): lax.ppermute(x, SPACE, pairs + [(target, source) for source, target in pa...]
    pallas_call x10, Pallas kernels: 16.9 us -> 18.9 us  [call(): pl.pallas_call(kernel, out_shape=out_shape, in_specs=specs, scratch_shape...]
  transfers between devices with their start and end apart: 7 -> 8, of which waited for: 4 -> 3; matrix products, arithmetic and copies ran while one was open for 0% -> 0% of each run, Pallas kernels for 6% -> 7%
where the time goes in v3:
time: 150 us
  blocking collectives  59.8 us (40%)
  starting transfers between devices  40.4 us (27%)
  waiting for transfers between devices  19.3 us (13%)
  Pallas kernels  18.9 us (13%)
  local copies, waits for them, and re-layouts  9.23 us (6%)
    all_to_all x2, blocking collectives, exchange(): return lax.all_to_all(x, axes, split_axis=0, concat_axis=0, tiled=True)  59.8 us
    ppermute x3, waiting for transfers between devices, swap_far(): lax.ppermute(x, SPACE, pairs + [(target, source) for source, target in pa...  19 us
    pallas_call x10, Pallas kernels, call(): pl.pallas_call(kernel, out_shape=out_shape, in_specs=specs, scratch_shape...  18.9 us
    all_to_all x2, starting transfers between devices, exchange(): return lax.all_to_all(x, axes, split_axis=0, concat_axis=0, tiled=True)  17 us
    ppermute x3, starting transfers between devices, swap_far(): lax.ppermute(x, SPACE, pairs + [(target, source) for source, target in pa...  14.7 us
    unnamed x43, local copies, waits for them, and re-layouts  9.23 us
    ppermute x3, starting transfers between devices, swap_mate(): return lax.ppermute(x, 'c', [(0, 1), (1, 0)])  8.66 us
  transfers between devices with their start and end apart: 8, of which 3 were waited for; matrix products, arithmetic and copies ran while one was open for 0% of the time, Pallas kernels for 7%

profile of v3, /device:TPU:1, one launch (start us, length us, event | category | flops | bytes accessed | tf_op | source)
XLA Modules:
  0.0 149.6 jit_solution(17972492680846368231)
XLA Ops:
  0.7 2.2 %shard_map.163 = (bf16[8,112,128]{2,1,0:T(8,128)(2,1)}, bf16[8,128,128]{2,1,0:T(8,128)(2,1)}) custom-call(bf16[1,128,1024]{2,1,0:T(8,128)(2,1)} %refs_3_.4, bf16[100,1024]{1,0:T(8,128)(2,1)} %refs_2_.9, bf16[1,128,512]{2,1,0:T(8,128)(2,1)} %refs_2_.5, bf16[1,128,512]{2,1,0:T(8,128)(2,1)} %refs_3_.3), custom_call_target="tpu_custom_call" | custom-call | flops 100000000 | bytes 1000000 | tf_op jit(solution)/shard_map/pallas_call | solution.py:89
  2.9 33.2 %all_to_all.20.refs_2_ = bf16[8,112,128]{2,1,0:T(8,128)(2,1)S(1)} all-to-all(bf16[8,112,128]{2,1,0:T(8,128)(2,1)} %get-tuple-element.28), channel_id=1, replica_groups=mesh['zh'=2,'y'=4,'x'=4,'zl'=8,'c'=2] {'zh','y'}, dimensions={0} | all-to-all | bytes 458752 | tf_op jit(solution)/shard_map/all_to_all | solution.py:347
  36.1 1.0 pad_maximum_fusion
  37.1 4.8 %collective-permute-start.1 = (bf16[1920,128]{1,0:T(8,128)(2,1)S(1)}, bf16[1920,128]{1,0:T(8,128)(2,1)S(1)}, u32[]{:S(2)}, u32[]{:S(2)}) collective-permute-start(bf16[1920,128]{1,0:T(8,128)(2,1)S(1)} %pad_maximum_fusion), channel_id=1, source_target_pairs={{0,1},{1,0},{2,3},{3,2},{4,5},{5,4},{6,7},{7,6},{8,9},{9,8},{10,11... | collective-permute-start | bytes 1474568 | tf_op jit(solution)/shard_map/ppermute | solution.py:343
  41.9 8.6 %collective-permute-start = (bf16[1920,128]{1,0:T(8,128)(2,1)S(1)}, bf16[1920,128]{1,0:T(8,128)(2,1)S(1)}, u32[]{:S(2)}, u32[]{:S(2)}) collective-permute-start(bf16[1920,128]{1,0:T(8,128)(2,1)S(1)} %pad_maximum_fusion), channel_id=1, source_target_pairs={{1,2},{3,4},{5,6},{7,8},{9,10},{11,12},{13,14},{15,16},{17,18},{19... | collective-permute-start | bytes 1474568 | tf_op jit(solution)/shard_map/ppermute | solution.py:339
  51.4 10.9 %collective-permute-done.refs_1_.refs_3_.refs_4_ = bf16[1920,128]{1,0:T(8,128)(2,1)S(1)} collective-permute-done((bf16[1920,128]{1,0:T(8,128)(2,1)S(1)}, bf16[1920,128]{1,0:T(8,128)(2,1)S(1)}, u32[]{:S(2)}, u32[]{:S(2)}) %collective-permute-start) | collective-permute-done | bytes 491552 | tf_op jit(solution)/shard_map/ppermute | solution.py:339
  62.3 2.9 %shard_map.165 = (f32[128,128]{1,0:T(8,128)}, f32[128,128]{1,0:T(8,128)S(1)}, f32[128,128]{1,0:T(8,128)}) custom-call(s32[1]{0:T(128)} %bitcast.refs_0_, bf16[1920,128]{1,0:T(8,128)(2,1)S(1)} %collective-permute-done.refs_1_.refs_3_.refs_4_, bf16[8,112,128]{2,1,0:T(8,128)(2,1)S(1)} %all_to_all.20.refs_2_, ...), custom_call_target="tpu_custom_call" | custom-call | flops 100000000 | bytes 1000000 | tf_op jit(solution)/shard_map/pallas_call | solution.py:89
  65.8 2.0 %collective-permute-start.2 = (f32[128,128]{1,0:T(8,128)}, f32[128,128]{1,0:T(8,128)S(1)}, u32[]{:S(2)}, u32[]{:S(2)}) collective-permute-start(f32[128,128]{1,0:T(8,128)} %get-tuple-element.33), channel_id=1, source_target_pairs={{1,2},{3,4},{5,6},{7,8},{9,10},{11,12},{13,14},{15,16},{17,18},{19... | collective-permute-start | bytes 196616 | tf_op jit(solution)/shard_map/ppermute | solution.py:339
  67.9 1.9 %collective-permute-start.3 = (f32[128,128]{1,0:T(8,128)}, f32[128,128]{1,0:T(8,128)}, u32[]{:S(2)}, u32[]{:S(2)}) collective-permute-start(f32[128,128]{1,0:T(8,128)} %get-tuple-element.34), channel_id=1, source_target_pairs={{0,1},{1,0},{2,3},{3,2},{4,5},{5,4},{6,7},{7,6},{8,9},{9,8},{10,11... | collective-permute-start | bytes 196616 | tf_op jit(solution)/shard_map/ppermute | solution.py:343
  69.9 0.9 copy-done.8
  70.8 3.4 %shard_map.166 = (f32[8,128,384]{2,1,0:T(8,128)S(1)}, bf16[128,512]{1,0:T(8,128)(2,1)S(1)}) custom-call(s32[1]{0:T(128)} %bitcast.3.refs_0_, s32[2,1]{1,0:T(2,128)S(1)} %copy.18.refs_1_, bf16[1,128,512]{2,1,0:T(8,128)(2,1)S(1)} %copy-done.8, bf16[1920,128]{1,0:T(8,128)(2,1)S(1)} %collective-permute-done.refs_1_.refs_3_.refs_4_, ...), custom_call_target="tpu_custom_call" | custom-call | flops 100000000 | bytes 1000000 | tf_op jit(solution)/shard_map/pallas_call | solution.py:89
  74.9 0.8 copy-done.13
  75.7 1.7 %shard_map.167 = (f32[128,128]{1,0:T(8,128)S(1)}, bf16[32,48,128]{2,1,0:T(8,128)(2,1)S(1)}) custom-call(f32[128,128]{1,0:T(8,128)S(1)} %copy-done.11, f32[128,128]{1,0:T(8,128)S(1)} %copy-done.13, f32[128,128]{1,0:T(8,128)} %collective-permute-done.3.refs_2_, bf16[1,128,1024]{2,1,0:T(8,128)(2,1)S(1)} %copy-done.1, bf16[128,512]{1,0:T(8,128)(2,1)S(1)} %get-tuple-element.35.refs_4_), custom_call_target="tpu_custom_call" | custom-call | flops 100000000 | bytes 1000000 | tf_op jit(solution)/shard_map/pallas_call | solution.py:89
  78.2 11.0 %all-to-all-start.1 = ((bf16[32,48,128]{2,1,0:T(8,128)(2,1)}), bf16[32,48,128]{2,1,0:T(8,128)(2,1)S(1)}, u32[]{:S(2)}, u32[]{:S(2)}) async-start(bf16[32,48,128]{2,1,0:T(8,128)(2,1)} %copy-done.7), calls=%async_computation.1 | async-start | bytes 786432 | tf_op jit(solution)/shard_map/all_to_all | solution.py:347
  89.2 1.2 copy-done.3
  90.4 0.9 copy-done.9
  91.3 5.6 %shard_map.168 = (bf16[1,128,1024]{2,1,0:T(8,128)(2,1)}, bf16[1,128,512]{2,1,0:T(8,128)(2,1)}, bf16[128,1024]{1,0:T(8,128)(2,1)S(1)}, f32[128,1024]{1,0:T(8,128)...) custom-call(f32[128,128]{1,0:T(8,128)S(1)} %get-tuple-element.36.refs_0_, bf16[100,1024]{1,0:T(8,128)(2,1)S(1)} %copy-done, ...), custom_call_target="tpu_custom_call" | custom-call | flops 100000000 | bytes 1000000 | tf_op jit(solution)/shard_map/pallas_call | solution.py:89
  100.1 6.0 %all-to-all-start.2 = ((bf16[16,48,128]{2,1,0:T(8,128)(2,1)}), bf16[16,48,128]{2,1,0:T(8,128)(2,1)S(1)}, u32[]{:S(2)}, u32[]{:S(2)}) async-start(bf16[16,48,128]{2,1,0:T(8,128)(2,1)} %shard_map.170), calls=%async_computation.2 | async-start | bytes 393216 | tf_op jit(solution)/shard_map/all_to_all | solution.py:347
  106.1 4.1 %collective-permute-start.4 = (bf16[128,1024]{1,0:T(8,128)(2,1)}, bf16[128,1024]{1,0:T(8,128)(2,1)S(1)}, u32[]{:S(2)}, u32[]{:S(2)}) collective-permute-start(bf16[128,1024]{1,0:T(8,128)(2,1)} %copy-done.15), channel_id=1, source_target_pairs={{1,2},{3,4},{5,6},{7,8},{9,10},{11,12},{13,14},{15,16},{17,18},{19... | collective-permute-start | bytes 786440 | tf_op jit(solution)/shard_map/ppermute | solution.py:339
  110.2 1.9 %collective-permute-start.5 = (bf16[128,1024]{1,0:T(8,128)(2,1)}, bf16[128,1024]{1,0:T(8,128)(2,1)S(1)}, u32[]{:S(2)}, u32[]{:S(2)}) collective-permute-start(bf16[128,1024]{1,0:T(8,128)(2,1)} %copy-done.14), channel_id=1, source_target_pairs={{0,1},{1,0},{2,3},{3,2},{4,5},{5,4},{6,7},{7,6},{8,9},{9,8},{10,11... | collective-permute-start | bytes 786440 | tf_op jit(solution)/shard_map/ppermute | solution.py:343
  112.1 8.1 %collective-permute-done.4.refs_1_ = bf16[128,1024]{1,0:T(8,128)(2,1)S(1)} collective-permute-done((bf16[128,1024]{1,0:T(8,128)(2,1)}, bf16[128,1024]{1,0:T(8,128)(2,1)S(1)}, u32[]{:S(2)}, u32[]{:S(2)}) %collective-permute-start.4) | collective-permute-done | bytes 262176 | tf_op jit(solution)/shard_map/ppermute | solution.py:339
  120.3 1.0 copy-done.5
  122.1 26.6 %all_to_all.21.refs_1_ = bf16[32,48,128]{2,1,0:T(8,128)(2,1)S(1)} all-to-all(bf16[32,48,128]{2,1,0:T(8,128)(2,1)S(1)} %shard_map.171), channel_id=1, replica_groups=mesh['zh'=2,'y'=4,'x'=4,'zl'=8,'c'=2] {'y','x','c'}, dimensions={0} | all-to-all | bytes 786432 | tf_op jit(solution)/shard_map/all_to_all | solution.py:347
  148.7 0.9 shard_map.172
  (48 shorter events, 6.9 us)
Async XLA Ops:
  0.6 49.9 %copy-start.17 = (f32[3,1024]{1,0:T(4,128)S(1)}, f32[3,1024]{1,0:T(4,128)}, u32[]{:S(2)}) copy-start(f32[3,1024]{1,0:T(4,128)} %refs_2_.6) | copy-start | bytes 36868
  0.6 49.9 %copy-start.16 = (s32[3,1024]{1,0:T(4,128)S(1)}, s32[3,1024]{1,0:T(4,128)}, u32[]{:S(2)}) copy-start(s32[3,1024]{1,0:T(4,128)} %refs_1_.5) | copy-start | bytes 36868
  0.7 49.9 %copy-start.19 = (f32[100]{0:T(128)S(1)}, f32[100]{0:T(128)}, u32[]{:S(2)}) copy-start(f32[100]{0:T(128)} %param.20) | copy-start | bytes 1204
  0.7 49.9 %copy-start.18 = (f32[1024]{0:T(1024)S(1)}, f32[1024]{0:T(1024)}, u32[]{:S(2)}) copy-start(f32[1024]{0:T(1024)} %param.19) | copy-start | bytes 12292
  0.7 61.7 %copy-start.6 = (f32[100,1024]{1,0:T(8,128)S(1)}, f32[100,1024]{1,0:T(8,128)}, u32[]{:S(2)}) copy-start(f32[100,1024]{1,0:T(8,128)} %refs_6_.1) | copy-start | bytes 1228804
  37.1 14.3 %collective-permute-start.1 = (bf16[1920,128]{1,0:T(8,128)(2,1)S(1)}, bf16[1920,128]{1,0:T(8,128)(2,1)S(1)}, u32[]{:S(2)}, u32[]{:S(2)}) collective-permute-start(bf16[1920,128]{1,0:T(8,128)(2,1)S(1)} %pad_maximum_fusion), channel_id=1, source_target_pairs={{0,1},{1,0},{2,3},{3,2},{4,5},{5,4},{6,7},{7,6},{8,9},{9,8},{10,11... | collective-permute-start | bytes 1474568 | tf_op jit(solution)/shard_map/ppermute | solution.py:343
  41.9 20.4 %collective-permute-start = (bf16[1920,128]{1,0:T(8,128)(2,1)S(1)}, bf16[1920,128]{1,0:T(8,128)(2,1)S(1)}, u32[]{:S(2)}, u32[]{:S(2)}) collective-permute-start(bf16[1920,128]{1,0:T(8,128)(2,1)S(1)} %pad_maximum_fusion), channel_id=1, source_target_pairs={{1,2},{3,4},{5,6},{7,8},{9,10},{11,12},{13,14},{15,16},{17,18},{19... | collective-permute-start | bytes 1474568 | tf_op jit(solution)/shard_map/ppermute | solution.py:339
  50.6 19.2 %copy-start.20 = (s32[2,1]{0,1:T(1,128)S(1)}, s32[2,1]{0,1:T(1,128)}, u32[]{:S(2)}) copy-start(s32[2,1]{0,1:T(1,128)} %param.23) | copy-start | bytes 28
  50.6 19.3 %copy-start.2 = (bf16[8,128,128]{2,1,0:T(8,128)(2,1)S(1)}, bf16[8,128,128]{2,1,0:T(8,128)(2,1)}, u32[]{:S(2)}) copy-start(bf16[8,128,128]{2,1,0:T(8,128)(2,1)} %get-tuple-element.29.refs_4_.refs_5_) | copy-start | bytes 786436
  65.8 9.0 %copy-start.1 = (bf16[1,128,1024]{2,1,0:T(8,128)(2,1)S(1)}, bf16[1,128,1024]{2,1,0:T(8,128)(2,1)}, u32[]{:S(2)}) copy-start(bf16[1,128,1024]{2,1,0:T(8,128)(2,1)} %refs_3_.4) | copy-start | bytes 786436
  65.8 8.4 %collective-permute-start.2 = (f32[128,128]{1,0:T(8,128)}, f32[128,128]{1,0:T(8,128)S(1)}, u32[]{:S(2)}, u32[]{:S(2)}) collective-permute-start(f32[128,128]{1,0:T(8,128)} %get-tuple-element.33), channel_id=1, source_target_pairs={{1,2},{3,4},{5,6},{7,8},{9,10},{11,12},{13,14},{15,16},{17,18},{19... | collective-permute-start | bytes 196616 | tf_op jit(solution)/shard_map/ppermute | solution.py:339
  67.9 7.0 %collective-permute-start.3 = (f32[128,128]{1,0:T(8,128)}, f32[128,128]{1,0:T(8,128)}, u32[]{:S(2)}, u32[]{:S(2)}) collective-permute-start(f32[128,128]{1,0:T(8,128)} %get-tuple-element.34), channel_id=1, source_target_pairs={{0,1},{1,0},{2,3},{3,2},{4,5},{5,4},{6,7},{7,6},{8,9},{9,8},{10,11... | collective-permute-start | bytes 196616 | tf_op jit(solution)/shard_map/ppermute | solution.py:343
  69.9 0.9 copy-start.8
  70.8 4.1 %copy-start.11 = (f32[128,128]{1,0:T(8,128)S(1)}, f32[128,128]{1,0:T(8,128)}, u32[]{:S(2)}) copy-start(f32[128,128]{1,0:T(8,128)} %copy-done.10) | copy-start | bytes 196612
  70.8 18.4 %copy-start = (bf16[100,1024]{1,0:T(8,128)(2,1)S(1)}, bf16[100,1024]{1,0:T(8,128)(2,1)}, u32[]{:S(2)}) copy-start(bf16[100,1024]{1,0:T(8,128)(2,1)} %refs_2_.9) | copy-start | bytes 614404
  74.9 0.8 copy-start.13
  78.2 21.2 %all-to-all-start.1 = ((bf16[32,48,128]{2,1,0:T(8,128)(2,1)}), bf16[32,48,128]{2,1,0:T(8,128)(2,1)S(1)}, u32[]{:S(2)}, u32[]{:S(2)}) async-start(bf16[32,48,128]{2,1,0:T(8,128)(2,1)} %copy-done.7), calls=%async_computation.1 | async-start | bytes 786432 | tf_op jit(solution)/shard_map/all_to_all | solution.py:347
  89.2 1.2 copy-start.3
  90.4 0.9 copy-start.9
  96.9 0.8 copy-start.4
  100.1 21.9 %all-to-all-start.2 = ((bf16[16,48,128]{2,1,0:T(8,128)(2,1)}), bf16[16,48,128]{2,1,0:T(8,128)(2,1)S(1)}, u32[]{:S(2)}, u32[]{:S(2)}) async-start(bf16[16,48,128]{2,1,0:T(8,128)(2,1)} %shard_map.170), calls=%async_computation.2 | async-start | bytes 393216 | tf_op jit(solution)/shard_map/all_to_all | solution.py:347
  106.1 14.1 %collective-permute-start.4 = (bf16[128,1024]{1,0:T(8,128)(2,1)}, bf16[128,1024]{1,0:T(8,128)(2,1)S(1)}, u32[]{:S(2)}, u32[]{:S(2)}) collective-permute-start(bf16[128,1024]{1,0:T(8,128)(2,1)} %copy-done.15), channel_id=1, source_target_pairs={{1,2},{3,4},{5,6},{7,8},{9,10},{11,12},{13,14},{15,16},{17,18},{19... | collective-permute-start | bytes 786440 | tf_op jit(solution)/shard_map/ppermute | solution.py:339
  110.2 10.0 %collective-permute-start.5 = (bf16[128,1024]{1,0:T(8,128)(2,1)}, bf16[128,1024]{1,0:T(8,128)(2,1)S(1)}, u32[]{:S(2)}, u32[]{:S(2)}) collective-permute-start(bf16[128,1024]{1,0:T(8,128)(2,1)} %copy-done.14), channel_id=1, source_target_pairs={{0,1},{1,0},{2,3},{3,2},{4,5},{5,4},{6,7},{7,6},{8,9},{9,8},{10,11... | collective-permute-start | bytes 786440 | tf_op jit(solution)/shard_map/ppermute | solution.py:343
  120.3 1.0 copy-start.5
  (5 other events, 3.4 us)

commit v4 on v3

v4 whole, which is shorter than its diff:
```python
import math

import jax
import jax.numpy as jnp
from jax import lax
from jax.experimental import pallas as pl
from jax.experimental.pallas import tpu as pltpu
from jax.sharding import Mesh
from jax.sharding import PartitionSpec as P

HEADS = 8
HEAD_DIM = 64
PAIR = 2 * HEAD_DIM
VARS = 100
VARS_SUB = 112
VARS_LANE = 128
MEMBERS = 8
NODES = 128
POINTS = 1024
SPAN = 3 * NODES
WIDTH = 1024
ATT = 512
SMOOTH_SQUARE = 0.0625
MASKED_SCORE = -1e30
SCALE = 1.0 / math.sqrt(HEAD_DIM)

AXES = ("zh", "y", "x", "zl", "c")
SIZES = (2, 4, 4, 8, 2)
ENS = ("zh", "y")
SPACE = ("x", "zl", "c")
NEAR = ("y", "x", "c")
NEAR_SIZE = 32
FAR = ("zh", "zl")
FAR_SIZE = 16
DEC_ROWS = WIDTH // NEAR_SIZE
WO_ROWS = ATT // NEAR_SIZE
ROWS = DEC_ROWS + WO_ROWS

WHOLE = 58 * 2**20
LONG = 2 * 10**10

F32 = jnp.float32
BF16 = jnp.bfloat16
NN = (((1,), (0,)), ((), ()))
NT = (((1,), (1,)), ((), ()))
TN = (((0,), (0,)), ((), ()))


def dot(a, b, dims):
    return lax.dot_general(a, b, dims, preferred_element_type=F32)


class Landing:
    def __init__(self, source, target, sem):
        self.target = target
        self.copy = pltpu.make_async_copy(source, target, sem)
        self.copy.start()

    def ready(self):
        self.copy.wait()
        return self.target


def call(body, out_shape, spaces, args, scratch=(), out_space=None, cost=10**8, limit=24 * 2**20):
    kinds = {
        "s": pl.BlockSpec(memory_space=pltpu.SMEM),
        "v": pl.BlockSpec(memory_space=pltpu.VMEM),
    }
    left = pl.BlockSpec(memory_space=pl.ANY)
    specs = [kinds.get(space, left) for space in spaces]
    landed = [i for i, space in enumerate(spaces) if space in "ltk"]
    outs = len(out_shape) if isinstance(out_shape, tuple) else 1
    if landed:
        targets = [
            pltpu.VMEM(args[i].shape if spaces[i] == "l" else (NODES, WIDTH), args[i].dtype)
            for i in landed
        ]
        scratch = [*targets, pltpu.SemaphoreType.DMA((len(landed),)), *scratch]

    def kernel(*refs):
        inputs = list(refs[: len(args)])
        results = refs[len(args) : len(args) + outs]
        rest = refs[len(args) + outs :]
        if landed:
            count = len(landed)
            for k, i in enumerate(landed):
                source = inputs[i]
                if spaces[i] == "t":
                    source = source.at[:, pl.ds(0, WIDTH)]
                if spaces[i] == "k":
                    source = source.at[:, pl.ds(WIDTH, WIDTH)]
                inputs[i] = Landing(source, rest[k], rest[count].at[k])
            rest = rest[count + 1 :]
        body(*inputs, *results, *rest)

    return pl.pallas_call(
        kernel,
        out_shape=out_shape,
        in_specs=specs,
        scratch_shapes=list(scratch),
        compiler_params=pltpu.CompilerParams(vmem_limit_bytes=limit),
        cost_estimate=pl.CostEstimate(flops=cost, bytes_accessed=10**6, transcendentals=0),
        **({} if out_space is None else {"out_specs": pl.BlockSpec(memory_space=out_space)}),
    )(*args)


def shape(dims, dtype):
    return jax.ShapeDtypeStruct(dims, dtype)


def smooth_slope(t):
    return t * lax.rsqrt(t * t + SMOOTH_SQUARE)


def split(x):
    high = x.astype(BF16)
    return high, (x - high.astype(F32)).astype(BF16)


def project_body(states_ref, dec_ref, proj_ref, pad_s):
    pad_s[...] = jnp.zeros(pad_s.shape, BF16)
    pad_s[0:VARS, :] = dec_ref.ready()[...]
    proj_ref[...] = dot(pad_s[...], states_ref.ready()[0], NT).astype(BF16)


def pack_body(states_hbm, key_hbm, value_hbm, after_ref, out_hbm, sems):
    copies = [
        pltpu.make_async_copy(states_hbm.at[0], out_hbm.at[:, pl.ds(0, WIDTH)], sems.at[0]),
        pltpu.make_async_copy(key_hbm.at[0], out_hbm.at[:, pl.ds(WIDTH, ATT)], sems.at[1]),
        pltpu.make_async_copy(value_hbm.at[0], out_hbm.at[:, pl.ds(WIDTH + ATT, ATT)], sems.at[2]),
    ]
    for copy in copies:
        copy.start()
    for copy in copies:
        copy.wait()


def pair_body(own_ref, other_ref, out_ref):
    own_ref, other_ref = own_ref.ready(), other_ref.ready()
    for i in range(out_ref.shape[0]):
        out_ref[i, 0:VARS_SUB, :] = own_ref[...]
        out_ref[i, VARS_SUB : 2 * VARS_SUB, :] = other_ref[...]


def bases(band):
    side = 2 * lax.rem(band, 2) - 1
    return (band + side) * NODES, band * NODES, (band - side) * NODES


def weights_body(band_ref, edges_ref, edge_weight_ref, area_ref, var_ref, mix_ref, weight_ref):
    edges = edges_ref[...]
    for part, base in enumerate(bases(band_ref[0])):
        place = lax.broadcasted_iota(jnp.int32, (NODES, POINTS), 0) + base
        mix = jnp.zeros((NODES, POINTS), F32)
        for slot in range(3):
            mix = mix + jnp.where(
                edges[slot : slot + 1, :] == place, edge_weight_ref[slot : slot + 1, :], 0.0
            )
        mix_ref[part * NODES : (part + 1) * NODES, :] = mix.astype(BF16)
    row = jnp.concatenate([var_ref[...], jnp.zeros((1, VARS_LANE - VARS), F32)], axis=1)
    column = jnp.transpose(jnp.broadcast_to(row, (VARS_LANE, VARS_LANE)))[0:VARS_SUB, 0:1]
    weight_ref[...] = column * area_ref[...]


def crps_body(
    member_ref,
    far_ref,
    mid_ref,
    mate_ref,
    mix_ref,
    weight_ref,
    target_ref,
    attn_ref,
    states_ref,
    far_states_ref,
    mate_states_ref,
    terms_ref,
    to_far_ref,
    own_ref,
    to_mate_ref,
    pred_s,
    grad_s,
):
    mix = mix_ref[...]
    for member in range(MEMBERS):
        rows = slice(member * VARS_SUB, (member + 1) * VARS_SUB)
        half = slice((member % 2) * VARS_SUB, (member % 2 + 1) * VARS_SUB)
        proj = jnp.concatenate([far_ref[rows], mid_ref[member // 2, half], mate_ref[rows]], axis=1)
        pred_s[member] = dot(proj, mix, NN)
    grad_s[...] = jnp.zeros(grad_s.shape, BF16)
    me = member_ref[0]
    for first in range(0, VARS, 16):
        rows = min(16, VARS - first)
        mine = pred_s[me, first : first + rows, :]
        total = jnp.zeros_like(mine)
        for member in range(MEMBERS):
            total = total + smooth_slope(mine - pred_s[member, first : first + rows, :])
        slopes = smooth_slope(mine - target_ref[first : first + rows, :]) - total * (
            1.0 / (MEMBERS - 1)
        )
        grad_s[first : first + rows, :] = (weight_ref[first : first + rows, :] * slopes).astype(
            BF16
        )
    grads = grad_s[...]
    sums = dot(mix, grads, NT)
    to_far_ref[...] = sums[0:NODES]
    own_ref[...] = sums[NODES : 2 * NODES]
    to_mate_ref[...] = sums[2 * NODES : SPAN]
    high, low = split(dot(grads, mix, NT))
    bands = (far_states_ref.ready(), states_ref.ready().at[0], mate_states_ref.ready())
    for block in range(WIDTH // NODES):
        cols = slice(block * NODES, (block + 1) * NODES)
        states = jnp.concatenate([band[:, cols] for band in bands], axis=0)
        dec = jnp.transpose(dot(high, states, NN) + dot(low, states, NN)).astype(BF16)
        count = NODES // DEC_ROWS
        terms_ref[block * count : (block + 1) * count, 0:DEC_ROWS, :] = dec.reshape(
            count, DEC_ROWS, VARS_LANE
        )
    attn_ref = attn_ref.ready()
    for block in range(ATT // PAIR):
        first = MEMBERS * VARS_SUB + block * NODES
        rows = slice(first, first + NODES)
        attn = jnp.concatenate([far_ref[rows], attn_ref[block], mate_ref[rows]], axis=0)
        wo = jnp.transpose(dot(high, attn, NN) + dot(low, attn, NN)).astype(BF16)
        count = NODES // WO_ROWS
        terms_ref[block * count : (block + 1) * count, DEC_ROWS:ROWS, :] = wo.reshape(
            count, WO_ROWS, VARS_LANE
        )


def sum_parts(in_ref, out_ref):
    total = in_ref[0].astype(F32)
    for i in range(1, in_ref.shape[0]):
        total = total + in_ref[i].astype(F32)
    total = total.astype(BF16)
    for i in range(out_ref.shape[0]):
        out_ref[i] = total


def near_body(in_ref, own_ref, far_ref, mate_ref, out_ref, total_ref):
    sum_parts(in_ref, out_ref)
    total_ref[...] = own_ref.ready()[...] + far_ref.ready()[...] + mate_ref.ready()[...]


def sum_body(in_ref, after_ref, out_ref):
    sum_parts(in_ref, out_ref)


def final_body(band_ref, all_ref, dec_ref, wo_ref, grad_dec_ref, done_ref, dec_s, wo_s):
    done_ref[...] = jnp.zeros(done_ref.shape, F32)
    dec_s[...] = jnp.zeros(dec_s.shape, BF16)
    dec_s[0:VARS, :] = dec_ref[...]
    band = band_ref[0]
    rows = all_ref[lax.div(band, 2), DEC_ROWS:ROWS, :]
    wo_s[...] = dot(rows, dec_s[...], NN)
    wo_ref[...] = wo_s[pl.ds(pl.multiple_of(lax.rem(band, 2) * 8, 8), 8), :]
    dec = all_ref[:, 0:DEC_ROWS, :].astype(F32).reshape(WIDTH, VARS_LANE)
    grad_dec_ref[...] = jnp.transpose(dec)[0:VARS, :]


def pair_masks(dtype):
    lane = lax.broadcasted_iota(jnp.int32, (1, PAIR), 1)
    return (lane < HEAD_DIM).astype(dtype), (lane >= HEAD_DIM).astype(dtype)


def band_blocks(far_ref, own_ref, mate_ref, pair, first):
    cols = slice(pair * PAIR, (pair + 1) * PAIR)
    side = slice(first + pair * PAIR, first + (pair + 1) * PAIR)
    return jnp.concatenate([far_ref[:, side], own_ref[0, :, cols], mate_ref[:, side]], axis=0)


def forward_body(
    band_ref, windows_ref, query_ref, key_ref, value_ref, far_ref, mate_ref, prob_ref, attn_ref
):
    query_ref, key_ref, value_ref = query_ref.ready(), key_ref.ready(), value_ref.ready()
    far_ref, mate_ref = far_ref.ready(), mate_ref.ready()
    lanes = lax.broadcasted_iota(jnp.int32, (1, NODES), 1)
    place = jnp.concatenate([lanes + base for base in bases(band_ref[0])], axis=1)
    inside = (place >= windows_ref[0, 0]) & (place < windows_ref[1, 0])
    masks = pair_masks(BF16)
    lane = lax.broadcasted_iota(jnp.int32, (1, PAIR), 1)
    for pair in range(HEADS // 2):
        cols = slice(pair * PAIR, (pair + 1) * PAIR)
        query = query_ref[0, :, cols]
        keys = band_blocks(far_ref, key_ref, mate_ref, pair, 0)
        values = band_blocks(far_ref, value_ref, mate_ref, pair, ATT)
        outs = []
        for half in range(2):
            scores = dot(query * masks[half], keys, NT) * SCALE
            scores = jnp.where(inside, scores, MASKED_SCORE)
            exponent = jnp.exp(scores - jnp.max(scores, axis=-1, keepdims=True))
            prob = exponent / jnp.sum(exponent, axis=-1, keepdims=True)
            prob_ref[2 * pair + half] = prob
            outs.append(dot(prob.astype(BF16), values, NN))
        attn_ref[pair] = jnp.where(lane < HEAD_DIM, outs[0], outs[1]).astype(BF16)


def backward_body(
    total_ref,
    dec_ref,
    out_weight_ref,
    query_ref,
    key_ref,
    value_ref,
    far_ref,
    mate_ref,
    prob_ref,
    after_ref,
    states_ref,
    grad_query_ref,
    to_far_ref,
    own_ref,
    to_mate_ref,
    done_ref,
    dec_s,
):
    done_ref[...] = jnp.zeros(done_ref.shape, F32)
    dec_s[...] = jnp.zeros(dec_s.shape, BF16)
    dec_s[0:VARS, :] = dec_ref.ready()[...]
    dec = dec_s[...]
    total = total_ref.ready()[...]
    grad_states = dot(
        jnp.concatenate(split(total), axis=1), jnp.concatenate([dec, dec], axis=0), NN
    ).astype(BF16)
    states_ref[0] = grad_states
    grad_out = dot(grad_states, out_weight_ref.ready()[...], NT).astype(BF16)
    query_ref, key_ref, value_ref = query_ref.ready(), key_ref.ready(), value_ref.ready()
    far_ref, mate_ref, prob_ref = far_ref.ready(), mate_ref.ready(), prob_ref.ready()
    masks = pair_masks(BF16)
    lane = lax.broadcasted_iota(jnp.int32, (1, PAIR), 1)
    first = lane < HEAD_DIM
    for pair in range(HEADS // 2):
        cols = slice(pair * PAIR, (pair + 1) * PAIR)
        vcols = slice(ATT + pair * PAIR, ATT + (pair + 1) * PAIR)
        query = query_ref[0, :, cols]
        keys = band_blocks(far_ref, key_ref, mate_ref, pair, 0)
        values = band_blocks(far_ref, value_ref, mate_ref, pair, ATT)
        grads = grad_out[:, cols]
        key_terms, value_terms, query_terms = [], [], []
        for half in range(2):
            prob = prob_ref[2 * pair + half]
            grad_prob = dot(grads * masks[half], values, NT)
            delta = jnp.sum(prob * grad_prob, axis=-1, keepdims=True)
            grad_scores = (prob * (grad_prob - delta)).astype(BF16)
            value_terms.append(dot(prob.astype(BF16), grads, TN))
            query_terms.append(dot(grad_scores, keys, NN))
            key_terms.append(dot(grad_scores, query, TN))
        grad_query_ref[0, :, cols] = (
            jnp.where(first, query_terms[0], query_terms[1]) * SCALE
        ).astype(BF16)
        key_term = jnp.where(first, key_terms[0], key_terms[1]) * SCALE
        value_term = jnp.where(first, value_terms[0], value_terms[1])
        for term, where in ((key_term, cols), (value_term, vcols)):
            to_far_ref[:, where] = term[0:NODES].astype(BF16)
            own_ref[:, where] = term[NODES : 2 * NODES]
            to_mate_ref[:, where] = term[2 * NODES : SPAN].astype(BF16)


def join_body(own_ref, far_ref, mate_ref, after_ref, key_ref, value_ref):
    own_ref, far_ref, mate_ref = own_ref.ready(), far_ref.ready(), mate_ref.ready()
    for first, ref in ((0, key_ref), (ATT, value_ref)):
        cols = slice(first, first + ATT)
        ref[0] = (
            own_ref[:, cols] + far_ref[:, cols].astype(F32) + mate_ref[:, cols].astype(F32)
        ).astype(BF16)


def swap_far(x):
    pairs = [(i, i + 1) for i in range(1, 63, 2)]
    return lax.ppermute(x, SPACE, pairs + [(target, source) for source, target in pairs])


def swap_mate(x):
    return lax.ppermute(x, "c", [(0, 1), (1, 0)])


def exchange(x, axes):
    return lax.all_to_all(x, axes, split_axis=0, concat_axis=0, tiled=True)


def per_device(
    node_states,
    query,
    key,
    value,
    out_weight,
    dec_weight,
    target,
    area_weight,
    var_weight,
    edges,
    edge_weight,
    windows,
):
    band = lax.axis_index(SPACE).astype(jnp.int32).reshape(1)
    member = (2 * lax.axis_index("y")).astype(jnp.int32).reshape(1)
    proj = call(
        project_body,
        shape((VARS_SUB, NODES), BF16),
        "ll",
        (node_states, dec_weight),
        scratch=[pltpu.VMEM((VARS_SUB, WIDTH), BF16)],
        limit=WHOLE,
    )
    other = lax.ppermute(proj, "zh", [(0, 1), (1, 0)])
    packed = call(
        pack_body,
        shape((NODES, 2 * WIDTH), BF16),
        "aaaa",
        (node_states, key, value, proj),
        scratch=[pltpu.SemaphoreType.DMA((3,))],
        out_space=pl.ANY,
        limit=WHOLE,
    )
    far_band, mate_band = swap_far(packed), swap_mate(packed)
    pairs = call(
        pair_body,
        shape((4, 2 * VARS_SUB, NODES), BF16),
        "ll",
        (proj, other),
        cost=LONG,
    )
    mid = exchange(pairs, "y")
    prob, attn = call(
        forward_body,
        (shape((HEADS, NODES, SPAN), F32), shape((ATT // PAIR, NODES, PAIR), BF16)),
        "sslllkk",
        (band, windows, query, key, value, far_band, mate_band),
    )
    mix, weight = call(
        weights_body,
        (shape((SPAN, POINTS), BF16), shape((VARS_SUB, POINTS), F32)),
        "svvvv",
        (band, edges, edge_weight, area_weight.reshape(1, -1), var_weight.reshape(1, -1)),
    )
    halo = jnp.concatenate([mid.reshape(-1, NODES), attn.reshape(-1, PAIR)], axis=0)
    block = shape((NODES, VARS_LANE), F32)
    terms, to_far, own, to_mate = call(
        crps_body,
        (shape((NEAR_SIZE, ROWS, VARS_LANE), BF16), block, block, block),
        "svvvvvvlltt",
        (
            member,
            swap_far(halo),
            mid,
            swap_mate(halo),
            mix,
            weight,
            target,
            attn,
            node_states,
            far_band,
            mate_band,
        ),
        scratch=[
            pltpu.VMEM((MEMBERS, VARS_SUB, POINTS), F32),
            pltpu.VMEM((VARS_LANE, POINTS), BF16),
        ],
    )
    near = exchange(terms, NEAR)
    near_sums, total = call(
        near_body,
        (shape((FAR_SIZE, ROWS, VARS_LANE), BF16), block),
        "vlll",
        (near, own, swap_far(to_far), swap_mate(to_mate)),
        cost=LONG,
    )
    along = exchange(near_sums, FAR)
    wide = (NODES, 2 * ATT)
    flag = shape((8, 128), F32)
    grad_states, grad_query, kv_far, kv_own, kv_mate, done = call(
        backward_body,
        (
            shape((1, NODES, WIDTH), BF16),
            shape((1, NODES, ATT), BF16),
            shape(wide, BF16),
            shape(wide, F32),
            shape(wide, BF16),
            flag,
        ),
        "llllllkkla",
        (
            total,
            dec_weight,
            out_weight,
            query,
            key,
            value,
            far_band,
            mate_band,
            prob,
            near_sums,
        ),
        scratch=[pltpu.VMEM((VARS_LANE, WIDTH), BF16)],
        limit=WHOLE,
    )
    far_sums = call(
        sum_body,
        shape((NEAR_SIZE, ROWS, VARS_LANE), BF16),
        "va",
        (along, done),
        cost=LONG,
    )
    everything = exchange(far_sums, NEAR)
    grad_wo, grad_dec, last = call(
        final_body,
        (shape((8, WIDTH), F32), shape((VARS, WIDTH), F32), flag),
        "svv",
        (band, everything, dec_weight),
        scratch=[pltpu.VMEM((VARS_LANE, WIDTH), BF16), pltpu.VMEM((WO_ROWS, WIDTH), F32)],
    )
    grad_key, grad_value = call(
        join_body,
        (shape((1, NODES, ATT), BF16), shape((1, NODES, ATT), BF16)),
        "llla",
        (kv_own, swap_far(kv_far), swap_mate(kv_mate), last),
    )
    return grad_states, grad_query, grad_key, grad_value, grad_wo, grad_dec


def solution(mesh):
    fine = Mesh(mesh.devices.reshape(SIZES), AXES)
    in_specs = (
        P(ENS, SPACE, None),
        P(ENS, SPACE, None),
        P(ENS, SPACE, None),
        P(ENS, SPACE, None),
        P(),
        P(),
        P(None, SPACE),
        P(SPACE),
        P(),
        P(None, SPACE),
        P(None, SPACE),
        P(None, SPACE),
    )
    out_specs = (
        P(ENS, SPACE, None),
        P(ENS, SPACE, None),
        P(ENS, SPACE, None),
        P(ENS, SPACE, None),
        P(SPACE, None),
        P(),
    )
    return jax.shard_map(
        per_device, mesh=fine, in_specs=in_specs, out_specs=out_specs, check_vma=False
    )
```

time: 150 us -> 154 us (1.027)
  the two profiles are of different devices: /device:TPU:1 before, /device:TPU:2 now
where the time goes in v4:
time: 154 us
  starting transfers between devices  72.5 us (47%)
  Pallas kernels  38.4 us (25%)
  waiting for transfers between devices  38.2 us (25%)
  local copies, waits for them, and re-layouts  3.4 us (2%)
    pallas_call x11, Pallas kernels, call(): pl.pallas_call(kernel, out_shape=out_shape, in_specs=specs, scratch_shape...  38.4 us
    ppermute x4, waiting for transfers between devices, swap_far(): lax.ppermute(x, SPACE, pairs + [(target, source) for source, target in pa...  27.2 us
    all_to_all x4, starting transfers between devices, exchange(): return lax.all_to_all(x, axes, split_axis=0, concat_axis=0, tiled=True)  24.7 us
    ppermute x4, starting transfers between devices, swap_far(): lax.ppermute(x, SPACE, pairs + [(target, source) for source, target in pa...  24.2 us
    ppermute x1, starting transfers between devices, per_device(): other = lax.ppermute(proj, 'zh', [(0, 1), (1, 0)])  15.7 us
    all_to_all x4, waiting for transfers between devices, exchange(): return lax.all_to_all(x, axes, split_axis=0, concat_axis=0, tiled=True)  11 us
    ppermute x4, starting transfers between devices, swap_mate(): return lax.ppermute(x, 'c', [(0, 1), (1, 0)])  7.81 us
    unnamed x41, local copies, waits for them, and re-layouts  3.4 us
  transfers between devices with their start and end apart: 13, of which 6 were waited for; matrix products, arithmetic and copies ran while one was open for 0% of the time, Pallas kernels for 19%

profile of v4, /device:TPU:2, one launch (start us, length us, event | category | flops | bytes accessed | tf_op | source)
XLA Modules:
  0.0 153.5 jit_solution(8971301657721483613)
XLA Ops:
  0.6 1.9 %shard_map.163.refs_0_.refs_3_ = bf16[112,128]{1,0:T(8,128)(2,1)} custom-call(bf16[1,128,1024]{2,1,0:T(8,128)(2,1)} %refs_8_.1, bf16[100,1024]{1,0:T(8,128)(2,1)} %refs_2_.9), custom_call_target="tpu_custom_call" | custom-call | flops 100000000 | bytes 1000000 | tf_op jit(solution)/shard_map/pallas_call | solution.py:96
  2.5 15.7 %collective-permute-start = (bf16[112,128]{1,0:T(8,128)(2,1)}, bf16[112,128]{1,0:T(8,128)(2,1)S(1)}, u32[]{:S(2)}, u32[]{:S(2)}) collective-permute-start(bf16[112,128]{1,0:T(8,128)(2,1)} %shard_map.163.refs_0_.refs_3_), channel_id=1, source_target_pairs={{0,256},{256,0},{1,257},{257,1},{2,258},{258,2},{3,259},{259,3},{4... | collective-permute-start | bytes 86024 | tf_op jit(solution)/shard_map/ppermute | solution.py:405
  18.3 17.0 %shard_map.165 = bf16[128,2048]{1,0:T(8,128)(2,1)} custom-call(bf16[1,128,1024]{2,1,0:T(8,128)(2,1)} %refs_8_.1, bf16[1,128,512]{2,1,0:T(8,128)(2,1)} %refs_4_.3, bf16[1,128,512]{2,1,0:T(8,128)(2,1)} %refs_5_.1, bf16[112,128]{1,0:T(8,128)(2,1)} %shard_map.163.refs_0_.refs_3_), custom_call_target="tpu_custom_call" | custom-call | flops 100000000 | bytes 1000000 | tf_op jit(solution)/shard_map/pallas_call | solution.py:96
  35.3 2.1 %collective-permute-start.2 = (bf16[128,2048]{1,0:T(8,128)(2,1)}, bf16[128,2048]{1,0:T(8,128)(2,1)S(1)}, u32[]{:S(2)}, u32[]{:S(2)}) collective-permute-start(bf16[128,2048]{1,0:T(8,128)(2,1)} %shard_map.165), channel_id=1, source_target_pairs={{0,1},{1,0},{2,3},{3,2},{4,5},{5,4},{6,7},{7,6},{8,9},{9,8},{10,11... | collective-permute-start | bytes 1572872 | tf_op jit(solution)/shard_map/ppermute | solution.py:374
  37.4 5.7 %collective-permute-start.1 = (bf16[128,2048]{1,0:T(8,128)(2,1)}, bf16[128,2048]{1,0:T(8,128)(2,1)S(1)}, u32[]{:S(2)}, u32[]{:S(2)}) collective-permute-start(bf16[128,2048]{1,0:T(8,128)(2,1)} %shard_map.165), channel_id=1, source_target_pairs={{1,2},{3,4},{5,6},{7,8},{9,10},{11,12},{13,14},{15,16},{17,18},{19... | collective-permute-start | bytes 1572872 | tf_op jit(solution)/shard_map/ppermute | solution.py:370
  44.7 4.6 %all-to-all-start = ((bf16[4,224,128]{2,1,0:T(8,128)(2,1)}), bf16[4,224,128]{2,1,0:T(8,128)(2,1)S(1)}, u32[]{:S(2)}, u32[]{:S(2)}) async-start(bf16[4,224,128]{2,1,0:T(8,128)(2,1)} %shard_map.164), calls=%async_computation | async-start | bytes 458752 | tf_op jit(solution)/shard_map/all_to_all | solution.py:378
  49.4 7.6 %collective-permute-done.1.refs_5_.refs_9_.refs_6_ = bf16[128,2048]{1,0:T(8,128)(2,1)S(1)} collective-permute-done((bf16[128,2048]{1,0:T(8,128)(2,1)}, bf16[128,2048]{1,0:T(8,128)(2,1)S(1)}, u32[]{:S(2)}, u32[]{:S(2)}) %collective-permute-start.1) | collective-permute-done | bytes 524320 | tf_op jit(solution)/shard_map/ppermute | solution.py:370
  57.1 4.0 %shard_map.166 = (f32[8,128,384]{2,1,0:T(8,128)S(1)}, bf16[4,128,128]{2,1,0:T(8,128)(2,1)S(1)}) custom-call(s32[1]{0:T(128)} %bitcast.2.refs_0_, s32[2,1]{1,0:T(2,128)S(1)} %copy.18.refs_1_, bf16[1,128,512]{2,1,0:T(8,128)(2,1)S(1)} %copy-done.7, bf16[1,128,512]{2,1,0:T(8,128)(2,1)S(1)} %copy-done.5, bf16[1,128,512]{2,1,0:T(8,128)(2,1)S(1)} %copy-done.6, ...), custom_call_target="tpu_custom_call" | custom-call | flops 100000000 | bytes 1000000 | tf_op jit(solution)/shard_map/pallas_call | solution.py:96
  61.1 1.2 copy-done.4
  62.3 1.9 %collective-permute-start.4 = (bf16[1408,128]{1,0:T(8,128)(2,1)S(1)}, bf16[1408,128]{1,0:T(8,128)(2,1)S(1)}, u32[]{:S(2)}, u32[]{:S(2)}) collective-permute-start(bf16[1408,128]{1,0:T(8,128)(2,1)S(1)} %pad_maximum_fusion), channel_id=1, source_target_pairs={{0,1},{1,0},{2,3},{3,2},{4,5},{5,4},{6,7},{7,6},{8,9},{9,8},{10,11... | collective-permute-start | bytes 1081352 | tf_op jit(solution)/shard_map/ppermute | solution.py:374
  64.2 6.5 %collective-permute-start.3 = (bf16[1408,128]{1,0:T(8,128)(2,1)S(1)}, bf16[1408,128]{1,0:T(8,128)(2,1)S(1)}, u32[]{:S(2)}, u32[]{:S(2)}) collective-permute-start(bf16[1408,128]{1,0:T(8,128)(2,1)S(1)} %pad_maximum_fusion), channel_id=1, source_target_pairs={{1,2},{3,4},{5,6},{7,8},{9,10},{11,12},{13,14},{15,16},{17,18},{19... | collective-permute-start | bytes 1081352 | tf_op jit(solution)/shard_map/ppermute | solution.py:370
  71.5 9.0 %collective-permute-done.3.refs_1_ = bf16[1408,128]{1,0:T(8,128)(2,1)S(1)} collective-permute-done((bf16[1408,128]{1,0:T(8,128)(2,1)S(1)}, bf16[1408,128]{1,0:T(8,128)(2,1)S(1)}, u32[]{:S(2)}, u32[]{:S(2)}) %collective-permute-start.3) | collective-permute-done | bytes 360480 | tf_op jit(solution)/shard_map/ppermute | solution.py:370
  80.5 4.4 %shard_map.168 = (bf16[32,48,128]{2,1,0:T(8,128)(2,1)}, f32[128,128]{1,0:T(8,128)S(1)}, f32[128,128]{1,0:T(8,128)S(1)}, f32[128,128]{1,0:T(8,128)S(1)}) custom-call(s32[1]{0:T(128)} %bitcast.refs_0_, bf16[1408,128]{1,0:T(8,128)(2,1)S(1)} %collective-permute-done.3.refs_1_, bf16[4,224,128]{2,1,0:T(8,128)(2,1)S(1)} %all-to-all-done.refs_2_, ...), custom_call_target="tpu_custom_call" | custom-call | flops 100000000 | bytes 1000000 | tf_op jit(solution)/shard_map/pallas_call | solution.py:96
  84.9 7.7 %all-to-all-start.1 = ((bf16[32,48,128]{2,1,0:T(8,128)(2,1)}), bf16[32,48,128]{2,1,0:T(8,128)(2,1)S(1)}, u32[]{:S(2)}, u32[]{:S(2)}) async-start(bf16[32,48,128]{2,1,0:T(8,128)(2,1)} %get-tuple-element.30), calls=%async_computation.1 | async-start | bytes 786432 | tf_op jit(solution)/shard_map/all_to_all | solution.py:378
  92.6 5.7 %collective-permute-start.5 = (f32[128,128]{1,0:T(8,128)S(1)}, f32[128,128]{1,0:T(8,128)S(1)}, u32[]{:S(2)}, u32[]{:S(2)}) collective-permute-start(f32[128,128]{1,0:T(8,128)S(1)} %get-tuple-element.32), channel_id=1, source_target_pairs={{1,2},{3,4},{5,6},{7,8},{9,10},{11,12},{13,14},{15,16},{17,18},{19... | collective-permute-start | bytes 196616 | tf_op jit(solution)/shard_map/ppermute | solution.py:370
  98.3 1.9 %collective-permute-start.6 = (f32[128,128]{1,0:T(8,128)S(1)}, f32[128,128]{1,0:T(8,128)S(1)}, u32[]{:S(2)}, u32[]{:S(2)}) collective-permute-start(f32[128,128]{1,0:T(8,128)S(1)} %get-tuple-element.33), channel_id=1, source_target_pairs={{0,1},{1,0},{2,3},{3,2},{4,5},{5,4},{6,7},{7,6},{8,9},{9,8},{10,11... | collective-permute-start | bytes 196616 | tf_op jit(solution)/shard_map/ppermute | solution.py:374
  100.3 5.4 %collective-permute-done.5.refs_2_ = f32[128,128]{1,0:T(8,128)S(1)} collective-permute-done((f32[128,128]{1,0:T(8,128)S(1)}, f32[128,128]{1,0:T(8,128)S(1)}, u32[]{:S(2)}, u32[]{:S(2)}) %collective-permute-start.5) | collective-permute-done | bytes 65568 | tf_op jit(solution)/shard_map/ppermute | solution.py:370
  107.4 4.9 %all-to-all-start.2 = ((bf16[16,48,128]{2,1,0:T(8,128)(2,1)}), bf16[16,48,128]{2,1,0:T(8,128)(2,1)S(1)}, u32[]{:S(2)}, u32[]{:S(2)}) async-start(bf16[16,48,128]{2,1,0:T(8,128)(2,1)} %get-tuple-element.36.refs_9_), calls=%async_computation.2 | async-start | bytes 393216 | tf_op jit(solution)/shard_map/all_to_all | solution.py:378
  112.3 6.0 %shard_map.170 = (bf16[1,128,1024]{2,1,0:T(8,128)(2,1)}, bf16[1,128,512]{2,1,0:T(8,128)(2,1)}, bf16[128,1024]{1,0:T(8,128)(2,1)}, f32[128,1024]{1,0:T(8,128)}, b...) custom-call(f32[128,128]{1,0:T(8,128)} %copy-done.11, bf16[100,1024]{1,0:T(8,128)(2,1)} %refs_2_.9, bf16[512,1024]{1,0:T(8,128)(2,1)} %refs_2_.8, ...), custom_call_target="tpu_custom_call" | custom-call | flops 100000000 | bytes 1000000 | tf_op jit(solution)/shard_map/pallas_call | solution.py:96
  118.3 10.1 %all-to-all-done.2.refs_0_ = bf16[16,48,128]{2,1,0:T(8,128)(2,1)S(1)} async-done(((bf16[16,48,128]{2,1,0:T(8,128)(2,1)}), bf16[16,48,128]{2,1,0:T(8,128)(2,1)S(1)}, u32[]{:S(2)}, u32[]{:S(2)}) %all-to-all-start.2) | async-done | bytes 196640 | tf_op jit(solution)/shard_map/all_to_all | solution.py:378
  129.9 7.5 %all-to-all-start.3 = ((bf16[32,48,128]{2,1,0:T(8,128)(2,1)}), bf16[32,48,128]{2,1,0:T(8,128)(2,1)S(1)}, u32[]{:S(2)}, u32[]{:S(2)}) async-start(bf16[32,48,128]{2,1,0:T(8,128)(2,1)} %shard_map.171), calls=%async_computation.3 | async-start | bytes 786432 | tf_op jit(solution)/shard_map/all_to_all | solution.py:378
  137.5 6.3 %collective-permute-start.7 = (bf16[128,1024]{1,0:T(8,128)(2,1)S(1)}, bf16[128,1024]{1,0:T(8,128)(2,1)S(1)}, u32[]{:S(2)}, u32[]{:S(2)}) collective-permute-start(bf16[128,1024]{1,0:T(8,128)(2,1)S(1)} %copy-done.18), channel_id=1, source_target_pairs={{1,2},{3,4},{5,6},{7,8},{9,10},{11,12},{13,14},{15,16},{17,18},{19... | collective-permute-start | bytes 786440 | tf_op jit(solution)/shard_map/ppermute | solution.py:370
  143.8 1.9 %collective-permute-start.8 = (bf16[128,1024]{1,0:T(8,128)(2,1)S(1)}, bf16[128,1024]{1,0:T(8,128)(2,1)S(1)}, u32[]{:S(2)}, u32[]{:S(2)}) collective-permute-start(bf16[128,1024]{1,0:T(8,128)(2,1)S(1)} %copy-done.17), channel_id=1, source_target_pairs={{0,1},{1,0},{2,3},{3,2},{4,5},{5,4},{6,7},{7,6},{8,9},{9,8},{10,11... | collective-permute-start | bytes 786440 | tf_op jit(solution)/shard_map/ppermute | solution.py:374
  147.4 5.2 %collective-permute-done.7.refs_1_ = bf16[128,1024]{1,0:T(8,128)(2,1)S(1)} collective-permute-done((bf16[128,1024]{1,0:T(8,128)(2,1)S(1)}, bf16[128,1024]{1,0:T(8,128)(2,1)S(1)}, u32[]{:S(2)}, u32[]{:S(2)}) %collective-permute-start.7) | collective-permute-done | bytes 262176 | tf_op jit(solution)/shard_map/ppermute | solution.py:370
  (55 shorter events, 8.2 us)
Async XLA Ops:
  2.5 40.6 %collective-permute-start = (bf16[112,128]{1,0:T(8,128)(2,1)}, bf16[112,128]{1,0:T(8,128)(2,1)S(1)}, u32[]{:S(2)}, u32[]{:S(2)}) collective-permute-start(bf16[112,128]{1,0:T(8,128)(2,1)} %shard_map.163.refs_0_.refs_3_), channel_id=1, source_target_pairs={{0,256},{256,0},{1,257},{257,1},{2,258},{258,2},{3,259},{259,3},{4... | collective-permute-start | bytes 86024 | tf_op jit(solution)/shard_map/ppermute | solution.py:405
  18.3 31.1 %copy-start.19 = (s32[2,1]{0,1:T(1,128)S(1)}, s32[2,1]{0,1:T(1,128)}, u32[]{:S(2)}) copy-start(s32[2,1]{0,1:T(1,128)} %param.23) | copy-start | bytes 28
  35.3 21.8 %copy-start.5 = (bf16[1,128,512]{2,1,0:T(8,128)(2,1)S(1)}, bf16[1,128,512]{2,1,0:T(8,128)(2,1)}, u32[]{:S(2)}) copy-start(bf16[1,128,512]{2,1,0:T(8,128)(2,1)} %refs_4_.3) | copy-start | bytes 393220
  35.3 14.1 %collective-permute-start.2 = (bf16[128,2048]{1,0:T(8,128)(2,1)}, bf16[128,2048]{1,0:T(8,128)(2,1)S(1)}, u32[]{:S(2)}, u32[]{:S(2)}) collective-permute-start(bf16[128,2048]{1,0:T(8,128)(2,1)} %shard_map.165), channel_id=1, source_target_pairs={{0,1},{1,0},{2,3},{3,2},{4,5},{5,4},{6,7},{7,6},{8,9},{9,8},{10,11... | collective-permute-start | bytes 1572872 | tf_op jit(solution)/shard_map/ppermute | solution.py:374
  37.4 19.7 %collective-permute-start.1 = (bf16[128,2048]{1,0:T(8,128)(2,1)}, bf16[128,2048]{1,0:T(8,128)(2,1)S(1)}, u32[]{:S(2)}, u32[]{:S(2)}) collective-permute-start(bf16[128,2048]{1,0:T(8,128)(2,1)} %shard_map.165), channel_id=1, source_target_pairs={{1,2},{3,4},{5,6},{7,8},{9,10},{11,12},{13,14},{15,16},{17,18},{19... | collective-permute-start | bytes 1572872 | tf_op jit(solution)/shard_map/ppermute | solution.py:370
  44.7 26.1 %copy-start.12 = (s32[3,1024]{1,0:T(4,128)S(1)}, s32[3,1024]{1,0:T(4,128)}, u32[]{:S(2)}) copy-start(s32[3,1024]{1,0:T(4,128)} %refs_1_.7) | copy-start | bytes 36868
  44.7 26.1 %copy-start.13 = (f32[3,1024]{1,0:T(4,128)S(1)}, f32[3,1024]{1,0:T(4,128)}, u32[]{:S(2)}) copy-start(f32[3,1024]{1,0:T(4,128)} %refs_2_.7) | copy-start | bytes 36868
  44.7 26.1 %copy-start.14 = (f32[1024]{0:T(1024)S(1)}, f32[1024]{0:T(1024)}, u32[]{:S(2)}) copy-start(f32[1024]{0:T(1024)} %param.19) | copy-start | bytes 12292
  44.7 26.1 %copy-start.16 = (f32[100]{0:T(128)S(1)}, f32[100]{0:T(128)}, u32[]{:S(2)}) copy-start(f32[100]{0:T(128)} %param.20) | copy-start | bytes 1204
  44.7 35.8 %copy-start.2 = (bf16[1,128,1024]{2,1,0:T(8,128)(2,1)S(1)}, bf16[1,128,1024]{2,1,0:T(8,128)(2,1)}, u32[]{:S(2)}) copy-start(bf16[1,128,1024]{2,1,0:T(8,128)(2,1)} %refs_8_.1) | copy-start | bytes 786436
  44.7 35.8 %copy-start.9 = (f32[100,1024]{1,0:T(8,128)S(1)}, f32[100,1024]{1,0:T(8,128)}, u32[]{:S(2)}) copy-start(f32[100,1024]{1,0:T(8,128)} %refs_6_.1) | copy-start | bytes 1228804
  44.7 17.5 %all-to-all-start = ((bf16[4,224,128]{2,1,0:T(8,128)(2,1)}), bf16[4,224,128]{2,1,0:T(8,128)(2,1)S(1)}, u32[]{:S(2)}, u32[]{:S(2)}) async-start(bf16[4,224,128]{2,1,0:T(8,128)(2,1)} %shard_map.164), calls=%async_computation | async-start | bytes 458752 | tf_op jit(solution)/shard_map/all_to_all | solution.py:378
  49.4 35.5 %copy-start = (bf16[128,2048]{1,0:T(8,128)(2,1)}, bf16[128,2048]{1,0:T(8,128)(2,1)S(1)}, u32[]{:S(2)}) copy-start(bf16[128,2048]{1,0:T(8,128)(2,1)S(1)} %collective-permute-done.2.refs_6_.refs_10_.refs_7_) | copy-start | bytes 1572868
  57.1 27.8 %copy-start.1 = (bf16[128,2048]{1,0:T(8,128)(2,1)}, bf16[128,2048]{1,0:T(8,128)(2,1)S(1)}, u32[]{:S(2)}) copy-start(bf16[128,2048]{1,0:T(8,128)(2,1)S(1)} %collective-permute-done.1.refs_5_.refs_9_.refs_6_) | copy-start | bytes 1572868
  62.3 9.2 %collective-permute-start.4 = (bf16[1408,128]{1,0:T(8,128)(2,1)S(1)}, bf16[1408,128]{1,0:T(8,128)(2,1)S(1)}, u32[]{:S(2)}, u32[]{:S(2)}) collective-permute-start(bf16[1408,128]{1,0:T(8,128)(2,1)S(1)} %pad_maximum_fusion), channel_id=1, source_target_pairs={{0,1},{1,0},{2,3},{3,2},{4,5},{5,4},{6,7},{7,6},{8,9},{9,8},{10,11... | collective-permute-start | bytes 1081352 | tf_op jit(solution)/shard_map/ppermute | solution.py:374
  64.2 16.2 %collective-permute-start.3 = (bf16[1408,128]{1,0:T(8,128)(2,1)S(1)}, bf16[1408,128]{1,0:T(8,128)(2,1)S(1)}, u32[]{:S(2)}, u32[]{:S(2)}) collective-permute-start(bf16[1408,128]{1,0:T(8,128)(2,1)S(1)} %pad_maximum_fusion), channel_id=1, source_target_pairs={{1,2},{3,4},{5,6},{7,8},{9,10},{11,12},{13,14},{15,16},{17,18},{19... | collective-permute-start | bytes 1081352 | tf_op jit(solution)/shard_map/ppermute | solution.py:370
  84.9 20.8 %all-to-all-start.1 = ((bf16[32,48,128]{2,1,0:T(8,128)(2,1)}), bf16[32,48,128]{2,1,0:T(8,128)(2,1)S(1)}, u32[]{:S(2)}, u32[]{:S(2)}) async-start(bf16[32,48,128]{2,1,0:T(8,128)(2,1)} %get-tuple-element.30), calls=%async_computation.1 | async-start | bytes 786432 | tf_op jit(solution)/shard_map/all_to_all | solution.py:378
  92.6 13.1 %collective-permute-start.5 = (f32[128,128]{1,0:T(8,128)S(1)}, f32[128,128]{1,0:T(8,128)S(1)}, u32[]{:S(2)}, u32[]{:S(2)}) collective-permute-start(f32[128,128]{1,0:T(8,128)S(1)} %get-tuple-element.32), channel_id=1, source_target_pairs={{1,2},{3,4},{5,6},{7,8},{9,10},{11,12},{13,14},{15,16},{17,18},{19... | collective-permute-start | bytes 196616 | tf_op jit(solution)/shard_map/ppermute | solution.py:370
  98.3 7.3 %collective-permute-start.6 = (f32[128,128]{1,0:T(8,128)S(1)}, f32[128,128]{1,0:T(8,128)S(1)}, u32[]{:S(2)}, u32[]{:S(2)}) collective-permute-start(f32[128,128]{1,0:T(8,128)S(1)} %get-tuple-element.33), channel_id=1, source_target_pairs={{0,1},{1,0},{2,3},{3,2},{4,5},{5,4},{6,7},{7,6},{8,9},{9,8},{10,11... | collective-permute-start | bytes 196616 | tf_op jit(solution)/shard_map/ppermute | solution.py:374
  107.4 21.1 %all-to-all-start.2 = ((bf16[16,48,128]{2,1,0:T(8,128)(2,1)}), bf16[16,48,128]{2,1,0:T(8,128)(2,1)S(1)}, u32[]{:S(2)}, u32[]{:S(2)}) async-start(bf16[16,48,128]{2,1,0:T(8,128)(2,1)} %get-tuple-element.36.refs_9_), calls=%async_computation.2 | async-start | bytes 393216 | tf_op jit(solution)/shard_map/all_to_all | solution.py:378
  129.9 22.7 %copy-start.8 = (f32[128,1024]{1,0:T(8,128)S(1)}, f32[128,1024]{1,0:T(8,128)}, u32[]{:S(2)}) copy-start(f32[128,1024]{1,0:T(8,128)} %get-tuple-element.39.refs_0_) | copy-start | bytes 1572868
  129.9 16.6 %all-to-all-start.3 = ((bf16[32,48,128]{2,1,0:T(8,128)(2,1)}), bf16[32,48,128]{2,1,0:T(8,128)(2,1)S(1)}, u32[]{:S(2)}, u32[]{:S(2)}) async-start(bf16[32,48,128]{2,1,0:T(8,128)(2,1)} %shard_map.171), calls=%async_computation.3 | async-start | bytes 786432 | tf_op jit(solution)/shard_map/all_to_all | solution.py:378
  137.5 15.2 %collective-permute-start.7 = (bf16[128,1024]{1,0:T(8,128)(2,1)S(1)}, bf16[128,1024]{1,0:T(8,128)(2,1)S(1)}, u32[]{:S(2)}, u32[]{:S(2)}) collective-permute-start(bf16[128,1024]{1,0:T(8,128)(2,1)S(1)} %copy-done.18), channel_id=1, source_target_pairs={{1,2},{3,4},{5,6},{7,8},{9,10},{11,12},{13,14},{15,16},{17,18},{19... | collective-permute-start | bytes 786440 | tf_op jit(solution)/shard_map/ppermute | solution.py:370
  143.8 8.9 %collective-permute-start.8 = (bf16[128,1024]{1,0:T(8,128)(2,1)S(1)}, bf16[128,1024]{1,0:T(8,128)(2,1)S(1)}, u32[]{:S(2)}, u32[]{:S(2)}) collective-permute-start(bf16[128,1024]{1,0:T(8,128)(2,1)S(1)} %copy-done.17), channel_id=1, source_target_pairs={{0,1},{1,0},{2,3},{3,2},{4,5},{5,4},{6,7},{7,6},{8,9},{9,8},{10,11... | collective-permute-start | bytes 786440 | tf_op jit(solution)/shard_map/ppermute | solution.py:374
  (9 other events, 87.2 us)

commit v5 on v4

--- a/solution.py
+++ b/solution.py
@@ -61,7 +61,7 @@
         return self.target
 
 
-def call(body, out_shape, spaces, args, scratch=(), out_space=None, cost=10**8, limit=24 * 2**20):
+def call(body, out_shape, spaces, args, scratch=(), cost=10**8, limit=24 * 2**20):
     kinds = {
         "s": pl.BlockSpec(memory_space=pltpu.SMEM),
         "v": pl.BlockSpec(memory_space=pltpu.VMEM),
@@ -100,7 +100,6 @@
         scratch_shapes=list(scratch),
         compiler_params=pltpu.CompilerParams(vmem_limit_bytes=limit),
         cost_estimate=pl.CostEstimate(flops=cost, bytes_accessed=10**6, transcendentals=0),
-        **({} if out_space is None else {"out_specs": pl.BlockSpec(memory_space=out_space)}),
     )(*args)
 
 
@@ -123,11 +122,11 @@
     proj_ref[...] = dot(pad_s[...], states_ref.ready()[0], NT).astype(BF16)
 
 
-def pack_body(states_hbm, key_hbm, value_hbm, after_ref, out_hbm, sems):
+def pack_body(states_hbm, key_hbm, value_hbm, after_ref, out_ref, sems):
     copies = [
-        pltpu.make_async_copy(states_hbm.at[0], out_hbm.at[:, pl.ds(0, WIDTH)], sems.at[0]),
-        pltpu.make_async_copy(key_hbm.at[0], out_hbm.at[:, pl.ds(WIDTH, ATT)], sems.at[1]),
-        pltpu.make_async_copy(value_hbm.at[0], out_hbm.at[:, pl.ds(WIDTH + ATT, ATT)], sems.at[2]),
+        pltpu.make_async_copy(states_hbm.at[0], out_ref.at[:, pl.ds(0, WIDTH)], sems.at[0]),
+        pltpu.make_async_copy(key_hbm.at[0], out_ref.at[:, pl.ds(WIDTH, ATT)], sems.at[1]),
+        pltpu.make_async_copy(value_hbm.at[0], out_ref.at[:, pl.ds(WIDTH + ATT, ATT)], sems.at[2]),
     ]
     for copy in copies:
         copy.start()
@@ -237,17 +236,15 @@
         out_ref[i] = total
 
 
-def near_body(in_ref, own_ref, far_ref, mate_ref, out_ref, total_ref):
+def near_body(in_ref, out_ref):
     sum_parts(in_ref, out_ref)
-    total_ref[...] = own_ref.ready()[...] + far_ref.ready()[...] + mate_ref.ready()[...]
 
 
 def sum_body(in_ref, after_ref, out_ref):
     sum_parts(in_ref, out_ref)
 
 
-def final_body(band_ref, all_ref, dec_ref, wo_ref, grad_dec_ref, done_ref, dec_s, wo_s):
-    done_ref[...] = jnp.zeros(done_ref.shape, F32)
+def final_body(band_ref, all_ref, dec_ref, after_ref, wo_ref, grad_dec_ref, dec_s, wo_s):
     dec_s[...] = jnp.zeros(dec_s.shape, BF16)
     dec_s[0:VARS, :] = dec_ref[...]
     band = band_ref[0]
@@ -296,7 +293,9 @@
 
 
 def backward_body(
-    total_ref,
+    own_sum_ref,
+    far_sum_ref,
+    mate_sum_ref,
     dec_ref,
     out_weight_ref,
     query_ref,
@@ -318,7 +317,7 @@
     dec_s[...] = jnp.zeros(dec_s.shape, BF16)
     dec_s[0:VARS, :] = dec_ref.ready()[...]
     dec = dec_s[...]
-    total = total_ref.ready()[...]
+    total = own_sum_ref.ready()[...] + far_sum_ref.ready()[...] + mate_sum_ref.ready()[...]
     grad_states = dot(
         jnp.concatenate(split(total), axis=1), jnp.concatenate([dec, dec], axis=0), NN
     ).astype(BF16)
@@ -356,7 +355,8 @@
             to_mate_ref[:, where] = term[2 * NODES : SPAN].astype(BF16)
 
 
-def join_body(own_ref, far_ref, mate_ref, after_ref, key_ref, value_ref):
+def join_body(own_ref, far_ref, mate_ref, key_ref, value_ref, done_ref):
+    done_ref[...] = jnp.zeros(done_ref.shape, F32)
     own_ref, far_ref, mate_ref = own_ref.ready(), far_ref.ready(), mate_ref.ready()
     for first, ref in ((0, key_ref), (ATT, value_ref)):
         cols = slice(first, first + ATT)
@@ -409,10 +409,9 @@
         "aaaa",
         (node_states, key, value, proj),
         scratch=[pltpu.SemaphoreType.DMA((3,))],
-        out_space=pl.ANY,
         limit=WHOLE,
     )
-    far_band, mate_band = swap_far(packed), swap_mate(packed)
+    mate_band, far_band = swap_mate(packed), swap_far(packed)
     pairs = call(
         pair_body,
         shape((4, 2 * VARS_SUB, NODES), BF16),
@@ -434,6 +433,7 @@
         (band, edges, edge_weight, area_weight.reshape(1, -1), var_weight.reshape(1, -1)),
     )
     halo = jnp.concatenate([mid.reshape(-1, NODES), attn.reshape(-1, PAIR)], axis=0)
+    mate_halo, far_halo = swap_mate(halo), swap_far(halo)
     block = shape((NODES, VARS_LANE), F32)
     terms, to_far, own, to_mate = call(
         crps_body,
@@ -441,9 +441,9 @@
         "svvvvvvlltt",
         (
             member,
-            swap_far(halo),
+            far_halo,
             mid,
-            swap_mate(halo),
+            mate_halo,
             mix,
             weight,
             target,
@@ -458,12 +458,9 @@
         ],
     )
     near = exchange(terms, NEAR)
-    near_sums, total = call(
-        near_body,
-        (shape((FAR_SIZE, ROWS, VARS_LANE), BF16), block),
-        "vlll",
-        (near, own, swap_far(to_far), swap_mate(to_mate)),
-        cost=LONG,
+    mate_sum, far_sum = swap_mate(to_mate), swap_far(to_far)
+    near_sums = call(
+        near_body, shape((FAR_SIZE, ROWS, VARS_LANE), BF16), "v", (near,), cost=LONG
     )
     along = exchange(near_sums, FAR)
     wide = (NODES, 2 * ATT)
@@ -478,9 +475,11 @@
             shape(wide, BF16),
             flag,
         ),
-        "llllllkkla",
+        "llllllllkkla",
         (
-            total,
+            own,
+            far_sum,
+            mate_sum,
             dec_weight,
             out_weight,
             query,
@@ -493,6 +492,7 @@
         ),
         scratch=[pltpu.VMEM((VARS_LANE, WIDTH), BF16)],
         limit=WHOLE,
+        cost=LONG,
     )
     far_sums = call(
         sum_body,
@@ -502,18 +502,20 @@
         cost=LONG,
     )
     everything = exchange(far_sums, NEAR)
-    grad_wo, grad_dec, last = call(
+    mate_term, far_term = swap_mate(kv_mate), swap_far(kv_far)
+    grad_key, grad_value, joined = call(
+        join_body,
+        (shape((1, NODES, ATT), BF16), shape((1, NODES, ATT), BF16), flag),
+        "lll",
+        (kv_own, far_term, mate_term),
+        cost=LONG,
+    )
+    grad_wo, grad_dec = call(
         final_body,
-        (shape((8, WIDTH), F32), shape((VARS, WIDTH), F32), flag),
-        "svv",
-        (band, everything, dec_weight),
+        (shape((8, WIDTH), F32), shape((VARS, WIDTH), F32)),
+        "svva",
+        (band, everything, dec_weight, joined),
         scratch=[pltpu.VMEM((VARS_LANE, WIDTH), BF16), pltpu.VMEM((WO_ROWS, WIDTH), F32)],
-    )
-    grad_key, grad_value = call(
-        join_body,
-        (shape((1, NODES, ATT), BF16), shape((1, NODES, ATT), BF16)),
-        "llla",
-        (kv_own, swap_far(kv_far), swap_mate(kv_mate), last),
     )
     return grad_states, grad_query, grad_key, grad_value, grad_wo, grad_dec
 

time: 154 us -> 134 us (0.87)
  the two profiles are of different devices: /device:TPU:2 before, /device:TPU:1 now
where the time goes in v5:
time: 134 us; the launch traced here: 133 us
  starting transfers between devices  81.6 us (61%)
  waiting for transfers between devices  23.2 us (17%)
  Pallas kernels  23 us (17%)
  local copies, waits for them, and re-layouts  4.02 us (3%)
    all_to_all x4, starting transfers between devices, exchange(): return lax.all_to_all(x, axes, split_axis=0, concat_axis=0, tiled=True)  45.2 us
    pallas_call x11, Pallas kernels, call(): pl.pallas_call(kernel, out_shape=out_shape, in_specs=specs, scratch_shape...  23 us
    ppermute x1, starting transfers between devices, per_device(): other = lax.ppermute(proj, 'zh', [(0, 1), (1, 0)])  16.3 us
    all_to_all x4, waiting for transfers between devices, exchange(): return lax.all_to_all(x, axes, split_axis=0, concat_axis=0, tiled=True)  15.7 us
    ppermute x4, starting transfers between devices, swap_far(): lax.ppermute(x, SPACE, pairs + [(target, source) for source, target in pa...  11.3 us
    ppermute x4, starting transfers between devices, swap_mate(): return lax.ppermute(x, 'c', [(0, 1), (1, 0)])  8.76 us
    ppermute x4, waiting for transfers between devices, swap_far(): lax.ppermute(x, SPACE, pairs + [(target, source) for source, target in pa...  7.48 us
    unnamed x41, local copies, waits for them, and re-layouts  4.02 us
  transfers between devices with their start and end apart: 13, of which 5 were waited for; matrix products, arithmetic and copies ran while one was open for 0% of the time, Pallas kernels for 12%

profile of v5, /device:TPU:1, one launch (start us, length us, event | category | flops | bytes accessed | tf_op | source)
XLA Modules:
  0.0 132.9 jit_solution(4375365165302007921)
XLA Ops:
  0.6 1.9 %shard_map.163.refs_0_.refs_3_ = bf16[112,128]{1,0:T(8,128)(2,1)} custom-call(bf16[1,128,1024]{2,1,0:T(8,128)(2,1)} %refs_8_.1, bf16[100,1024]{1,0:T(8,128)(2,1)} %refs_2_.7), custom_call_target="tpu_custom_call" | custom-call | flops 100000000 | bytes 1000000 | tf_op jit(solution)/shard_map/pallas_call | solution.py:96
  2.5 16.3 %collective-permute-start = (bf16[112,128]{1,0:T(8,128)(2,1)}, bf16[112,128]{1,0:T(8,128)(2,1)S(1)}, u32[]{:S(2)}, u32[]{:S(2)}) collective-permute-start(bf16[112,128]{1,0:T(8,128)(2,1)} %shard_map.163.refs_0_.refs_3_), channel_id=1, source_target_pairs={{0,256},{256,0},{1,257},{257,1},{2,258},{258,2},{3,259},{259,3},{4... | collective-permute-start | bytes 86024 | tf_op jit(solution)/shard_map/ppermute | solution.py:405
  18.8 1.9 %shard_map.165 = bf16[128,2048]{1,0:T(8,128)(2,1)} custom-call(bf16[1,128,1024]{2,1,0:T(8,128)(2,1)} %refs_8_.1, bf16[1,128,512]{2,1,0:T(8,128)(2,1)} %refs_6_.3, bf16[1,128,512]{2,1,0:T(8,128)(2,1)} %refs_7_.1, bf16[112,128]{1,0:T(8,128)(2,1)} %shard_map.163.refs_0_.refs_3_), custom_call_target="tpu_custom_call" | custom-call | flops 100000000 | bytes 1000000 | tf_op jit(solution)/shard_map/pallas_call | solution.py:96
  20.7 3.0 %collective-permute-start.2 = (bf16[128,2048]{1,0:T(8,128)(2,1)}, bf16[128,2048]{1,0:T(8,128)(2,1)S(1)}, u32[]{:S(2)}, u32[]{:S(2)}) collective-permute-start(bf16[128,2048]{1,0:T(8,128)(2,1)} %shard_map.165), channel_id=1, source_target_pairs={{0,1},{1,0},{2,3},{3,2},{4,5},{5,4},{6,7},{7,6},{8,9},{9,8},{10,11... | collective-permute-start | bytes 1572872 | tf_op jit(solution)/shard_map/ppermute | solution.py:374
  23.7 2.5 %collective-permute-start.1 = (bf16[128,2048]{1,0:T(8,128)(2,1)}, bf16[128,2048]{1,0:T(8,128)(2,1)S(1)}, u32[]{:S(2)}, u32[]{:S(2)}) collective-permute-start(bf16[128,2048]{1,0:T(8,128)(2,1)} %shard_map.165), channel_id=1, source_target_pairs={{1,2},{3,4},{5,6},{7,8},{9,10},{11,12},{13,14},{15,16},{17,18},{19... | collective-permute-start | bytes 1572872 | tf_op jit(solution)/shard_map/ppermute | solution.py:370
  27.9 4.3 %all-to-all-start = ((bf16[4,224,128]{2,1,0:T(8,128)(2,1)}), bf16[4,224,128]{2,1,0:T(8,128)(2,1)S(1)}, u32[]{:S(2)}, u32[]{:S(2)}) async-start(bf16[4,224,128]{2,1,0:T(8,128)(2,1)} %shard_map.164), calls=%async_computation | async-start | bytes 458752 | tf_op jit(solution)/shard_map/all_to_all | solution.py:378
  32.3 2.3 %collective-permute-done.1.refs_5_.refs_9_.refs_8_ = bf16[128,2048]{1,0:T(8,128)(2,1)S(1)} collective-permute-done((bf16[128,2048]{1,0:T(8,128)(2,1)}, bf16[128,2048]{1,0:T(8,128)(2,1)S(1)}, u32[]{:S(2)}, u32[]{:S(2)}) %collective-permute-start.1) | collective-permute-done | bytes 524320 | tf_op jit(solution)/shard_map/ppermute | solution.py:370
  34.7 4.0 %shard_map.166 = (f32[8,128,384]{2,1,0:T(8,128)S(1)}, bf16[4,128,128]{2,1,0:T(8,128)(2,1)S(1)}) custom-call(s32[1]{0:T(128)} %bitcast.2.refs_0_, s32[2,1]{1,0:T(2,128)S(1)} %copy.18.refs_1_, bf16[1,128,512]{2,1,0:T(8,128)(2,1)S(1)} %copy-done.7, bf16[1,128,512]{2,1,0:T(8,128)(2,1)S(1)} %copy-done.4, bf16[1,128,512]{2,1,0:T(8,128)(2,1)S(1)} %copy-done.5, ...), custom_call_target="tpu_custom_call" | custom-call | flops 100000000 | bytes 1000000 | tf_op jit(solution)/shard_map/pallas_call | solution.py:96
  38.7 1.2 copy-done.9
  39.9 1.9 %collective-permute-start.4 = (bf16[1408,128]{1,0:T(8,128)(2,1)S(1)}, bf16[1408,128]{1,0:T(8,128)(2,1)S(1)}, u32[]{:S(2)}, u32[]{:S(2)}) collective-permute-start(bf16[1408,128]{1,0:T(8,128)(2,1)S(1)} %pad_maximum_fusion), channel_id=1, source_target_pairs={{0,1},{1,0},{2,3},{3,2},{4,5},{5,4},{6,7},{7,6},{8,9},{9,8},{10,11... | collective-permute-start | bytes 1081352 | tf_op jit(solution)/shard_map/ppermute | solution.py:374
  41.8 2.8 %collective-permute-start.3 = (bf16[1408,128]{1,0:T(8,128)(2,1)S(1)}, bf16[1408,128]{1,0:T(8,128)(2,1)S(1)}, u32[]{:S(2)}, u32[]{:S(2)}) collective-permute-start(bf16[1408,128]{1,0:T(8,128)(2,1)S(1)} %pad_maximum_fusion), channel_id=1, source_target_pairs={{1,2},{3,4},{5,6},{7,8},{9,10},{11,12},{13,14},{15,16},{17,18},{19... | collective-permute-start | bytes 1081352 | tf_op jit(solution)/shard_map/ppermute | solution.py:370
  45.4 5.1 %collective-permute-done.3.refs_1_ = bf16[1408,128]{1,0:T(8,128)(2,1)S(1)} collective-permute-done((bf16[1408,128]{1,0:T(8,128)(2,1)S(1)}, bf16[1408,128]{1,0:T(8,128)(2,1)S(1)}, u32[]{:S(2)}, u32[]{:S(2)}) %collective-permute-start.3) | collective-permute-done | bytes 360480 | tf_op jit(solution)/shard_map/ppermute | solution.py:370
  50.6 4.4 %shard_map.168 = (bf16[32,48,128]{2,1,0:T(8,128)(2,1)}, f32[128,128]{1,0:T(8,128)S(1)}, f32[128,128]{1,0:T(8,128)S(1)}, f32[128,128]{1,0:T(8,128)S(1)}) custom-call(s32[1]{0:T(128)} %bitcast.refs_0_, bf16[1408,128]{1,0:T(8,128)(2,1)S(1)} %collective-permute-done.3.refs_1_, bf16[4,224,128]{2,1,0:T(8,128)(2,1)S(1)} %all-to-all-done.refs_2_, ...), custom_call_target="tpu_custom_call" | custom-call | flops 100000000 | bytes 1000000 | tf_op jit(solution)/shard_map/pallas_call | solution.py:96
  55.6 23.4 %all-to-all-start.1 = ((bf16[32,48,128]{2,1,0:T(8,128)(2,1)}), bf16[32,48,128]{2,1,0:T(8,128)(2,1)S(1)}, u32[]{:S(2)}, u32[]{:S(2)}) async-start(bf16[32,48,128]{2,1,0:T(8,128)(2,1)} %get-tuple-element.32), calls=%async_computation.1 | async-start | bytes 786432 | tf_op jit(solution)/shard_map/all_to_all | solution.py:378
  79.0 1.9 %collective-permute-start.5 = (f32[128,128]{1,0:T(8,128)S(1)}, f32[128,128]{1,0:T(8,128)S(1)}, u32[]{:S(2)}, u32[]{:S(2)}) collective-permute-start(f32[128,128]{1,0:T(8,128)S(1)} %get-tuple-element.29), channel_id=1, source_target_pairs={{1,2},{3,4},{5,6},{7,8},{9,10},{11,12},{13,14},{15,16},{17,18},{19... | collective-permute-start | bytes 196616 | tf_op jit(solution)/shard_map/ppermute | solution.py:370
  81.0 1.9 %collective-permute-start.6 = (f32[128,128]{1,0:T(8,128)S(1)}, f32[128,128]{1,0:T(8,128)S(1)}, u32[]{:S(2)}, u32[]{:S(2)}) collective-permute-start(f32[128,128]{1,0:T(8,128)S(1)} %get-tuple-element.30), channel_id=1, source_target_pairs={{0,1},{1,0},{2,3},{3,2},{4,5},{5,4},{6,7},{7,6},{8,9},{9,8},{10,11... | collective-permute-start | bytes 196616 | tf_op jit(solution)/shard_map/ppermute | solution.py:374
  82.9 6.3 %all-to-all-done.1.refs_0_ = bf16[32,48,128]{2,1,0:T(8,128)(2,1)S(1)} async-done(((bf16[32,48,128]{2,1,0:T(8,128)(2,1)}), bf16[32,48,128]{2,1,0:T(8,128)(2,1)S(1)}, u32[]{:S(2)}, u32[]{:S(2)}) %all-to-all-start.1) | async-done | bytes 393248 | tf_op jit(solution)/shard_map/all_to_all | solution.py:378
  89.9 5.4 %all-to-all-start.2 = ((bf16[16,48,128]{2,1,0:T(8,128)(2,1)}), bf16[16,48,128]{2,1,0:T(8,128)(2,1)S(1)}, u32[]{:S(2)}, u32[]{:S(2)}) async-start(bf16[16,48,128]{2,1,0:T(8,128)(2,1)} %shard_map.169.refs_11_), calls=%async_computation.2 | async-start | bytes 393216 | tf_op jit(solution)/shard_map/all_to_all | solution.py:378
  96.0 6.1 %shard_map.170 = (bf16[1,128,1024]{2,1,0:T(8,128)(2,1)}, bf16[1,128,512]{2,1,0:T(8,128)(2,1)}, bf16[128,1024]{1,0:T(8,128)(2,1)}, f32[128,1024]{1,0:T(8,128)}, b...) custom-call(f32[128,128]{1,0:T(8,128)} %copy-done.10, f32[128,128]{1,0:T(8,128)} %copy-done.17, f32[128,128]{1,0:T(8,128)} %copy-done.18, ...), custom_call_target="tpu_custom_call" | custom-call | flops 20000000000 | bytes 1000000 | tf_op jit(solution)/shard_map/pallas_call | solution.py:96
  102.1 4.1 %collective-permute-start.7 = (bf16[128,1024]{1,0:T(8,128)(2,1)}, bf16[128,1024]{1,0:T(8,128)(2,1)S(1)}, u32[]{:S(2)}, u32[]{:S(2)}) collective-permute-start(bf16[128,1024]{1,0:T(8,128)(2,1)} %get-tuple-element.36), channel_id=1, source_target_pairs={{1,2},{3,4},{5,6},{7,8},{9,10},{11,12},{13,14},{15,16},{17,18},{19... | collective-permute-start | bytes 786440 | tf_op jit(solution)/shard_map/ppermute | solution.py:370
  106.2 1.9 %collective-permute-start.8 = (bf16[128,1024]{1,0:T(8,128)(2,1)}, bf16[128,1024]{1,0:T(8,128)(2,1)S(1)}, u32[]{:S(2)}, u32[]{:S(2)}) collective-permute-start(bf16[128,1024]{1,0:T(8,128)(2,1)} %get-tuple-element.37), channel_id=1, source_target_pairs={{0,1},{1,0},{2,3},{3,2},{4,5},{5,4},{6,7},{7,6},{8,9},{9,8},{10,11... | collective-permute-start | bytes 786440 | tf_op jit(solution)/shard_map/ppermute | solution.py:374
  109.7 12.1 %all-to-all-start.3 = ((bf16[32,48,128]{2,1,0:T(8,128)(2,1)}), bf16[32,48,128]{2,1,0:T(8,128)(2,1)S(1)}, u32[]{:S(2)}, u32[]{:S(2)}) async-start(bf16[32,48,128]{2,1,0:T(8,128)(2,1)} %shard_map.172), calls=%async_computation.3 | async-start | bytes 786432 | tf_op jit(solution)/shard_map/all_to_all | solution.py:378
  122.7 9.3 %all-to-all-done.3.refs_1_ = bf16[32,48,128]{2,1,0:T(8,128)(2,1)S(1)} async-done(((bf16[32,48,128]{2,1,0:T(8,128)(2,1)}), bf16[32,48,128]{2,1,0:T(8,128)(2,1)S(1)}, u32[]{:S(2)}, u32[]{:S(2)}) %all-to-all-start.3) | async-done | bytes 393248 | tf_op jit(solution)/shard_map/all_to_all | solution.py:378
  132.0 0.9 shard_map.173
  (55 shorter events, 6.9 us)
Async XLA Ops:
  2.5 23.7 %collective-permute-start = (bf16[112,128]{1,0:T(8,128)(2,1)}, bf16[112,128]{1,0:T(8,128)(2,1)S(1)}, u32[]{:S(2)}, u32[]{:S(2)}) collective-permute-start(bf16[112,128]{1,0:T(8,128)(2,1)} %shard_map.163.refs_0_.refs_3_), channel_id=1, source_target_pairs={{0,256},{256,0},{1,257},{257,1},{2,258},{258,2},{3,259},{259,3},{4... | collective-permute-start | bytes 86024 | tf_op jit(solution)/shard_map/ppermute | solution.py:405
  20.7 14.0 %copy-start.4 = (bf16[1,128,512]{2,1,0:T(8,128)(2,1)S(1)}, bf16[1,128,512]{2,1,0:T(8,128)(2,1)}, u32[]{:S(2)}) copy-start(bf16[1,128,512]{2,1,0:T(8,128)(2,1)} %refs_6_.3) | copy-start | bytes 393220
  20.7 14.0 %copy-start.5 = (bf16[1,128,512]{2,1,0:T(8,128)(2,1)S(1)}, bf16[1,128,512]{2,1,0:T(8,128)(2,1)}, u32[]{:S(2)}) copy-start(bf16[1,128,512]{2,1,0:T(8,128)(2,1)} %refs_7_.1) | copy-start | bytes 393220
  20.7 14.0 %copy-start.7 = (bf16[1,128,512]{2,1,0:T(8,128)(2,1)S(1)}, bf16[1,128,512]{2,1,0:T(8,128)(2,1)}, u32[]{:S(2)}) copy-start(bf16[1,128,512]{2,1,0:T(8,128)(2,1)} %refs_5_.1) | copy-start | bytes 393220
  20.7 11.6 %collective-permute-start.2 = (bf16[128,2048]{1,0:T(8,128)(2,1)}, bf16[128,2048]{1,0:T(8,128)(2,1)S(1)}, u32[]{:S(2)}, u32[]{:S(2)}) collective-permute-start(bf16[128,2048]{1,0:T(8,128)(2,1)} %shard_map.165), channel_id=1, source_target_pairs={{0,1},{1,0},{2,3},{3,2},{4,5},{5,4},{6,7},{7,6},{8,9},{9,8},{10,11... | collective-permute-start | bytes 1572872 | tf_op jit(solution)/shard_map/ppermute | solution.py:374
  23.7 10.9 %collective-permute-start.1 = (bf16[128,2048]{1,0:T(8,128)(2,1)}, bf16[128,2048]{1,0:T(8,128)(2,1)S(1)}, u32[]{:S(2)}, u32[]{:S(2)}) collective-permute-start(bf16[128,2048]{1,0:T(8,128)(2,1)} %shard_map.165), channel_id=1, source_target_pairs={{1,2},{3,4},{5,6},{7,8},{9,10},{11,12},{13,14},{15,16},{17,18},{19... | collective-permute-start | bytes 1572872 | tf_op jit(solution)/shard_map/ppermute | solution.py:370
  27.8 16.8 %copy-start.11 = (s32[3,1024]{1,0:T(4,128)S(1)}, s32[3,1024]{1,0:T(4,128)}, u32[]{:S(2)}) copy-start(s32[3,1024]{1,0:T(4,128)} %refs_1_.6) | copy-start | bytes 36868
  27.8 16.8 %copy-start.12 = (f32[3,1024]{1,0:T(4,128)S(1)}, f32[3,1024]{1,0:T(4,128)}, u32[]{:S(2)}) copy-start(f32[3,1024]{1,0:T(4,128)} %refs_2_.6) | copy-start | bytes 36868
  27.8 16.8 %copy-start.13 = (f32[1024]{0:T(1024)S(1)}, f32[1024]{0:T(1024)}, u32[]{:S(2)}) copy-start(f32[1024]{0:T(1024)} %param.19) | copy-start | bytes 12292
  27.9 16.8 %copy-start.14 = (f32[100]{0:T(128)S(1)}, f32[100]{0:T(128)}, u32[]{:S(2)}) copy-start(f32[100]{0:T(128)} %param.20) | copy-start | bytes 1204
  27.9 22.7 %copy-start = (bf16[1,128,1024]{2,1,0:T(8,128)(2,1)S(1)}, bf16[1,128,1024]{2,1,0:T(8,128)(2,1)}, u32[]{:S(2)}) copy-start(bf16[1,128,1024]{2,1,0:T(8,128)(2,1)} %refs_8_.1) | copy-start | bytes 786436
  27.9 22.7 %copy-start.6 = (f32[100,1024]{1,0:T(8,128)S(1)}, f32[100,1024]{1,0:T(8,128)}, u32[]{:S(2)}) copy-start(f32[100,1024]{1,0:T(8,128)} %refs_6_.2) | copy-start | bytes 1228804
  27.9 12.0 %all-to-all-start = ((bf16[4,224,128]{2,1,0:T(8,128)(2,1)}), bf16[4,224,128]{2,1,0:T(8,128)(2,1)S(1)}, u32[]{:S(2)}, u32[]{:S(2)}) async-start(bf16[4,224,128]{2,1,0:T(8,128)(2,1)} %shard_map.164), calls=%async_computation | async-start | bytes 458752 | tf_op jit(solution)/shard_map/all_to_all | solution.py:378
  32.3 22.6 %copy-start.1 = (bf16[128,2048]{1,0:T(8,128)(2,1)}, bf16[128,2048]{1,0:T(8,128)(2,1)S(1)}, u32[]{:S(2)}) copy-start(bf16[128,2048]{1,0:T(8,128)(2,1)S(1)} %collective-permute-done.2.refs_6_.refs_10_.refs_9_) | copy-start | bytes 1572868
  34.7 20.3 %copy-start.2 = (bf16[128,2048]{1,0:T(8,128)(2,1)}, bf16[128,2048]{1,0:T(8,128)(2,1)S(1)}, u32[]{:S(2)}) copy-start(bf16[128,2048]{1,0:T(8,128)(2,1)S(1)} %collective-permute-done.1.refs_5_.refs_9_.refs_8_) | copy-start | bytes 1572868
  39.9 5.5 %collective-permute-start.4 = (bf16[1408,128]{1,0:T(8,128)(2,1)S(1)}, bf16[1408,128]{1,0:T(8,128)(2,1)S(1)}, u32[]{:S(2)}, u32[]{:S(2)}) collective-permute-start(bf16[1408,128]{1,0:T(8,128)(2,1)S(1)} %pad_maximum_fusion), channel_id=1, source_target_pairs={{0,1},{1,0},{2,3},{3,2},{4,5},{5,4},{6,7},{7,6},{8,9},{9,8},{10,11... | collective-permute-start | bytes 1081352 | tf_op jit(solution)/shard_map/ppermute | solution.py:374
  41.8 8.7 %collective-permute-start.3 = (bf16[1408,128]{1,0:T(8,128)(2,1)S(1)}, bf16[1408,128]{1,0:T(8,128)(2,1)S(1)}, u32[]{:S(2)}, u32[]{:S(2)}) collective-permute-start(bf16[1408,128]{1,0:T(8,128)(2,1)S(1)} %pad_maximum_fusion), channel_id=1, source_target_pairs={{1,2},{3,4},{5,6},{7,8},{9,10},{11,12},{13,14},{15,16},{17,18},{19... | collective-permute-start | bytes 1081352 | tf_op jit(solution)/shard_map/ppermute | solution.py:370
  55.6 33.6 %all-to-all-start.1 = ((bf16[32,48,128]{2,1,0:T(8,128)(2,1)}), bf16[32,48,128]{2,1,0:T(8,128)(2,1)S(1)}, u32[]{:S(2)}, u32[]{:S(2)}) async-start(bf16[32,48,128]{2,1,0:T(8,128)(2,1)} %get-tuple-element.32), calls=%async_computation.1 | async-start | bytes 786432 | tf_op jit(solution)/shard_map/all_to_all | solution.py:378
  79.0 16.3 %collective-permute-start.5 = (f32[128,128]{1,0:T(8,128)S(1)}, f32[128,128]{1,0:T(8,128)S(1)}, u32[]{:S(2)}, u32[]{:S(2)}) collective-permute-start(f32[128,128]{1,0:T(8,128)S(1)} %get-tuple-element.29), channel_id=1, source_target_pairs={{1,2},{3,4},{5,6},{7,8},{9,10},{11,12},{13,14},{15,16},{17,18},{19... | collective-permute-start | bytes 196616 | tf_op jit(solution)/shard_map/ppermute | solution.py:370
  81.0 14.4 %collective-permute-start.6 = (f32[128,128]{1,0:T(8,128)S(1)}, f32[128,128]{1,0:T(8,128)S(1)}, u32[]{:S(2)}, u32[]{:S(2)}) collective-permute-start(f32[128,128]{1,0:T(8,128)S(1)} %get-tuple-element.30), channel_id=1, source_target_pairs={{0,1},{1,0},{2,3},{3,2},{4,5},{5,4},{6,7},{7,6},{8,9},{9,8},{10,11... | collective-permute-start | bytes 196616 | tf_op jit(solution)/shard_map/ppermute | solution.py:374
  89.9 18.3 %all-to-all-start.2 = ((bf16[16,48,128]{2,1,0:T(8,128)(2,1)}), bf16[16,48,128]{2,1,0:T(8,128)(2,1)S(1)}, u32[]{:S(2)}, u32[]{:S(2)}) async-start(bf16[16,48,128]{2,1,0:T(8,128)(2,1)} %shard_map.169.refs_11_), calls=%async_computation.2 | async-start | bytes 393216 | tf_op jit(solution)/shard_map/all_to_all | solution.py:378
  102.1 19.7 %collective-permute-start.7 = (bf16[128,1024]{1,0:T(8,128)(2,1)}, bf16[128,1024]{1,0:T(8,128)(2,1)S(1)}, u32[]{:S(2)}, u32[]{:S(2)}) collective-permute-start(bf16[128,1024]{1,0:T(8,128)(2,1)} %get-tuple-element.36), channel_id=1, source_target_pairs={{1,2},{3,4},{5,6},{7,8},{9,10},{11,12},{13,14},{15,16},{17,18},{19... | collective-permute-start | bytes 786440 | tf_op jit(solution)/shard_map/ppermute | solution.py:370
  106.2 15.7 %collective-permute-start.8 = (bf16[128,1024]{1,0:T(8,128)(2,1)}, bf16[128,1024]{1,0:T(8,128)(2,1)S(1)}, u32[]{:S(2)}, u32[]{:S(2)}) collective-permute-start(bf16[128,1024]{1,0:T(8,128)(2,1)} %get-tuple-element.37), channel_id=1, source_target_pairs={{0,1},{1,0},{2,3},{3,2},{4,5},{5,4},{6,7},{7,6},{8,9},{9,8},{10,11... | collective-permute-start | bytes 786440 | tf_op jit(solution)/shard_map/ppermute | solution.py:374
  109.7 22.3 %all-to-all-start.3 = ((bf16[32,48,128]{2,1,0:T(8,128)(2,1)}), bf16[32,48,128]{2,1,0:T(8,128)(2,1)S(1)}, u32[]{:S(2)}, u32[]{:S(2)}) async-start(bf16[32,48,128]{2,1,0:T(8,128)(2,1)} %shard_map.172), calls=%async_computation.3 | async-start | bytes 786432 | tf_op jit(solution)/shard_map/all_to_all | solution.py:378
  (9 other events, 41.0 us)

commit v6 on v5

--- a/solution.py
+++ b/solution.py
@@ -163,16 +163,16 @@
 
 def crps_body(
     member_ref,
+    mate_ref,
+    mid_ref,
     far_ref,
-    mid_ref,
-    mate_ref,
     mix_ref,
     weight_ref,
     target_ref,
     attn_ref,
     states_ref,
+    mate_states_ref,
     far_states_ref,
-    mate_states_ref,
     terms_ref,
     to_far_ref,
     own_ref,
@@ -240,7 +240,7 @@
     sum_parts(in_ref, out_ref)
 
 
-def sum_body(in_ref, after_ref, out_ref):
+def sum_body(in_ref, out_ref):
     sum_parts(in_ref, out_ref)
 
 
@@ -267,7 +267,7 @@
 
 
 def forward_body(
-    band_ref, windows_ref, query_ref, key_ref, value_ref, far_ref, mate_ref, prob_ref, attn_ref
+    band_ref, windows_ref, query_ref, key_ref, value_ref, mate_ref, far_ref, prob_ref, attn_ref
 ):
     query_ref, key_ref, value_ref = query_ref.ready(), key_ref.ready(), value_ref.ready()
     far_ref, mate_ref = far_ref.ready(), mate_ref.ready()
@@ -310,10 +310,8 @@
     to_far_ref,
     own_ref,
     to_mate_ref,
-    done_ref,
     dec_s,
 ):
-    done_ref[...] = jnp.zeros(done_ref.shape, F32)
     dec_s[...] = jnp.zeros(dec_s.shape, BF16)
     dec_s[0:VARS, :] = dec_ref.ready()[...]
     dec = dec_s[...]
@@ -424,7 +422,7 @@
         forward_body,
         (shape((HEADS, NODES, SPAN), F32), shape((ATT // PAIR, NODES, PAIR), BF16)),
         "sslllkk",
-        (band, windows, query, key, value, far_band, mate_band),
+        (band, windows, query, key, value, mate_band, far_band),
     )
     mix, weight = call(
         weights_body,
@@ -441,16 +439,16 @@
         "svvvvvvlltt",
         (
             member,
+            mate_halo,
+            mid,
             far_halo,
-            mid,
-            mate_halo,
             mix,
             weight,
             target,
             attn,
             node_states,
+            mate_band,
             far_band,
-            mate_band,
         ),
         scratch=[
             pltpu.VMEM((MEMBERS, VARS_SUB, POINTS), F32),
@@ -465,7 +463,7 @@
     along = exchange(near_sums, FAR)
     wide = (NODES, 2 * ATT)
     flag = shape((8, 128), F32)
-    grad_states, grad_query, kv_far, kv_own, kv_mate, done = call(
+    grad_states, grad_query, kv_far, kv_own, kv_mate = call(
         backward_body,
         (
             shape((1, NODES, WIDTH), BF16),
@@ -473,7 +471,6 @@
             shape(wide, BF16),
             shape(wide, F32),
             shape(wide, BF16),
-            flag,
         ),
         "llllllllkkla",
         (
@@ -497,8 +494,8 @@
     far_sums = call(
         sum_body,
         shape((NEAR_SIZE, ROWS, VARS_LANE), BF16),
-        "va",
-        (along, done),
+        "v",
+        (along,),
         cost=LONG,
     )
     everything = exchange(far_sums, NEAR)

time: 134 us -> 128 us (0.955)
  waiting for transfers between devices: 23.2 us -> 18 us
    ppermute x4, waiting for transfers between devices: 7.48 us -> 2.38 us  [swap_far(): lax.ppermute(x, SPACE, pairs + [(target, source) for source, target in pa...]
    ppermute x4, starting transfers between devices: 11.3 us -> 14.1 us  [swap_far(): lax.ppermute(x, SPACE, pairs + [(target, source) for source, target in pa...]
    unnamed x41 -> x39, local copies, waits for them, and re-layouts: 4.02 us -> 3.33 us
  transfers between devices with their start and end apart: 13 -> 13, of which waited for: 5 -> 3; matrix products, arithmetic and copies ran while one was open for 0% -> 0% of each run, Pallas kernels for 12% -> 12%
where the time goes in v6:
time: 128 us
  starting transfers between devices  82.1 us (64%)
  Pallas kernels  23 us (18%)
  waiting for transfers between devices  18 us (14%)
  local copies, waits for them, and re-layouts  3.33 us (3%)
    all_to_all x4, starting transfers between devices, exchange(): return lax.all_to_all(x, axes, split_axis=0, concat_axis=0, tiled=True)  43.9 us
    pallas_call x11, Pallas kernels, call(): pl.pallas_call(kernel, out_shape=out_shape, in_specs=specs, scratch_shape...  23 us
    ppermute x1, starting transfers between devices, per_device(): other = lax.ppermute(proj, 'zh', [(0, 1), (1, 0)])  16.3 us
    all_to_all x4, waiting for transfers between devices, exchange(): return lax.all_to_all(x, axes, split_axis=0, concat_axis=0, tiled=True)  15.6 us
    ppermute x4, starting transfers between devices, swap_far(): lax.ppermute(x, SPACE, pairs + [(target, source) for source, target in pa...  14.1 us
    ppermute x4, starting transfers between devices, swap_mate(): return lax.ppermute(x, 'c', [(0, 1), (1, 0)])  7.81 us
    unnamed x39, local copies, waits for them, and re-layouts  3.33 us
  transfers between devices with their start and end apart: 13, of which 3 were waited for; matrix products, arithmetic and copies ran while one was open for 0% of the time, Pallas kernels for 12%

profile of v6, /device:TPU:1, one launch (start us, length us, event | category | flops | bytes accessed | tf_op | source)
XLA Modules:
  0.0 127.6 jit_solution(4236237435673035871)
XLA Ops:
  0.6 1.9 %shard_map.163.refs_0_.refs_3_ = bf16[112,128]{1,0:T(8,128)(2,1)} custom-call(bf16[1,128,1024]{2,1,0:T(8,128)(2,1)} %refs_8_.1, bf16[100,1024]{1,0:T(8,128)(2,1)} %refs_2_.7), custom_call_target="tpu_custom_call" | custom-call | flops 100000000 | bytes 1000000 | tf_op jit(solution)/shard_map/pallas_call | solution.py:96
  2.5 16.3 %collective-permute-start = (bf16[112,128]{1,0:T(8,128)(2,1)}, bf16[112,128]{1,0:T(8,128)(2,1)S(1)}, u32[]{:S(2)}, u32[]{:S(2)}) collective-permute-start(bf16[112,128]{1,0:T(8,128)(2,1)} %shard_map.163.refs_0_.refs_3_), channel_id=1, source_target_pairs={{0,256},{256,0},{1,257},{257,1},{2,258},{258,2},{3,259},{259,3},{4... | collective-permute-start | bytes 86024 | tf_op jit(solution)/shard_map/ppermute | solution.py:403
  18.8 1.9 %shard_map.165 = bf16[128,2048]{1,0:T(8,128)(2,1)} custom-call(bf16[1,128,1024]{2,1,0:T(8,128)(2,1)} %refs_8_.1, bf16[1,128,512]{2,1,0:T(8,128)(2,1)} %refs_6_.3, bf16[1,128,512]{2,1,0:T(8,128)(2,1)} %refs_7_.1, bf16[112,128]{1,0:T(8,128)(2,1)} %shard_map.163.refs_0_.refs_3_), custom_call_target="tpu_custom_call" | custom-call | flops 100000000 | bytes 1000000 | tf_op jit(solution)/shard_map/pallas_call | solution.py:96
  20.7 3.6 %collective-permute-start.2 = (bf16[128,2048]{1,0:T(8,128)(2,1)}, bf16[128,2048]{1,0:T(8,128)(2,1)S(1)}, u32[]{:S(2)}, u32[]{:S(2)}) collective-permute-start(bf16[128,2048]{1,0:T(8,128)(2,1)} %shard_map.165), channel_id=1, source_target_pairs={{1,2},{3,4},{5,6},{7,8},{9,10},{11,12},{13,14},{15,16},{17,18},{19... | collective-permute-start | bytes 1572872 | tf_op jit(solution)/shard_map/ppermute | solution.py:368
  24.3 1.9 %collective-permute-start.1 = (bf16[128,2048]{1,0:T(8,128)(2,1)}, bf16[128,2048]{1,0:T(8,128)(2,1)S(1)}, u32[]{:S(2)}, u32[]{:S(2)}) collective-permute-start(bf16[128,2048]{1,0:T(8,128)(2,1)} %shard_map.165), channel_id=1, source_target_pairs={{0,1},{1,0},{2,3},{3,2},{4,5},{5,4},{6,7},{7,6},{8,9},{9,8},{10,11... | collective-permute-start | bytes 1572872 | tf_op jit(solution)/shard_map/ppermute | solution.py:372
  27.9 4.3 %all-to-all-start = ((bf16[4,224,128]{2,1,0:T(8,128)(2,1)}), bf16[4,224,128]{2,1,0:T(8,128)(2,1)S(1)}, u32[]{:S(2)}, u32[]{:S(2)}) async-start(bf16[4,224,128]{2,1,0:T(8,128)(2,1)} %shard_map.164), calls=%async_computation | async-start | bytes 458752 | tf_op jit(solution)/shard_map/all_to_all | solution.py:376
  32.4 4.0 %shard_map.166 = (f32[8,128,384]{2,1,0:T(8,128)S(1)}, bf16[4,128,128]{2,1,0:T(8,128)(2,1)S(1)}) custom-call(s32[1]{0:T(128)} %bitcast.2.refs_0_, s32[2,1]{1,0:T(2,128)S(1)} %copy.18.refs_1_, bf16[1,128,512]{2,1,0:T(8,128)(2,1)S(1)} %copy-done.7, bf16[1,128,512]{2,1,0:T(8,128)(2,1)S(1)} %copy-done.4, bf16[1,128,512]{2,1,0:T(8,128)(2,1)S(1)} %copy-done.5, ...), custom_call_target="tpu_custom_call" | custom-call | flops 100000000 | bytes 1000000 | tf_op jit(solution)/shard_map/pallas_call | solution.py:96
  36.4 1.2 copy-done.9
  37.6 4.4 %collective-permute-start.4 = (bf16[1408,128]{1,0:T(8,128)(2,1)S(1)}, bf16[1408,128]{1,0:T(8,128)(2,1)S(1)}, u32[]{:S(2)}, u32[]{:S(2)}) collective-permute-start(bf16[1408,128]{1,0:T(8,128)(2,1)S(1)} %pad_maximum_fusion), channel_id=1, source_target_pairs={{1,2},{3,4},{5,6},{7,8},{9,10},{11,12},{13,14},{15,16},{17,18},{19... | collective-permute-start | bytes 1081352 | tf_op jit(solution)/shard_map/ppermute | solution.py:368
  42.1 1.9 %collective-permute-start.3 = (bf16[1408,128]{1,0:T(8,128)(2,1)S(1)}, bf16[1408,128]{1,0:T(8,128)(2,1)S(1)}, u32[]{:S(2)}, u32[]{:S(2)}) collective-permute-start(bf16[1408,128]{1,0:T(8,128)(2,1)S(1)} %pad_maximum_fusion), channel_id=1, source_target_pairs={{0,1},{1,0},{2,3},{3,2},{4,5},{5,4},{6,7},{7,6},{8,9},{9,8},{10,11... | collective-permute-start | bytes 1081352 | tf_op jit(solution)/shard_map/ppermute | solution.py:372
  44.8 2.4 %collective-permute-done.4.refs_3_ = bf16[1408,128]{1,0:T(8,128)(2,1)S(1)} collective-permute-done((bf16[1408,128]{1,0:T(8,128)(2,1)S(1)}, bf16[1408,128]{1,0:T(8,128)(2,1)S(1)}, u32[]{:S(2)}, u32[]{:S(2)}) %collective-permute-start.4) | collective-permute-done | bytes 360480 | tf_op jit(solution)/shard_map/ppermute | solution.py:368
  47.2 4.4 %shard_map.168 = (bf16[32,48,128]{2,1,0:T(8,128)(2,1)}, f32[128,128]{1,0:T(8,128)S(1)}, f32[128,128]{1,0:T(8,128)S(1)}, f32[128,128]{1,0:T(8,128)S(1)}) custom-call(s32[1]{0:T(128)} %bitcast.refs_0_, bf16[1408,128]{1,0:T(8,128)(2,1)S(1)} %collective-permute-done.3.refs_1_, bf16[4,224,128]{2,1,0:T(8,128)(2,1)S(1)} %all-to-all-done.refs_2_, ...), custom_call_target="tpu_custom_call" | custom-call | flops 100000000 | bytes 1000000 | tf_op jit(solution)/shard_map/pallas_call | solution.py:96
  52.2 22.0 %all-to-all-start.1 = ((bf16[32,48,128]{2,1,0:T(8,128)(2,1)}), bf16[32,48,128]{2,1,0:T(8,128)(2,1)S(1)}, u32[]{:S(2)}, u32[]{:S(2)}) async-start(bf16[32,48,128]{2,1,0:T(8,128)(2,1)} %get-tuple-element.31), calls=%async_computation.1 | async-start | bytes 786432 | tf_op jit(solution)/shard_map/all_to_all | solution.py:376
  74.3 1.9 %collective-permute-start.5 = (f32[128,128]{1,0:T(8,128)S(1)}, f32[128,128]{1,0:T(8,128)S(1)}, u32[]{:S(2)}, u32[]{:S(2)}) collective-permute-start(f32[128,128]{1,0:T(8,128)S(1)} %get-tuple-element.28), channel_id=1, source_target_pairs={{1,2},{3,4},{5,6},{7,8},{9,10},{11,12},{13,14},{15,16},{17,18},{19... | collective-permute-start | bytes 196616 | tf_op jit(solution)/shard_map/ppermute | solution.py:368
  76.2 1.9 %collective-permute-start.6 = (f32[128,128]{1,0:T(8,128)S(1)}, f32[128,128]{1,0:T(8,128)S(1)}, u32[]{:S(2)}, u32[]{:S(2)}) collective-permute-start(f32[128,128]{1,0:T(8,128)S(1)} %get-tuple-element.29), channel_id=1, source_target_pairs={{0,1},{1,0},{2,3},{3,2},{4,5},{5,4},{6,7},{7,6},{8,9},{9,8},{10,11... | collective-permute-start | bytes 196616 | tf_op jit(solution)/shard_map/ppermute | solution.py:372
  78.1 6.3 %all-to-all-done.1.refs_0_ = bf16[32,48,128]{2,1,0:T(8,128)(2,1)S(1)} async-done(((bf16[32,48,128]{2,1,0:T(8,128)(2,1)}), bf16[32,48,128]{2,1,0:T(8,128)(2,1)S(1)}, u32[]{:S(2)}, u32[]{:S(2)}) %all-to-all-start.1) | async-done | bytes 393248 | tf_op jit(solution)/shard_map/all_to_all | solution.py:376
  85.2 6.3 %all-to-all-start.2 = ((bf16[16,48,128]{2,1,0:T(8,128)(2,1)}), bf16[16,48,128]{2,1,0:T(8,128)(2,1)S(1)}, u32[]{:S(2)}, u32[]{:S(2)}) async-start(bf16[16,48,128]{2,1,0:T(8,128)(2,1)} %shard_map.169.refs_11_), calls=%async_computation.2 | async-start | bytes 393216 | tf_op jit(solution)/shard_map/all_to_all | solution.py:376
  92.2 6.1 %shard_map.170 = (bf16[1,128,1024]{2,1,0:T(8,128)(2,1)}, bf16[1,128,512]{2,1,0:T(8,128)(2,1)}, bf16[128,1024]{1,0:T(8,128)(2,1)}, f32[128,1024]{1,0:T(8,128)}, bf16[128,1024]{1,0:T(8,128)(2,1)}) custom-call(f32[128,128]{1,0:T(8,128)} %copy-done.10, f32[128,128]{1,0:T(8,128)} %copy-done.16, f32[128,128]{1,0:T(8,128)} %copy-done.17, ...), custom_call_target="tpu_custom_call" | custom-call | flops 20000000000 | bytes 1000000 | tf_op jit(solution)/shard_map/pallas_call | solution.py:96
  98.3 4.1 %collective-permute-start.7 = (bf16[128,1024]{1,0:T(8,128)(2,1)}, bf16[128,1024]{1,0:T(8,128)(2,1)S(1)}, u32[]{:S(2)}, u32[]{:S(2)}) collective-permute-start(bf16[128,1024]{1,0:T(8,128)(2,1)} %get-tuple-element.35), channel_id=1, source_target_pairs={{1,2},{3,4},{5,6},{7,8},{9,10},{11,12},{13,14},{15,16},{17,18},{19... | collective-permute-start | bytes 786440 | tf_op jit(solution)/shard_map/ppermute | solution.py:368
  102.4 2.1 %collective-permute-start.8 = (bf16[128,1024]{1,0:T(8,128)(2,1)}, bf16[128,1024]{1,0:T(8,128)(2,1)S(1)}, u32[]{:S(2)}, u32[]{:S(2)}) collective-permute-start(bf16[128,1024]{1,0:T(8,128)(2,1)} %get-tuple-element.36), channel_id=1, source_target_pairs={{0,1},{1,0},{2,3},{3,2},{4,5},{5,4},{6,7},{7,6},{8,9},{9,8},{10,11... | collective-permute-start | bytes 786440 | tf_op jit(solution)/shard_map/ppermute | solution.py:372
  105.2 11.3 %all-to-all-start.3 = ((bf16[32,48,128]{2,1,0:T(8,128)(2,1)}), bf16[32,48,128]{2,1,0:T(8,128)(2,1)S(1)}, u32[]{:S(2)}, u32[]{:S(2)}) async-start(bf16[32,48,128]{2,1,0:T(8,128)(2,1)} %shard_map.172), calls=%async_computation.3 | async-start | bytes 786432 | tf_op jit(solution)/shard_map/all_to_all | solution.py:376
  116.6 0.8 shard_map.171
  117.4 9.3 %all-to-all-done.3.refs_1_ = bf16[32,48,128]{2,1,0:T(8,128)(2,1)S(1)} async-done(((bf16[32,48,128]{2,1,0:T(8,128)(2,1)}), bf16[32,48,128]{2,1,0:T(8,128)(2,1)S(1)}, u32[]{:S(2)}, u32[]{:S(2)}) %all-to-all-start.3) | async-done | bytes 393248 | tf_op jit(solution)/shard_map/all_to_all | solution.py:376
  126.7 0.9 shard_map.173
  (53 shorter events, 5.3 us)
Async XLA Ops:
  2.5 23.8 %collective-permute-start = (bf16[112,128]{1,0:T(8,128)(2,1)}, bf16[112,128]{1,0:T(8,128)(2,1)S(1)}, u32[]{:S(2)}, u32[]{:S(2)}) collective-permute-start(bf16[112,128]{1,0:T(8,128)(2,1)} %shard_map.163.refs_0_.refs_3_), channel_id=1, source_target_pairs={{0,256},{256,0},{1,257},{257,1},{2,258},{258,2},{3,259},{259,3},{4... | collective-permute-start | bytes 86024 | tf_op jit(solution)/shard_map/ppermute | solution.py:403
  18.8 13.4 %copy-start.18 = (s32[2,1]{0,1:T(1,128)S(1)}, s32[2,1]{0,1:T(1,128)}, u32[]{:S(2)}) copy-start(s32[2,1]{0,1:T(1,128)} %param.23) | copy-start | bytes 28
  20.7 11.7 %copy-start.4 = (bf16[1,128,512]{2,1,0:T(8,128)(2,1)S(1)}, bf16[1,128,512]{2,1,0:T(8,128)(2,1)}, u32[]{:S(2)}) copy-start(bf16[1,128,512]{2,1,0:T(8,128)(2,1)} %refs_6_.3) | copy-start | bytes 393220
  20.7 11.6 %collective-permute-start.2 = (bf16[128,2048]{1,0:T(8,128)(2,1)}, bf16[128,2048]{1,0:T(8,128)(2,1)S(1)}, u32[]{:S(2)}, u32[]{:S(2)}) collective-permute-start(bf16[128,2048]{1,0:T(8,128)(2,1)} %shard_map.165), channel_id=1, source_target_pairs={{1,2},{3,4},{5,6},{7,8},{9,10},{11,12},{13,14},{15,16},{17,18},{19... | collective-permute-start | bytes 1572872 | tf_op jit(solution)/shard_map/ppermute | solution.py:368
  24.3 8.0 %collective-permute-start.1 = (bf16[128,2048]{1,0:T(8,128)(2,1)}, bf16[128,2048]{1,0:T(8,128)(2,1)S(1)}, u32[]{:S(2)}, u32[]{:S(2)}) collective-permute-start(bf16[128,2048]{1,0:T(8,128)(2,1)} %shard_map.165), channel_id=1, source_target_pairs={{0,1},{1,0},{2,3},{3,2},{4,5},{5,4},{6,7},{7,6},{8,9},{9,8},{10,11... | collective-permute-start | bytes 1572872 | tf_op jit(solution)/shard_map/ppermute | solution.py:372
  27.8 16.2 %copy-start.11 = (s32[3,1024]{1,0:T(4,128)S(1)}, s32[3,1024]{1,0:T(4,128)}, u32[]{:S(2)}) copy-start(s32[3,1024]{1,0:T(4,128)} %refs_1_.6) | copy-start | bytes 36868
  27.8 16.2 %copy-start.12 = (f32[3,1024]{1,0:T(4,128)S(1)}, f32[3,1024]{1,0:T(4,128)}, u32[]{:S(2)}) copy-start(f32[3,1024]{1,0:T(4,128)} %refs_2_.6) | copy-start | bytes 36868
  27.8 16.2 %copy-start.13 = (f32[1024]{0:T(1024)S(1)}, f32[1024]{0:T(1024)}, u32[]{:S(2)}) copy-start(f32[1024]{0:T(1024)} %param.19) | copy-start | bytes 12292
  27.9 16.2 %copy-start.14 = (f32[100]{0:T(128)S(1)}, f32[100]{0:T(128)}, u32[]{:S(2)}) copy-start(f32[100]{0:T(128)} %param.20) | copy-start | bytes 1204
  27.9 19.3 %copy-start = (bf16[1,128,1024]{2,1,0:T(8,128)(2,1)S(1)}, bf16[1,128,1024]{2,1,0:T(8,128)(2,1)}, u32[]{:S(2)}) copy-start(bf16[1,128,1024]{2,1,0:T(8,128)(2,1)} %refs_8_.1) | copy-start | bytes 786436
  27.9 19.3 %copy-start.6 = (f32[100,1024]{1,0:T(8,128)S(1)}, f32[100,1024]{1,0:T(8,128)}, u32[]{:S(2)}) copy-start(f32[100,1024]{1,0:T(8,128)} %refs_6_.2) | copy-start | bytes 1228804
  27.9 9.7 %all-to-all-start = ((bf16[4,224,128]{2,1,0:T(8,128)(2,1)}), bf16[4,224,128]{2,1,0:T(8,128)(2,1)S(1)}, u32[]{:S(2)}, u32[]{:S(2)}) async-start(bf16[4,224,128]{2,1,0:T(8,128)(2,1)} %shard_map.164), calls=%async_computation | async-start | bytes 458752 | tf_op jit(solution)/shard_map/all_to_all | solution.py:376
  32.3 19.3 %copy-start.1 = (bf16[128,2048]{1,0:T(8,128)(2,1)}, bf16[128,2048]{1,0:T(8,128)(2,1)S(1)}, u32[]{:S(2)}) copy-start(bf16[128,2048]{1,0:T(8,128)(2,1)S(1)} %collective-permute-done.2.refs_6_.refs_10_.refs_8_) | copy-start | bytes 1572868
  32.3 19.3 %copy-start.2 = (bf16[128,2048]{1,0:T(8,128)(2,1)}, bf16[128,2048]{1,0:T(8,128)(2,1)S(1)}, u32[]{:S(2)}) copy-start(bf16[128,2048]{1,0:T(8,128)(2,1)S(1)} %collective-permute-done.1.refs_5_.refs_9_) | copy-start | bytes 1572868
  37.6 9.5 %collective-permute-start.4 = (bf16[1408,128]{1,0:T(8,128)(2,1)S(1)}, bf16[1408,128]{1,0:T(8,128)(2,1)S(1)}, u32[]{:S(2)}, u32[]{:S(2)}) collective-permute-start(bf16[1408,128]{1,0:T(8,128)(2,1)S(1)} %pad_maximum_fusion), channel_id=1, source_target_pairs={{1,2},{3,4},{5,6},{7,8},{9,10},{11,12},{13,14},{15,16},{17,18},{19... | collective-permute-start | bytes 1081352 | tf_op jit(solution)/shard_map/ppermute | solution.py:368
  42.1 5.1 %collective-permute-start.3 = (bf16[1408,128]{1,0:T(8,128)(2,1)S(1)}, bf16[1408,128]{1,0:T(8,128)(2,1)S(1)}, u32[]{:S(2)}, u32[]{:S(2)}) collective-permute-start(bf16[1408,128]{1,0:T(8,128)(2,1)S(1)} %pad_maximum_fusion), channel_id=1, source_target_pairs={{0,1},{1,0},{2,3},{3,2},{4,5},{5,4},{6,7},{7,6},{8,9},{9,8},{10,11... | collective-permute-start | bytes 1081352 | tf_op jit(solution)/shard_map/ppermute | solution.py:372
  52.2 32.2 %all-to-all-start.1 = ((bf16[32,48,128]{2,1,0:T(8,128)(2,1)}), bf16[32,48,128]{2,1,0:T(8,128)(2,1)S(1)}, u32[]{:S(2)}, u32[]{:S(2)}) async-start(bf16[32,48,128]{2,1,0:T(8,128)(2,1)} %get-tuple-element.31), calls=%async_computation.1 | async-start | bytes 786432 | tf_op jit(solution)/shard_map/all_to_all | solution.py:376
  74.3 17.2 %collective-permute-start.5 = (f32[128,128]{1,0:T(8,128)S(1)}, f32[128,128]{1,0:T(8,128)S(1)}, u32[]{:S(2)}, u32[]{:S(2)}) collective-permute-start(f32[128,128]{1,0:T(8,128)S(1)} %get-tuple-element.28), channel_id=1, source_target_pairs={{1,2},{3,4},{5,6},{7,8},{9,10},{11,12},{13,14},{15,16},{17,18},{19... | collective-permute-start | bytes 196616 | tf_op jit(solution)/shard_map/ppermute | solution.py:368
  76.2 15.3 %collective-permute-start.6 = (f32[128,128]{1,0:T(8,128)S(1)}, f32[128,128]{1,0:T(8,128)S(1)}, u32[]{:S(2)}, u32[]{:S(2)}) collective-permute-start(f32[128,128]{1,0:T(8,128)S(1)} %get-tuple-element.29), channel_id=1, source_target_pairs={{0,1},{1,0},{2,3},{3,2},{4,5},{5,4},{6,7},{7,6},{8,9},{9,8},{10,11... | collective-permute-start | bytes 196616 | tf_op jit(solution)/shard_map/ppermute | solution.py:372
  85.2 19.2 %all-to-all-start.2 = ((bf16[16,48,128]{2,1,0:T(8,128)(2,1)}), bf16[16,48,128]{2,1,0:T(8,128)(2,1)S(1)}, u32[]{:S(2)}, u32[]{:S(2)}) async-start(bf16[16,48,128]{2,1,0:T(8,128)(2,1)} %shard_map.169.refs_11_), calls=%async_computation.2 | async-start | bytes 393216 | tf_op jit(solution)/shard_map/all_to_all | solution.py:376
  98.3 18.3 %collective-permute-start.7 = (bf16[128,1024]{1,0:T(8,128)(2,1)}, bf16[128,1024]{1,0:T(8,128)(2,1)S(1)}, u32[]{:S(2)}, u32[]{:S(2)}) collective-permute-start(bf16[128,1024]{1,0:T(8,128)(2,1)} %get-tuple-element.35), channel_id=1, source_target_pairs={{1,2},{3,4},{5,6},{7,8},{9,10},{11,12},{13,14},{15,16},{17,18},{19... | collective-permute-start | bytes 786440 | tf_op jit(solution)/shard_map/ppermute | solution.py:368
  102.4 14.2 %copy-start.15 = (f32[128,1024]{1,0:T(8,128)S(1)}, f32[128,1024]{1,0:T(8,128)}, u32[]{:S(2)}) copy-start(f32[128,1024]{1,0:T(8,128)} %get-tuple-element.34.refs_0_) | copy-start | bytes 1572868
  102.4 14.2 %collective-permute-start.8 = (bf16[128,1024]{1,0:T(8,128)(2,1)}, bf16[128,1024]{1,0:T(8,128)(2,1)S(1)}, u32[]{:S(2)}, u32[]{:S(2)}) collective-permute-start(bf16[128,1024]{1,0:T(8,128)(2,1)} %get-tuple-element.36), channel_id=1, source_target_pairs={{0,1},{1,0},{2,3},{3,2},{4,5},{5,4},{6,7},{7,6},{8,9},{9,8},{10,11... | collective-permute-start | bytes 786440 | tf_op jit(solution)/shard_map/ppermute | solution.py:372
  105.2 21.5 %all-to-all-start.3 = ((bf16[32,48,128]{2,1,0:T(8,128)(2,1)}), bf16[32,48,128]{2,1,0:T(8,128)(2,1)S(1)}, u32[]{:S(2)}, u32[]{:S(2)}) async-start(bf16[32,48,128]{2,1,0:T(8,128)(2,1)} %shard_map.172), calls=%async_computation.3 | async-start | bytes 786432 | tf_op jit(solution)/shard_map/all_to_all | solution.py:376
  (8 other events, 37.3 us)

commit v7 on v6

--- a/solution.py
+++ b/solution.py
@@ -35,6 +35,8 @@
 DEC_ROWS = WIDTH // NEAR_SIZE
 WO_ROWS = ATT // NEAR_SIZE
 ROWS = DEC_ROWS + WO_ROWS
+OWN_ROWS = 2
+SENT = DEC_ROWS + 8
 
 WHOLE = 58 * 2**20
 LONG = 2 * 10**10
@@ -173,6 +175,7 @@
     states_ref,
     mate_states_ref,
     far_states_ref,
+    after_ref,
     terms_ref,
     to_far_ref,
     own_ref,
@@ -205,52 +208,65 @@
     to_far_ref[...] = sums[0:NODES]
     own_ref[...] = sums[NODES : 2 * NODES]
     to_mate_ref[...] = sums[2 * NODES : SPAN]
-    high, low = split(dot(grads, mix, NT))
+    turned = dot(grads, mix, NT).astype(BF16)
     bands = (far_states_ref.ready(), states_ref.ready().at[0], mate_states_ref.ready())
     for block in range(WIDTH // NODES):
         cols = slice(block * NODES, (block + 1) * NODES)
         states = jnp.concatenate([band[:, cols] for band in bands], axis=0)
-        dec = jnp.transpose(dot(high, states, NN) + dot(low, states, NN)).astype(BF16)
+        dec = jnp.transpose(dot(turned, states, NN)).astype(BF16)
         count = NODES // DEC_ROWS
         terms_ref[block * count : (block + 1) * count, 0:DEC_ROWS, :] = dec.reshape(
             count, DEC_ROWS, VARS_LANE
         )
     attn_ref = attn_ref.ready()
+    source = lax.broadcasted_iota(jnp.int32, (PAIR, PAIR), 1)
+    place = ((source & 6) << 4) + ((source & 8) << 1) + ((source & 112) >> 3) + (source & 1)
+    order = (lax.broadcasted_iota(jnp.int32, (PAIR, PAIR), 0) == place).astype(BF16)
     for block in range(ATT // PAIR):
         first = MEMBERS * VARS_SUB + block * NODES
         rows = slice(first, first + NODES)
         attn = jnp.concatenate([far_ref[rows], attn_ref[block], mate_ref[rows]], axis=0)
-        wo = jnp.transpose(dot(high, attn, NN) + dot(low, attn, NN)).astype(BF16)
-        count = NODES // WO_ROWS
-        terms_ref[block * count : (block + 1) * count, DEC_ROWS:ROWS, :] = wo.reshape(
-            count, WO_ROWS, VARS_LANE
-        )
-
-
-def sum_parts(in_ref, out_ref):
+        wo = dot(order, dot(turned, attn, NN).astype(BF16), NT).astype(BF16)
+        for part in range(NODES // WO_ROWS):
+            row, core = part // 2, part % 2
+            terms_ref[(row * 4 + block) * 2 + core, DEC_ROWS:ROWS, :] = wo[
+                part * WO_ROWS : (part + 1) * WO_ROWS
+            ]
+
+
+def total_of(in_ref):
     total = in_ref[0].astype(F32)
     for i in range(1, in_ref.shape[0]):
         total = total + in_ref[i].astype(F32)
-    total = total.astype(BF16)
-    for i in range(out_ref.shape[0]):
+    return total
+
+
+def near_body(in_ref, out_ref):
+    total = total_of(in_ref)
+    dec = total[0:DEC_ROWS].astype(BF16)
+    rest = jnp.zeros((SENT - DEC_ROWS - OWN_ROWS, VARS_LANE), F32)
+    for i in range(FAR_SIZE):
+        first = DEC_ROWS + OWN_ROWS * (i % 8)
+        wo = jnp.concatenate([total[first : first + OWN_ROWS], rest], axis=0)
+        out_ref[i, 0:DEC_ROWS, :] = dec
+        out_ref[i, DEC_ROWS:SENT, :] = wo.astype(BF16)
+
+
+def sum_body(in_ref, out_ref):
+    total = total_of(in_ref).astype(BF16)
+    for i in range(NEAR_SIZE):
         out_ref[i] = total
 
 
-def near_body(in_ref, out_ref):
-    sum_parts(in_ref, out_ref)
-
-
-def sum_body(in_ref, out_ref):
-    sum_parts(in_ref, out_ref)
-
-
-def final_body(band_ref, all_ref, dec_ref, after_ref, wo_ref, grad_dec_ref, dec_s, wo_s):
+def final_body(band_ref, all_ref, dec_ref, after_ref, wo_ref, grad_dec_ref, dec_s):
     dec_s[...] = jnp.zeros(dec_s.shape, BF16)
     dec_s[0:VARS, :] = dec_ref[...]
-    band = band_ref[0]
-    rows = all_ref[lax.div(band, 2), DEC_ROWS:ROWS, :]
-    wo_s[...] = dot(rows, dec_s[...], NN)
-    wo_ref[...] = wo_s[pl.ds(pl.multiple_of(lax.rem(band, 2) * 8, 8), 8), :]
+    column, core = lax.div(band_ref[0], 16), lax.rem(band_ref[0], 2)
+    rows = [
+        all_ref[(row * 4 + column) * 2 + core, DEC_ROWS:SENT, :].astype(F32)[0:OWN_ROWS]
+        for row in range(4)
+    ]
+    wo_ref[...] = dot(jnp.concatenate(rows, axis=0).astype(BF16), dec_s[...], NN)
     dec = all_ref[:, 0:DEC_ROWS, :].astype(F32).reshape(WIDTH, VARS_LANE)
     grad_dec_ref[...] = jnp.transpose(dec)[0:VARS, :]
 
@@ -266,30 +282,52 @@
     return jnp.concatenate([far_ref[:, side], own_ref[0, :, cols], mate_ref[:, side]], axis=0)
 
 
+def probabilities(inside, query_ref, key_ref, mate_ref, far_ref, pair):
+    masks = pair_masks(BF16)
+    query = query_ref[0, :, pair * PAIR : (pair + 1) * PAIR]
+    keys = band_blocks(far_ref, key_ref, mate_ref, pair, 0)
+    probs = []
+    for half in range(2):
+        scores = dot(query * masks[half], keys, NT) * SCALE
+        scores = jnp.where(inside, scores, MASKED_SCORE)
+        exponent = jnp.exp(scores - jnp.max(scores, axis=-1, keepdims=True))
+        probs.append(exponent / jnp.sum(exponent, axis=-1, keepdims=True))
+    return probs
+
+
+def window(band_ref, windows_ref):
+    lanes = lax.broadcasted_iota(jnp.int32, (1, NODES), 1)
+    place = jnp.concatenate([lanes + base for base in bases(band_ref[0])], axis=1)
+    return (place >= windows_ref[0, 0]) & (place < windows_ref[1, 0])
+
+
 def forward_body(
-    band_ref, windows_ref, query_ref, key_ref, value_ref, mate_ref, far_ref, prob_ref, attn_ref
+    band_ref, windows_ref, query_ref, key_ref, value_ref, mate_ref, far_ref, attn_ref
 ):
     query_ref, key_ref, value_ref = query_ref.ready(), key_ref.ready(), value_ref.ready()
     far_ref, mate_ref = far_ref.ready(), mate_ref.ready()
-    lanes = lax.broadcasted_iota(jnp.int32, (1, NODES), 1)
-    place = jnp.concatenate([lanes + base for base in bases(band_ref[0])], axis=1)
-    inside = (place >= windows_ref[0, 0]) & (place < windows_ref[1, 0])
-    masks = pair_masks(BF16)
+    inside = window(band_ref, windows_ref)
     lane = lax.broadcasted_iota(jnp.int32, (1, PAIR), 1)
     for pair in range(HEADS // 2):
-        cols = slice(pair * PAIR, (pair + 1) * PAIR)
-        query = query_ref[0, :, cols]
-        keys = band_blocks(far_ref, key_ref, mate_ref, pair, 0)
         values = band_blocks(far_ref, value_ref, mate_ref, pair, ATT)
-        outs = []
-        for half in range(2):
-            scores = dot(query * masks[half], keys, NT) * SCALE
-            scores = jnp.where(inside, scores, MASKED_SCORE)
-            exponent = jnp.exp(scores - jnp.max(scores, axis=-1, keepdims=True))
-            prob = exponent / jnp.sum(exponent, axis=-1, keepdims=True)
-            prob_ref[2 * pair + half] = prob
-            outs.append(dot(prob.astype(BF16), values, NN))
+        outs = [
+            dot(prob.astype(BF16), values, NN)
+            for prob in probabilities(inside, query_ref, key_ref, mate_ref, far_ref, pair)
+        ]
         attn_ref[pair] = jnp.where(lane < HEAD_DIM, outs[0], outs[1]).astype(BF16)
+
+
+def prob_body(
+    band_ref, windows_ref, query_ref, key_ref, mate_ref, far_ref, after_ref, prob_ref, done_ref
+):
+    done_ref[...] = jnp.zeros(done_ref.shape, F32)
+    query_ref, key_ref = query_ref.ready(), key_ref.ready()
+    far_ref, mate_ref = far_ref.ready(), mate_ref.ready()
+    inside = window(band_ref, windows_ref)
+    for pair in range(HEADS // 2):
+        probs = probabilities(inside, query_ref, key_ref, mate_ref, far_ref, pair)
+        prob_ref[2 * pair] = probs[0]
+        prob_ref[2 * pair + 1] = probs[1]
 
 
 def backward_body(
@@ -418,9 +456,9 @@
         cost=LONG,
     )
     mid = exchange(pairs, "y")
-    prob, attn = call(
+    attn = call(
         forward_body,
-        (shape((HEADS, NODES, SPAN), F32), shape((ATT // PAIR, NODES, PAIR), BF16)),
+        shape((ATT // PAIR, NODES, PAIR), BF16),
         "sslllkk",
         (band, windows, query, key, value, mate_band, far_band),
     )
@@ -432,11 +470,19 @@
     )
     halo = jnp.concatenate([mid.reshape(-1, NODES), attn.reshape(-1, PAIR)], axis=0)
     mate_halo, far_halo = swap_mate(halo), swap_far(halo)
+    flag = shape((8, 128), F32)
+    prob, done = call(
+        prob_body,
+        (shape((HEADS, NODES, SPAN), F32), flag),
+        "ssllkka",
+        (band, windows, query, key, mate_band, far_band, halo),
+        cost=LONG,
+    )
     block = shape((NODES, VARS_LANE), F32)
     terms, to_far, own, to_mate = call(
         crps_body,
         (shape((NEAR_SIZE, ROWS, VARS_LANE), BF16), block, block, block),
-        "svvvvvvlltt",
+        "svvvvvvllttv",
         (
             member,
             mate_halo,
@@ -449,6 +495,7 @@
             node_states,
             mate_band,
             far_band,
+            done,
         ),
         scratch=[
             pltpu.VMEM((MEMBERS, VARS_SUB, POINTS), F32),
@@ -458,11 +505,10 @@
     near = exchange(terms, NEAR)
     mate_sum, far_sum = swap_mate(to_mate), swap_far(to_far)
     near_sums = call(
-        near_body, shape((FAR_SIZE, ROWS, VARS_LANE), BF16), "v", (near,), cost=LONG
+        near_body, shape((FAR_SIZE, SENT, VARS_LANE), BF16), "v", (near,), cost=LONG
     )
     along = exchange(near_sums, FAR)
     wide = (NODES, 2 * ATT)
-    flag = shape((8, 128), F32)
     grad_states, grad_query, kv_far, kv_own, kv_mate = call(
         backward_body,
         (
@@ -493,7 +539,7 @@
     )
     far_sums = call(
         sum_body,
-        shape((NEAR_SIZE, ROWS, VARS_LANE), BF16),
+        shape((NEAR_SIZE, SENT, VARS_LANE), BF16),
         "v",
         (along,),
         cost=LONG,
@@ -512,7 +558,7 @@
         (shape((8, WIDTH), F32), shape((VARS, WIDTH), F32)),
         "svva",
         (band, everything, dec_weight, joined),
-        scratch=[pltpu.VMEM((VARS_LANE, WIDTH), BF16), pltpu.VMEM((WO_ROWS, WIDTH), F32)],
+        scratch=[pltpu.VMEM((VARS_LANE, WIDTH), BF16)],
     )
     return grad_states, grad_query, grad_key, grad_value, grad_wo, grad_dec
 

time: 128 us -> 126 us (0.984)
  starting transfers between devices: 82.1 us -> 80 us
    all_to_all x4, starting transfers between devices: 43.9 us -> 41.8 us  [exchange(): return lax.all_to_all(x, axes, split_axis=0, concat_axis=0, tiled=True)]
    pallas_call x11 -> x12, Pallas kernels: 23 us -> 23.8 us  [call(): pl.pallas_call(kernel, out_shape=out_shape, in_specs=specs, scratch_shape...]
  transfers between devices with their start and end apart: 13 -> 13, of which waited for: 3 -> 4; matrix products, arithmetic and copies ran while one was open for 0% -> 0% of each run, Pallas kernels for 12% -> 13%
where the time goes in v7:
time: 126 us; the launch traced here: 125 us
  starting transfers between devices  80 us (63%)
  Pallas kernels  23.8 us (19%)
  waiting for transfers between devices  18 us (14%)
  local copies, waits for them, and re-layouts  2.16 us (2%)
    all_to_all x4, starting transfers between devices, exchange(): return lax.all_to_all(x, axes, split_axis=0, concat_axis=0, tiled=True)  41.8 us
    pallas_call x12, Pallas kernels, call(): pl.pallas_call(kernel, out_shape=out_shape, in_specs=specs, scratch_shape...  23.8 us
    all_to_all x4, waiting for transfers between devices, exchange(): return lax.all_to_all(x, axes, split_axis=0, concat_axis=0, tiled=True)  16.5 us
    ppermute x1, starting transfers between devices, per_device(): other = lax.ppermute(proj, 'zh', [(0, 1), (1, 0)])  16.3 us
    ppermute x4, starting transfers between devices, swap_far(): lax.ppermute(x, SPACE, pairs + [(target, source) for source, target in pa...  14.2 us
    ppermute x4, starting transfers between devices, swap_mate(): return lax.ppermute(x, 'c', [(0, 1), (1, 0)])  7.81 us
  transfers between devices with their start and end apart: 13, of which 4 were waited for; matrix products, arithmetic and copies ran while one was open for 0% of the time, Pallas kernels for 13%

profile of v7, /device:TPU:1, one launch (start us, length us, event | category | flops | bytes accessed | tf_op | source)
XLA Modules:
  0.0 125.0 jit_solution(16243613014275173249)
XLA Ops:
  0.6 1.9 %shard_map.163.refs_0_.refs_3_ = bf16[112,128]{1,0:T(8,128)(2,1)} custom-call(bf16[1,128,1024]{2,1,0:T(8,128)(2,1)} %refs_8_.1, bf16[100,1024]{1,0:T(8,128)(2,1)} %refs_2_.9), custom_call_target="tpu_custom_call" | custom-call | flops 100000000 | bytes 1000000 | tf_op jit(solution)/shard_map/pallas_call | solution.py:98
  2.5 16.3 %collective-permute-start = (bf16[112,128]{1,0:T(8,128)(2,1)}, bf16[112,128]{1,0:T(8,128)(2,1)S(1)}, u32[]{:S(2)}, u32[]{:S(2)}) collective-permute-start(bf16[112,128]{1,0:T(8,128)(2,1)} %shard_map.163.refs_0_.refs_3_), channel_id=1, source_target_pairs={{0,256},{256,0},{1,257},{257,1},{2,258},{258,2},{3,259},{259,3},{4... | collective-permute-start | bytes 86024 | tf_op jit(solution)/shard_map/ppermute | solution.py:441
  18.9 1.9 %shard_map.165 = bf16[128,2048]{1,0:T(8,128)(2,1)} custom-call(bf16[1,128,1024]{2,1,0:T(8,128)(2,1)} %refs_8_.1, bf16[1,128,512]{2,1,0:T(8,128)(2,1)} %refs_6_.3, bf16[1,128,512]{2,1,0:T(8,128)(2,1)} %refs_7_.1, bf16[112,128]{1,0:T(8,128)(2,1)} %shard_map.163.refs_0_.refs_3_), custom_call_target="tpu_custom_call" | custom-call | flops 100000000 | bytes 1000000 | tf_op jit(solution)/shard_map/pallas_call | solution.py:98
  20.8 3.6 %collective-permute-start.2 = (bf16[128,2048]{1,0:T(8,128)(2,1)}, bf16[128,2048]{1,0:T(8,128)(2,1)S(1)}, u32[]{:S(2)}, u32[]{:S(2)}) collective-permute-start(bf16[128,2048]{1,0:T(8,128)(2,1)} %shard_map.165), channel_id=1, source_target_pairs={{1,2},{3,4},{5,6},{7,8},{9,10},{11,12},{13,14},{15,16},{17,18},{19... | collective-permute-start | bytes 1572872 | tf_op jit(solution)/shard_map/ppermute | solution.py:406
  24.4 1.9 %collective-permute-start.1 = (bf16[128,2048]{1,0:T(8,128)(2,1)}, bf16[128,2048]{1,0:T(8,128)(2,1)S(1)}, u32[]{:S(2)}, u32[]{:S(2)}) collective-permute-start(bf16[128,2048]{1,0:T(8,128)(2,1)} %shard_map.165), channel_id=1, source_target_pairs={{0,1},{1,0},{2,3},{3,2},{4,5},{5,4},{6,7},{7,6},{8,9},{9,8},{10,11... | collective-permute-start | bytes 1572872 | tf_op jit(solution)/shard_map/ppermute | solution.py:410
  27.9 4.2 %all-to-all-start = ((bf16[4,224,128]{2,1,0:T(8,128)(2,1)}), bf16[4,224,128]{2,1,0:T(8,128)(2,1)S(1)}, u32[]{:S(2)}, u32[]{:S(2)}) async-start(bf16[4,224,128]{2,1,0:T(8,128)(2,1)} %shard_map.164), calls=%async_computation | async-start | bytes 458752 | tf_op jit(solution)/shard_map/all_to_all | solution.py:414
  33.0 2.9 %shard_map.166.refs_7_ = bf16[4,128,128]{2,1,0:T(8,128)(2,1)S(1)} custom-call(s32[1]{0:T(128)} %bitcast.2.refs_0_, s32[2,1]{1,0:T(2,128)S(1)} %copy.18.refs_1_, bf16[1,128,512]{2,1,0:T(8,128)(2,1)S(1)} %copy-done.7, bf16[1,128,512]{2,1,0:T(8,128)(2,1)S(1)} %copy-done.4, bf16[1,128,512]{2,1,0:T(8,128)(2,1)S(1)} %copy-done.5, ...), custom_call_target="tpu_custom_call" | custom-call | flops 100000000 | bytes 1000000 | tf_op jit(solution)/shard_map/pallas_call | solution.py:98
  35.9 1.5 %all-to-all-done.refs_2_ = bf16[4,224,128]{2,1,0:T(8,128)(2,1)S(1)} async-done(((bf16[4,224,128]{2,1,0:T(8,128)(2,1)}), bf16[4,224,128]{2,1,0:T(8,128)(2,1)S(1)}, u32[]{:S(2)}, u32[]{:S(2)}) %all-to-all-start) | async-done | bytes 229408 | tf_op jit(solution)/shard_map/all_to_all | solution.py:414
  37.5 4.6 %collective-permute-start.4 = (bf16[1408,128]{1,0:T(8,128)(2,1)S(1)}, bf16[1408,128]{1,0:T(8,128)(2,1)S(1)}, u32[]{:S(2)}, u32[]{:S(2)}) collective-permute-start(bf16[1408,128]{1,0:T(8,128)(2,1)S(1)} %pad_maximum_fusion.refs_6_), channel_id=1, source_target_pairs={{1,2},{3,4},{5,6},{7,8},{9,10},{11,12},{13,14},{15,16},{17,18},{19... | collective-permute-start | bytes 1081352 | tf_op jit(solution)/shard_map/ppermute | solution.py:406
  42.1 1.9 %collective-permute-start.3 = (bf16[1408,128]{1,0:T(8,128)(2,1)S(1)}, bf16[1408,128]{1,0:T(8,128)(2,1)S(1)}, u32[]{:S(2)}, u32[]{:S(2)}) collective-permute-start(bf16[1408,128]{1,0:T(8,128)(2,1)S(1)} %pad_maximum_fusion.refs_6_), channel_id=1, source_target_pairs={{0,1},{1,0},{2,3},{3,2},{4,5},{5,4},{6,7},{7,6},{8,9},{9,8},{10,11... | collective-permute-start | bytes 1081352 | tf_op jit(solution)/shard_map/ppermute | solution.py:410
  44.0 1.7 %shard_map.168 = (f32[8,128,384]{2,1,0:T(8,128)S(1)}, f32[8,128]{1,0:T(8,128)S(1)}) custom-call(s32[1]{0:T(128)} %bitcast.2.refs_0_, s32[2,1]{1,0:T(2,128)S(1)} %copy.18.refs_1_, bf16[1,128,512]{2,1,0:T(8,128)(2,1)S(1)} %copy-done.7, bf16[1,128,512]{2,1,0:T(8,128)(2,1)S(1)} %copy-done.4, ...), custom_call_target="tpu_custom_call" | custom-call | flops 20000000000 | bytes 1000000 | tf_op jit(solution)/shard_map/pallas_call | solution.py:98
  45.7 1.5 %collective-permute-done.4.refs_3_ = bf16[1408,128]{1,0:T(8,128)(2,1)S(1)} collective-permute-done((bf16[1408,128]{1,0:T(8,128)(2,1)S(1)}, bf16[1408,128]{1,0:T(8,128)(2,1)S(1)}, u32[]{:S(2)}, u32[]{:S(2)}) %collective-permute-start.4) | collective-permute-done | bytes 360480 | tf_op jit(solution)/shard_map/ppermute | solution.py:406
  47.2 4.6 %shard_map.169 = (bf16[32,48,128]{2,1,0:T(8,128)(2,1)}, f32[128,128]{1,0:T(8,128)S(1)}, f32[128,128]{1,0:T(8,128)S(1)}, f32[128,128]{1,0:T(8,128)S(1)}) custom-call(s32[1]{0:T(128)} %bitcast.refs_0_, bf16[1408,128]{1,0:T(8,128)(2,1)S(1)} %collective-permute-done.3.refs_1_, bf16[4,224,128]{2,1,0:T(8,128)(2,1)S(1)} %all-to-all-done.refs_2_, ...), custom_call_target="tpu_custom_call" | custom-call | flops 100000000 | bytes 1000000 | tf_op jit(solution)/shard_map/pallas_call | solution.py:98
  52.4 20.0 %all-to-all-start.1 = ((bf16[32,48,128]{2,1,0:T(8,128)(2,1)}), bf16[32,48,128]{2,1,0:T(8,128)(2,1)S(1)}, u32[]{:S(2)}, u32[]{:S(2)}) async-start(bf16[32,48,128]{2,1,0:T(8,128)(2,1)} %get-tuple-element.31), calls=%async_computation.1 | async-start | bytes 786432 | tf_op jit(solution)/shard_map/all_to_all | solution.py:414
  72.4 1.9 %collective-permute-start.5 = (f32[128,128]{1,0:T(8,128)S(1)}, f32[128,128]{1,0:T(8,128)S(1)}, u32[]{:S(2)}, u32[]{:S(2)}) collective-permute-start(f32[128,128]{1,0:T(8,128)S(1)} %get-tuple-element.28), channel_id=1, source_target_pairs={{1,2},{3,4},{5,6},{7,8},{9,10},{11,12},{13,14},{15,16},{17,18},{19... | collective-permute-start | bytes 196616 | tf_op jit(solution)/shard_map/ppermute | solution.py:406
  74.3 1.9 %collective-permute-start.6 = (f32[128,128]{1,0:T(8,128)S(1)}, f32[128,128]{1,0:T(8,128)S(1)}, u32[]{:S(2)}, u32[]{:S(2)}) collective-permute-start(f32[128,128]{1,0:T(8,128)S(1)} %get-tuple-element.29), channel_id=1, source_target_pairs={{0,1},{1,0},{2,3},{3,2},{4,5},{5,4},{6,7},{7,6},{8,9},{9,8},{10,11... | collective-permute-start | bytes 196616 | tf_op jit(solution)/shard_map/ppermute | solution.py:410
  76.3 6.3 %all-to-all-done.1.refs_0_ = bf16[32,48,128]{2,1,0:T(8,128)(2,1)S(1)} async-done(((bf16[32,48,128]{2,1,0:T(8,128)(2,1)}), bf16[32,48,128]{2,1,0:T(8,128)(2,1)S(1)}, u32[]{:S(2)}, u32[]{:S(2)}) %all-to-all-start.1) | async-done | bytes 393248 | tf_op jit(solution)/shard_map/all_to_all | solution.py:414
  83.3 6.4 %all-to-all-start.2 = ((bf16[16,40,128]{2,1,0:T(8,128)(2,1)}), bf16[16,40,128]{2,1,0:T(8,128)(2,1)S(1)}, u32[]{:S(2)}, u32[]{:S(2)}) async-start(bf16[16,40,128]{2,1,0:T(8,128)(2,1)} %shard_map.170.refs_11_), calls=%async_computation.2 | async-start | bytes 327680 | tf_op jit(solution)/shard_map/all_to_all | solution.py:414
  90.3 6.1 %shard_map.171 = (bf16[1,128,1024]{2,1,0:T(8,128)(2,1)}, bf16[1,128,512]{2,1,0:T(8,128)(2,1)}, bf16[128,1024]{1,0:T(8,128)(2,1)}, f32[128,1024]{1,0:T(8,128)}, bf16[128,1024]{1,0:T(8,128)(2,1)}) custom-call(f32[128,128]{1,0:T(8,128)} %copy-done.9, f32[128,128]{1,0:T(8,128)} %copy-done.16, f32[128,128]{1,0:T(8,128)} %copy-done.17, bf16[100,1024]{1,0:T(8,128)(2,1)} %refs_2_.9, ...), custom_call_target="tpu_custom_call" | custom-call | flops 20000000000 | bytes 1000000 | tf_op jit(solution)/shard_map/pallas_call | solution.py:98
  96.4 4.1 %collective-permute-start.7 = (bf16[128,1024]{1,0:T(8,128)(2,1)}, bf16[128,1024]{1,0:T(8,128)(2,1)S(1)}, u32[]{:S(2)}, u32[]{:S(2)}) collective-permute-start(bf16[128,1024]{1,0:T(8,128)(2,1)} %get-tuple-element.35), channel_id=1, source_target_pairs={{1,2},{3,4},{5,6},{7,8},{9,10},{11,12},{13,14},{15,16},{17,18},{19... | collective-permute-start | bytes 786440 | tf_op jit(solution)/shard_map/ppermute | solution.py:406
  100.5 2.1 %collective-permute-start.8 = (bf16[128,1024]{1,0:T(8,128)(2,1)}, bf16[128,1024]{1,0:T(8,128)(2,1)S(1)}, u32[]{:S(2)}, u32[]{:S(2)}) collective-permute-start(bf16[128,1024]{1,0:T(8,128)(2,1)} %get-tuple-element.36), channel_id=1, source_target_pairs={{0,1},{1,0},{2,3},{3,2},{4,5},{5,4},{6,7},{7,6},{8,9},{9,8},{10,11... | collective-permute-start | bytes 786440 | tf_op jit(solution)/shard_map/ppermute | solution.py:410
  103.4 11.2 %all-to-all-start.3 = ((bf16[32,40,128]{2,1,0:T(8,128)(2,1)}), bf16[32,40,128]{2,1,0:T(8,128)(2,1)S(1)}, u32[]{:S(2)}, u32[]{:S(2)}) async-start(bf16[32,40,128]{2,1,0:T(8,128)(2,1)} %shard_map.173), calls=%async_computation.3 | async-start | bytes 655360 | tf_op jit(solution)/shard_map/all_to_all | solution.py:414
  115.5 8.6 %all-to-all-done.3.refs_1_ = bf16[32,40,128]{2,1,0:T(8,128)(2,1)S(1)} async-done(((bf16[32,40,128]{2,1,0:T(8,128)(2,1)}), bf16[32,40,128]{2,1,0:T(8,128)(2,1)S(1)}, u32[]{:S(2)}, u32[]{:S(2)}) %all-to-all-start.3) | async-done | bytes 327712 | tf_op jit(solution)/shard_map/all_to_all | solution.py:414
  124.1 0.9 shard_map.174
  (54 shorter events, 6.1 us)
Async XLA Ops:
  2.5 23.8 %collective-permute-start = (bf16[112,128]{1,0:T(8,128)(2,1)}, bf16[112,128]{1,0:T(8,128)(2,1)S(1)}, u32[]{:S(2)}, u32[]{:S(2)}) collective-permute-start(bf16[112,128]{1,0:T(8,128)(2,1)} %shard_map.163.refs_0_.refs_3_), channel_id=1, source_target_pairs={{0,256},{256,0},{1,257},{257,1},{2,258},{258,2},{3,259},{259,3},{4... | collective-permute-start | bytes 86024 | tf_op jit(solution)/shard_map/ppermute | solution.py:441
  18.8 13.3 %copy-start.18 = (s32[2,1]{0,1:T(1,128)S(1)}, s32[2,1]{0,1:T(1,128)}, u32[]{:S(2)}) copy-start(s32[2,1]{0,1:T(1,128)} %param.23) | copy-start | bytes 28
  18.8 13.4 %copy-start.10 = (s32[3,1024]{1,0:T(4,128)S(1)}, s32[3,1024]{1,0:T(4,128)}, u32[]{:S(2)}) copy-start(s32[3,1024]{1,0:T(4,128)} %refs_1_.7) | copy-start | bytes 36868
  18.8 13.4 %copy-start.11 = (f32[3,1024]{1,0:T(4,128)S(1)}, f32[3,1024]{1,0:T(4,128)}, u32[]{:S(2)}) copy-start(f32[3,1024]{1,0:T(4,128)} %refs_2_.7) | copy-start | bytes 36868
  18.8 13.3 %copy-start.12 = (f32[1024]{0:T(1024)S(1)}, f32[1024]{0:T(1024)}, u32[]{:S(2)}) copy-start(f32[1024]{0:T(1024)} %param.19) | copy-start | bytes 12292
  18.9 13.3 %copy-start.13 = (f32[100]{0:T(128)S(1)}, f32[100]{0:T(128)}, u32[]{:S(2)}) copy-start(f32[100]{0:T(128)} %param.20) | copy-start | bytes 1204
  20.7 12.2 %copy-start.4 = (bf16[1,128,512]{2,1,0:T(8,128)(2,1)S(1)}, bf16[1,128,512]{2,1,0:T(8,128)(2,1)}, u32[]{:S(2)}) copy-start(bf16[1,128,512]{2,1,0:T(8,128)(2,1)} %refs_6_.3) | copy-start | bytes 393220
  20.8 12.2 %copy-start.5 = (bf16[1,128,512]{2,1,0:T(8,128)(2,1)S(1)}, bf16[1,128,512]{2,1,0:T(8,128)(2,1)}, u32[]{:S(2)}) copy-start(bf16[1,128,512]{2,1,0:T(8,128)(2,1)} %refs_7_.1) | copy-start | bytes 393220
  20.8 12.2 %copy-start.7 = (bf16[1,128,512]{2,1,0:T(8,128)(2,1)S(1)}, bf16[1,128,512]{2,1,0:T(8,128)(2,1)}, u32[]{:S(2)}) copy-start(bf16[1,128,512]{2,1,0:T(8,128)(2,1)} %refs_5_.1) | copy-start | bytes 393220
  20.8 12.2 %collective-permute-start.2 = (bf16[128,2048]{1,0:T(8,128)(2,1)}, bf16[128,2048]{1,0:T(8,128)(2,1)S(1)}, u32[]{:S(2)}, u32[]{:S(2)}) collective-permute-start(bf16[128,2048]{1,0:T(8,128)(2,1)} %shard_map.165), channel_id=1, source_target_pairs={{1,2},{3,4},{5,6},{7,8},{9,10},{11,12},{13,14},{15,16},{17,18},{19... | collective-permute-start | bytes 1572872 | tf_op jit(solution)/shard_map/ppermute | solution.py:406
  24.4 8.6 %collective-permute-start.1 = (bf16[128,2048]{1,0:T(8,128)(2,1)}, bf16[128,2048]{1,0:T(8,128)(2,1)S(1)}, u32[]{:S(2)}, u32[]{:S(2)}) collective-permute-start(bf16[128,2048]{1,0:T(8,128)(2,1)} %shard_map.165), channel_id=1, source_target_pairs={{0,1},{1,0},{2,3},{3,2},{4,5},{5,4},{6,7},{7,6},{8,9},{9,8},{10,11... | collective-permute-start | bytes 1572872 | tf_op jit(solution)/shard_map/ppermute | solution.py:410
  27.9 9.6 %all-to-all-start = ((bf16[4,224,128]{2,1,0:T(8,128)(2,1)}), bf16[4,224,128]{2,1,0:T(8,128)(2,1)S(1)}, u32[]{:S(2)}, u32[]{:S(2)}) async-start(bf16[4,224,128]{2,1,0:T(8,128)(2,1)} %shard_map.164), calls=%async_computation | async-start | bytes 458752 | tf_op jit(solution)/shard_map/all_to_all | solution.py:414
  32.9 14.2 %copy-start.1 = (bf16[128,2048]{1,0:T(8,128)(2,1)}, bf16[128,2048]{1,0:T(8,128)(2,1)S(1)}, u32[]{:S(2)}) copy-start(bf16[128,2048]{1,0:T(8,128)(2,1)S(1)} %collective-permute-done.2.refs_6_.refs_5_.refs_10_.refs_8_) | copy-start | bytes 1572868
  33.0 14.2 %copy-start.2 = (bf16[128,2048]{1,0:T(8,128)(2,1)}, bf16[128,2048]{1,0:T(8,128)(2,1)S(1)}, u32[]{:S(2)}) copy-start(bf16[128,2048]{1,0:T(8,128)(2,1)S(1)} %collective-permute-done.1.refs_5_.refs_4_.refs_9_) | copy-start | bytes 1572868
  37.5 9.7 %collective-permute-start.4 = (bf16[1408,128]{1,0:T(8,128)(2,1)S(1)}, bf16[1408,128]{1,0:T(8,128)(2,1)S(1)}, u32[]{:S(2)}, u32[]{:S(2)}) collective-permute-start(bf16[1408,128]{1,0:T(8,128)(2,1)S(1)} %pad_maximum_fusion.refs_6_), channel_id=1, source_target_pairs={{1,2},{3,4},{5,6},{7,8},{9,10},{11,12},{13,14},{15,16},{17,18},{19... | collective-permute-start | bytes 1081352 | tf_op jit(solution)/shard_map/ppermute | solution.py:406
  42.1 5.1 %collective-permute-start.3 = (bf16[1408,128]{1,0:T(8,128)(2,1)S(1)}, bf16[1408,128]{1,0:T(8,128)(2,1)S(1)}, u32[]{:S(2)}, u32[]{:S(2)}) collective-permute-start(bf16[1408,128]{1,0:T(8,128)(2,1)S(1)} %pad_maximum_fusion.refs_6_), channel_id=1, source_target_pairs={{0,1},{1,0},{2,3},{3,2},{4,5},{5,4},{6,7},{7,6},{8,9},{9,8},{10,11... | collective-permute-start | bytes 1081352 | tf_op jit(solution)/shard_map/ppermute | solution.py:410
  52.4 30.1 %all-to-all-start.1 = ((bf16[32,48,128]{2,1,0:T(8,128)(2,1)}), bf16[32,48,128]{2,1,0:T(8,128)(2,1)S(1)}, u32[]{:S(2)}, u32[]{:S(2)}) async-start(bf16[32,48,128]{2,1,0:T(8,128)(2,1)} %get-tuple-element.31), calls=%async_computation.1 | async-start | bytes 786432 | tf_op jit(solution)/shard_map/all_to_all | solution.py:414
  72.4 17.3 %collective-permute-start.5 = (f32[128,128]{1,0:T(8,128)S(1)}, f32[128,128]{1,0:T(8,128)S(1)}, u32[]{:S(2)}, u32[]{:S(2)}) collective-permute-start(f32[128,128]{1,0:T(8,128)S(1)} %get-tuple-element.28), channel_id=1, source_target_pairs={{1,2},{3,4},{5,6},{7,8},{9,10},{11,12},{13,14},{15,16},{17,18},{19... | collective-permute-start | bytes 196616 | tf_op jit(solution)/shard_map/ppermute | solution.py:406
  74.3 15.4 %collective-permute-start.6 = (f32[128,128]{1,0:T(8,128)S(1)}, f32[128,128]{1,0:T(8,128)S(1)}, u32[]{:S(2)}, u32[]{:S(2)}) collective-permute-start(f32[128,128]{1,0:T(8,128)S(1)} %get-tuple-element.29), channel_id=1, source_target_pairs={{0,1},{1,0},{2,3},{3,2},{4,5},{5,4},{6,7},{7,6},{8,9},{9,8},{10,11... | collective-permute-start | bytes 196616 | tf_op jit(solution)/shard_map/ppermute | solution.py:410
  83.3 19.3 %all-to-all-start.2 = ((bf16[16,40,128]{2,1,0:T(8,128)(2,1)}), bf16[16,40,128]{2,1,0:T(8,128)(2,1)S(1)}, u32[]{:S(2)}, u32[]{:S(2)}) async-start(bf16[16,40,128]{2,1,0:T(8,128)(2,1)} %shard_map.170.refs_11_), calls=%async_computation.2 | async-start | bytes 327680 | tf_op jit(solution)/shard_map/all_to_all | solution.py:414
  96.4 18.2 %collective-permute-start.7 = (bf16[128,1024]{1,0:T(8,128)(2,1)}, bf16[128,1024]{1,0:T(8,128)(2,1)S(1)}, u32[]{:S(2)}, u32[]{:S(2)}) collective-permute-start(bf16[128,1024]{1,0:T(8,128)(2,1)} %get-tuple-element.35), channel_id=1, source_target_pairs={{1,2},{3,4},{5,6},{7,8},{9,10},{11,12},{13,14},{15,16},{17,18},{19... | collective-permute-start | bytes 786440 | tf_op jit(solution)/shard_map/ppermute | solution.py:406
  100.5 14.1 %copy-start.15 = (f32[128,1024]{1,0:T(8,128)S(1)}, f32[128,1024]{1,0:T(8,128)}, u32[]{:S(2)}) copy-start(f32[128,1024]{1,0:T(8,128)} %get-tuple-element.34.refs_0_) | copy-start | bytes 1572868
  100.5 14.1 %collective-permute-start.8 = (bf16[128,1024]{1,0:T(8,128)(2,1)}, bf16[128,1024]{1,0:T(8,128)(2,1)S(1)}, u32[]{:S(2)}, u32[]{:S(2)}) collective-permute-start(bf16[128,1024]{1,0:T(8,128)(2,1)} %get-tuple-element.36), channel_id=1, source_target_pairs={{0,1},{1,0},{2,3},{3,2},{4,5},{5,4},{6,7},{7,6},{8,9},{9,8},{10,11... | collective-permute-start | bytes 786440 | tf_op jit(solution)/shard_map/ppermute | solution.py:410
  103.4 20.8 %all-to-all-start.3 = ((bf16[32,40,128]{2,1,0:T(8,128)(2,1)}), bf16[32,40,128]{2,1,0:T(8,128)(2,1)S(1)}, u32[]{:S(2)}, u32[]{:S(2)}) async-start(bf16[32,40,128]{2,1,0:T(8,128)(2,1)} %shard_map.173), calls=%async_computation.3 | async-start | bytes 655360 | tf_op jit(solution)/shard_map/all_to_all | solution.py:414
  (8 other events, 37.6 us)

commit v8 on v7

--- a/solution.py
+++ b/solution.py
@@ -243,13 +243,12 @@
 
 def near_body(in_ref, out_ref):
     total = total_of(in_ref)
-    dec = total[0:DEC_ROWS].astype(BF16)
+    dec = total[0:DEC_ROWS]
     rest = jnp.zeros((SENT - DEC_ROWS - OWN_ROWS, VARS_LANE), F32)
     for i in range(FAR_SIZE):
         first = DEC_ROWS + OWN_ROWS * (i % 8)
-        wo = jnp.concatenate([total[first : first + OWN_ROWS], rest], axis=0)
-        out_ref[i, 0:DEC_ROWS, :] = dec
-        out_ref[i, DEC_ROWS:SENT, :] = wo.astype(BF16)
+        sent = jnp.concatenate([dec, total[first : first + OWN_ROWS], rest], axis=0)
+        out_ref[i] = sent.astype(BF16)
 
 
 def sum_body(in_ref, out_ref):
@@ -263,7 +262,7 @@
     dec_s[0:VARS, :] = dec_ref[...]
     column, core = lax.div(band_ref[0], 16), lax.rem(band_ref[0], 2)
     rows = [
-        all_ref[(row * 4 + column) * 2 + core, DEC_ROWS:SENT, :].astype(F32)[0:OWN_ROWS]
+        all_ref[(row * 4 + column) * 2 + core].astype(F32)[DEC_ROWS : DEC_ROWS + OWN_ROWS]
         for row in range(4)
     ]
     wo_ref[...] = dot(jnp.concatenate(rows, axis=0).astype(BF16), dec_s[...], NN)

time: 126 us -> 126 us (level)
  no operation moved by 1% of the time
where the time goes in v8:
time: 126 us; the launch traced here: 125 us
  starting transfers between devices  80 us (63%)
  Pallas kernels  23.8 us (19%)
  waiting for transfers between devices  18 us (14%)
  local copies, waits for them, and re-layouts  2.16 us (2%)
    all_to_all x4, starting transfers between devices, exchange(): return lax.all_to_all(x, axes, split_axis=0, concat_axis=0, tiled=True)  41.8 us
    pallas_call x12, Pallas kernels, call(): pl.pallas_call(kernel, out_shape=out_shape, in_specs=specs, scratch_shape...  23.8 us
    all_to_all x4, waiting for transfers between devices, exchange(): return lax.all_to_all(x, axes, split_axis=0, concat_axis=0, tiled=True)  16.5 us
    ppermute x1, starting transfers between devices, per_device(): other = lax.ppermute(proj, 'zh', [(0, 1), (1, 0)])  16.3 us
    ppermute x4, starting transfers between devices, swap_far(): lax.ppermute(x, SPACE, pairs + [(target, source) for source, target in pa...  14.2 us
    ppermute x4, starting transfers between devices, swap_mate(): return lax.ppermute(x, 'c', [(0, 1), (1, 0)])  7.81 us
  transfers between devices with their start and end apart: 13, of which 4 were waited for; matrix products, arithmetic and copies ran while one was open for 0% of the time, Pallas kernels for 13%

profile of v8, /device:TPU:1, one launch (start us, length us, event | category | flops | bytes accessed | tf_op | source)
XLA Modules:
  0.0 125.0 jit_solution(16243613014275173249)
XLA Ops:
  0.6 1.9 %shard_map.163.refs_0_.refs_3_ = bf16[112,128]{1,0:T(8,128)(2,1)} custom-call(bf16[1,128,1024]{2,1,0:T(8,128)(2,1)} %refs_8_.1, bf16[100,1024]{1,0:T(8,128)(2,1)} %refs_2_.9), custom_call_target="tpu_custom_call" | custom-call | flops 100000000 | bytes 1000000 | tf_op jit(solution)/shard_map/pallas_call | solution.py:98
  2.5 16.3 %collective-permute-start = (bf16[112,128]{1,0:T(8,128)(2,1)}, bf16[112,128]{1,0:T(8,128)(2,1)S(1)}, u32[]{:S(2)}, u32[]{:S(2)}) collective-permute-start(bf16[112,128]{1,0:T(8,128)(2,1)} %shard_map.163.refs_0_.refs_3_), channel_id=1, source_target_pairs={{0,256},{256,0},{1,257},{257,1},{2,258},{258,2},{3,259},{259,3},{4... | collective-permute-start | bytes 86024 | tf_op jit(solution)/shard_map/ppermute | solution.py:440
  18.9 1.9 %shard_map.165 = bf16[128,2048]{1,0:T(8,128)(2,1)} custom-call(bf16[1,128,1024]{2,1,0:T(8,128)(2,1)} %refs_8_.1, bf16[1,128,512]{2,1,0:T(8,128)(2,1)} %refs_6_.3, bf16[1,128,512]{2,1,0:T(8,128)(2,1)} %refs_7_.1, bf16[112,128]{1,0:T(8,128)(2,1)} %shard_map.163.refs_0_.refs_3_), custom_call_target="tpu_custom_call" | custom-call | flops 100000000 | bytes 1000000 | tf_op jit(solution)/shard_map/pallas_call | solution.py:98
  20.8 3.6 %collective-permute-start.2 = (bf16[128,2048]{1,0:T(8,128)(2,1)}, bf16[128,2048]{1,0:T(8,128)(2,1)S(1)}, u32[]{:S(2)}, u32[]{:S(2)}) collective-permute-start(bf16[128,2048]{1,0:T(8,128)(2,1)} %shard_map.165), channel_id=1, source_target_pairs={{1,2},{3,4},{5,6},{7,8},{9,10},{11,12},{13,14},{15,16},{17,18},{19... | collective-permute-start | bytes 1572872 | tf_op jit(solution)/shard_map/ppermute | solution.py:405
  24.4 1.9 %collective-permute-start.1 = (bf16[128,2048]{1,0:T(8,128)(2,1)}, bf16[128,2048]{1,0:T(8,128)(2,1)S(1)}, u32[]{:S(2)}, u32[]{:S(2)}) collective-permute-start(bf16[128,2048]{1,0:T(8,128)(2,1)} %shard_map.165), channel_id=1, source_target_pairs={{0,1},{1,0},{2,3},{3,2},{4,5},{5,4},{6,7},{7,6},{8,9},{9,8},{10,11... | collective-permute-start | bytes 1572872 | tf_op jit(solution)/shard_map/ppermute | solution.py:409
  27.9 4.2 %all-to-all-start = ((bf16[4,224,128]{2,1,0:T(8,128)(2,1)}), bf16[4,224,128]{2,1,0:T(8,128)(2,1)S(1)}, u32[]{:S(2)}, u32[]{:S(2)}) async-start(bf16[4,224,128]{2,1,0:T(8,128)(2,1)} %shard_map.164), calls=%async_computation | async-start | bytes 458752 | tf_op jit(solution)/shard_map/all_to_all | solution.py:413
  33.0 2.9 %shard_map.166.refs_7_ = bf16[4,128,128]{2,1,0:T(8,128)(2,1)S(1)} custom-call(s32[1]{0:T(128)} %bitcast.2.refs_0_, s32[2,1]{1,0:T(2,128)S(1)} %copy.18.refs_1_, bf16[1,128,512]{2,1,0:T(8,128)(2,1)S(1)} %copy-done.7, bf16[1,128,512]{2,1,0:T(8,128)(2,1)S(1)} %copy-done.4, bf16[1,128,512]{2,1,0:T(8,128)(2,1)S(1)} %copy-done.5, ...), custom_call_target="tpu_custom_call" | custom-call | flops 100000000 | bytes 1000000 | tf_op jit(solution)/shard_map/pallas_call | solution.py:98
  35.9 1.5 %all-to-all-done.refs_2_ = bf16[4,224,128]{2,1,0:T(8,128)(2,1)S(1)} async-done(((bf16[4,224,128]{2,1,0:T(8,128)(2,1)}), bf16[4,224,128]{2,1,0:T(8,128)(2,1)S(1)}, u32[]{:S(2)}, u32[]{:S(2)}) %all-to-all-start) | async-done | bytes 229408 | tf_op jit(solution)/shard_map/all_to_all | solution.py:413
  37.5 4.6 %collective-permute-start.4 = (bf16[1408,128]{1,0:T(8,128)(2,1)S(1)}, bf16[1408,128]{1,0:T(8,128)(2,1)S(1)}, u32[]{:S(2)}, u32[]{:S(2)}) collective-permute-start(bf16[1408,128]{1,0:T(8,128)(2,1)S(1)} %pad_maximum_fusion.refs_6_), channel_id=1, source_target_pairs={{1,2},{3,4},{5,6},{7,8},{9,10},{11,12},{13,14},{15,16},{17,18},{19... | collective-permute-start | bytes 1081352 | tf_op jit(solution)/shard_map/ppermute | solution.py:405
  42.1 1.9 %collective-permute-start.3 = (bf16[1408,128]{1,0:T(8,128)(2,1)S(1)}, bf16[1408,128]{1,0:T(8,128)(2,1)S(1)}, u32[]{:S(2)}, u32[]{:S(2)}) collective-permute-start(bf16[1408,128]{1,0:T(8,128)(2,1)S(1)} %pad_maximum_fusion.refs_6_), channel_id=1, source_target_pairs={{0,1},{1,0},{2,3},{3,2},{4,5},{5,4},{6,7},{7,6},{8,9},{9,8},{10,11... | collective-permute-start | bytes 1081352 | tf_op jit(solution)/shard_map/ppermute | solution.py:409
  44.0 1.7 %shard_map.168 = (f32[8,128,384]{2,1,0:T(8,128)S(1)}, f32[8,128]{1,0:T(8,128)S(1)}) custom-call(s32[1]{0:T(128)} %bitcast.2.refs_0_, s32[2,1]{1,0:T(2,128)S(1)} %copy.18.refs_1_, bf16[1,128,512]{2,1,0:T(8,128)(2,1)S(1)} %copy-done.7, bf16[1,128,512]{2,1,0:T(8,128)(2,1)S(1)} %copy-done.4, ...), custom_call_target="tpu_custom_call" | custom-call | flops 20000000000 | bytes 1000000 | tf_op jit(solution)/shard_map/pallas_call | solution.py:98
  45.7 1.5 %collective-permute-done.4.refs_3_ = bf16[1408,128]{1,0:T(8,128)(2,1)S(1)} collective-permute-done((bf16[1408,128]{1,0:T(8,128)(2,1)S(1)}, bf16[1408,128]{1,0:T(8,128)(2,1)S(1)}, u32[]{:S(2)}, u32[]{:S(2)}) %collective-permute-start.4) | collective-permute-done | bytes 360480 | tf_op jit(solution)/shard_map/ppermute | solution.py:405
  47.2 4.6 %shard_map.169 = (bf16[32,48,128]{2,1,0:T(8,128)(2,1)}, f32[128,128]{1,0:T(8,128)S(1)}, f32[128,128]{1,0:T(8,128)S(1)}, f32[128,128]{1,0:T(8,128)S(1)}) custom-call(s32[1]{0:T(128)} %bitcast.refs_0_, bf16[1408,128]{1,0:T(8,128)(2,1)S(1)} %collective-permute-done.3.refs_1_, bf16[4,224,128]{2,1,0:T(8,128)(2,1)S(1)} %all-to-all-done.refs_2_, ...), custom_call_target="tpu_custom_call" | custom-call | flops 100000000 | bytes 1000000 | tf_op jit(solution)/shard_map/pallas_call | solution.py:98
  52.4 20.0 %all-to-all-start.1 = ((bf16[32,48,128]{2,1,0:T(8,128)(2,1)}), bf16[32,48,128]{2,1,0:T(8,128)(2,1)S(1)}, u32[]{:S(2)}, u32[]{:S(2)}) async-start(bf16[32,48,128]{2,1,0:T(8,128)(2,1)} %get-tuple-element.31), calls=%async_computation.1 | async-start | bytes 786432 | tf_op jit(solution)/shard_map/all_to_all | solution.py:413
  72.4 1.9 %collective-permute-start.5 = (f32[128,128]{1,0:T(8,128)S(1)}, f32[128,128]{1,0:T(8,128)S(1)}, u32[]{:S(2)}, u32[]{:S(2)}) collective-permute-start(f32[128,128]{1,0:T(8,128)S(1)} %get-tuple-element.28), channel_id=1, source_target_pairs={{1,2},{3,4},{5,6},{7,8},{9,10},{11,12},{13,14},{15,16},{17,18},{19... | collective-permute-start | bytes 196616 | tf_op jit(solution)/shard_map/ppermute | solution.py:405
  74.3 1.9 %collective-permute-start.6 = (f32[128,128]{1,0:T(8,128)S(1)}, f32[128,128]{1,0:T(8,128)S(1)}, u32[]{:S(2)}, u32[]{:S(2)}) collective-permute-start(f32[128,128]{1,0:T(8,128)S(1)} %get-tuple-element.29), channel_id=1, source_target_pairs={{0,1},{1,0},{2,3},{3,2},{4,5},{5,4},{6,7},{7,6},{8,9},{9,8},{10,11... | collective-permute-start | bytes 196616 | tf_op jit(solution)/shard_map/ppermute | solution.py:409
  76.3 6.3 %all-to-all-done.1.refs_0_ = bf16[32,48,128]{2,1,0:T(8,128)(2,1)S(1)} async-done(((bf16[32,48,128]{2,1,0:T(8,128)(2,1)}), bf16[32,48,128]{2,1,0:T(8,128)(2,1)S(1)}, u32[]{:S(2)}, u32[]{:S(2)}) %all-to-all-start.1) | async-done | bytes 393248 | tf_op jit(solution)/shard_map/all_to_all | solution.py:413
  83.3 6.4 %all-to-all-start.2 = ((bf16[16,40,128]{2,1,0:T(8,128)(2,1)}), bf16[16,40,128]{2,1,0:T(8,128)(2,1)S(1)}, u32[]{:S(2)}, u32[]{:S(2)}) async-start(bf16[16,40,128]{2,1,0:T(8,128)(2,1)} %shard_map.170.refs_11_), calls=%async_computation.2 | async-start | bytes 327680 | tf_op jit(solution)/shard_map/all_to_all | solution.py:413
  90.3 6.1 %shard_map.171 = (bf16[1,128,1024]{2,1,0:T(8,128)(2,1)}, bf16[1,128,512]{2,1,0:T(8,128)(2,1)}, bf16[128,1024]{1,0:T(8,128)(2,1)}, f32[128,1024]{1,0:T(8,128)}, bf16[128,1024]{1,0:T(8,128)(2,1)}) custom-call(f32[128,128]{1,0:T(8,128)} %copy-done.9, f32[128,128]{1,0:T(8,128)} %copy-done.16, f32[128,128]{1,0:T(8,128)} %copy-done.17, bf16[100,1024]{1,0:T(8,128)(2,1)} %refs_2_.9, ...), custom_call_target="tpu_custom_call" | custom-call | flops 20000000000 | bytes 1000000 | tf_op jit(solution)/shard_map/pallas_call | solution.py:98
  96.4 4.1 %collective-permute-start.7 = (bf16[128,1024]{1,0:T(8,128)(2,1)}, bf16[128,1024]{1,0:T(8,128)(2,1)S(1)}, u32[]{:S(2)}, u32[]{:S(2)}) collective-permute-start(bf16[128,1024]{1,0:T(8,128)(2,1)} %get-tuple-element.35), channel_id=1, source_target_pairs={{1,2},{3,4},{5,6},{7,8},{9,10},{11,12},{13,14},{15,16},{17,18},{19... | collective-permute-start | bytes 786440 | tf_op jit(solution)/shard_map/ppermute | solution.py:405
  100.5 2.1 %collective-permute-start.8 = (bf16[128,1024]{1,0:T(8,128)(2,1)}, bf16[128,1024]{1,0:T(8,128)(2,1)S(1)}, u32[]{:S(2)}, u32[]{:S(2)}) collective-permute-start(bf16[128,1024]{1,0:T(8,128)(2,1)} %get-tuple-element.36), channel_id=1, source_target_pairs={{0,1},{1,0},{2,3},{3,2},{4,5},{5,4},{6,7},{7,6},{8,9},{9,8},{10,11... | collective-permute-start | bytes 786440 | tf_op jit(solution)/shard_map/ppermute | solution.py:409
  103.4 11.2 %all-to-all-start.3 = ((bf16[32,40,128]{2,1,0:T(8,128)(2,1)}), bf16[32,40,128]{2,1,0:T(8,128)(2,1)S(1)}, u32[]{:S(2)}, u32[]{:S(2)}) async-start(bf16[32,40,128]{2,1,0:T(8,128)(2,1)} %shard_map.173), calls=%async_computation.3 | async-start | bytes 655360 | tf_op jit(solution)/shard_map/all_to_all | solution.py:413
  115.5 8.6 %all-to-all-done.3.refs_1_ = bf16[32,40,128]{2,1,0:T(8,128)(2,1)S(1)} async-done(((bf16[32,40,128]{2,1,0:T(8,128)(2,1)}), bf16[32,40,128]{2,1,0:T(8,128)(2,1)S(1)}, u32[]{:S(2)}, u32[]{:S(2)}) %all-to-all-start.3) | async-done | bytes 327712 | tf_op jit(solution)/shard_map/all_to_all | solution.py:413
  124.1 0.9 shard_map.174
  (54 shorter events, 6.1 us)
Async XLA Ops:
  2.5 23.8 %collective-permute-start = (bf16[112,128]{1,0:T(8,128)(2,1)}, bf16[112,128]{1,0:T(8,128)(2,1)S(1)}, u32[]{:S(2)}, u32[]{:S(2)}) collective-permute-start(bf16[112,128]{1,0:T(8,128)(2,1)} %shard_map.163.refs_0_.refs_3_), channel_id=1, source_target_pairs={{0,256},{256,0},{1,257},{257,1},{2,258},{258,2},{3,259},{259,3},{4... | collective-permute-start | bytes 86024 | tf_op jit(solution)/shard_map/ppermute | solution.py:440
  18.8 13.3 %copy-start.18 = (s32[2,1]{0,1:T(1,128)S(1)}, s32[2,1]{0,1:T(1,128)}, u32[]{:S(2)}) copy-start(s32[2,1]{0,1:T(1,128)} %param.23) | copy-start | bytes 28
  18.8 13.4 %copy-start.10 = (s32[3,1024]{1,0:T(4,128)S(1)}, s32[3,1024]{1,0:T(4,128)}, u32[]{:S(2)}) copy-start(s32[3,1024]{1,0:T(4,128)} %refs_1_.7) | copy-start | bytes 36868
  18.8 13.4 %copy-start.11 = (f32[3,1024]{1,0:T(4,128)S(1)}, f32[3,1024]{1,0:T(4,128)}, u32[]{:S(2)}) copy-start(f32[3,1024]{1,0:T(4,128)} %refs_2_.7) | copy-start | bytes 36868
  18.8 13.3 %copy-start.12 = (f32[1024]{0:T(1024)S(1)}, f32[1024]{0:T(1024)}, u32[]{:S(2)}) copy-start(f32[1024]{0:T(1024)} %param.19) | copy-start | bytes 12292
  18.9 13.3 %copy-start.13 = (f32[100]{0:T(128)S(1)}, f32[100]{0:T(128)}, u32[]{:S(2)}) copy-start(f32[100]{0:T(128)} %param.20) | copy-start | bytes 1204
  20.7 12.2 %copy-start.4 = (bf16[1,128,512]{2,1,0:T(8,128)(2,1)S(1)}, bf16[1,128,512]{2,1,0:T(8,128)(2,1)}, u32[]{:S(2)}) copy-start(bf16[1,128,512]{2,1,0:T(8,128)(2,1)} %refs_6_.3) | copy-start | bytes 393220
  20.8 12.2 %copy-start.5 = (bf16[1,128,512]{2,1,0:T(8,128)(2,1)S(1)}, bf16[1,128,512]{2,1,0:T(8,128)(2,1)}, u32[]{:S(2)}) copy-start(bf16[1,128,512]{2,1,0:T(8,128)(2,1)} %refs_7_.1) | copy-start | bytes 393220
  20.8 12.2 %copy-start.7 = (bf16[1,128,512]{2,1,0:T(8,128)(2,1)S(1)}, bf16[1,128,512]{2,1,0:T(8,128)(2,1)}, u32[]{:S(2)}) copy-start(bf16[1,128,512]{2,1,0:T(8,128)(2,1)} %refs_5_.1) | copy-start | bytes 393220
  20.8 12.2 %collective-permute-start.2 = (bf16[128,2048]{1,0:T(8,128)(2,1)}, bf16[128,2048]{1,0:T(8,128)(2,1)S(1)}, u32[]{:S(2)}, u32[]{:S(2)}) collective-permute-start(bf16[128,2048]{1,0:T(8,128)(2,1)} %shard_map.165), channel_id=1, source_target_pairs={{1,2},{3,4},{5,6},{7,8},{9,10},{11,12},{13,14},{15,16},{17,18},{19... | collective-permute-start | bytes 1572872 | tf_op jit(solution)/shard_map/ppermute | solution.py:405
  24.4 8.6 %collective-permute-start.1 = (bf16[128,2048]{1,0:T(8,128)(2,1)}, bf16[128,2048]{1,0:T(8,128)(2,1)S(1)}, u32[]{:S(2)}, u32[]{:S(2)}) collective-permute-start(bf16[128,2048]{1,0:T(8,128)(2,1)} %shard_map.165), channel_id=1, source_target_pairs={{0,1},{1,0},{2,3},{3,2},{4,5},{5,4},{6,7},{7,6},{8,9},{9,8},{10,11... | collective-permute-start | bytes 1572872 | tf_op jit(solution)/shard_map/ppermute | solution.py:409
  27.9 9.6 %all-to-all-start = ((bf16[4,224,128]{2,1,0:T(8,128)(2,1)}), bf16[4,224,128]{2,1,0:T(8,128)(2,1)S(1)}, u32[]{:S(2)}, u32[]{:S(2)}) async-start(bf16[4,224,128]{2,1,0:T(8,128)(2,1)} %shard_map.164), calls=%async_computation | async-start | bytes 458752 | tf_op jit(solution)/shard_map/all_to_all | solution.py:413
  32.9 14.2 %copy-start.1 = (bf16[128,2048]{1,0:T(8,128)(2,1)}, bf16[128,2048]{1,0:T(8,128)(2,1)S(1)}, u32[]{:S(2)}) copy-start(bf16[128,2048]{1,0:T(8,128)(2,1)S(1)} %collective-permute-done.2.refs_6_.refs_5_.refs_10_.refs_8_) | copy-start | bytes 1572868
  33.0 14.2 %copy-start.2 = (bf16[128,2048]{1,0:T(8,128)(2,1)}, bf16[128,2048]{1,0:T(8,128)(2,1)S(1)}, u32[]{:S(2)}) copy-start(bf16[128,2048]{1,0:T(8,128)(2,1)S(1)} %collective-permute-done.1.refs_5_.refs_4_.refs_9_) | copy-start | bytes 1572868
  37.5 9.7 %collective-permute-start.4 = (bf16[1408,128]{1,0:T(8,128)(2,1)S(1)}, bf16[1408,128]{1,0:T(8,128)(2,1)S(1)}, u32[]{:S(2)}, u32[]{:S(2)}) collective-permute-start(bf16[1408,128]{1,0:T(8,128)(2,1)S(1)} %pad_maximum_fusion.refs_6_), channel_id=1, source_target_pairs={{1,2},{3,4},{5,6},{7,8},{9,10},{11,12},{13,14},{15,16},{17,18},{19... | collective-permute-start | bytes 1081352 | tf_op jit(solution)/shard_map/ppermute | solution.py:405
  42.1 5.1 %collective-permute-start.3 = (bf16[1408,128]{1,0:T(8,128)(2,1)S(1)}, bf16[1408,128]{1,0:T(8,128)(2,1)S(1)}, u32[]{:S(2)}, u32[]{:S(2)}) collective-permute-start(bf16[1408,128]{1,0:T(8,128)(2,1)S(1)} %pad_maximum_fusion.refs_6_), channel_id=1, source_target_pairs={{0,1},{1,0},{2,3},{3,2},{4,5},{5,4},{6,7},{7,6},{8,9},{9,8},{10,11... | collective-permute-start | bytes 1081352 | tf_op jit(solution)/shard_map/ppermute | solution.py:409
  52.4 30.1 %all-to-all-start.1 = ((bf16[32,48,128]{2,1,0:T(8,128)(2,1)}), bf16[32,48,128]{2,1,0:T(8,128)(2,1)S(1)}, u32[]{:S(2)}, u32[]{:S(2)}) async-start(bf16[32,48,128]{2,1,0:T(8,128)(2,1)} %get-tuple-element.31), calls=%async_computation.1 | async-start | bytes 786432 | tf_op jit(solution)/shard_map/all_to_all | solution.py:413
  72.4 17.3 %collective-permute-start.5 = (f32[128,128]{1,0:T(8,128)S(1)}, f32[128,128]{1,0:T(8,128)S(1)}, u32[]{:S(2)}, u32[]{:S(2)}) collective-permute-start(f32[128,128]{1,0:T(8,128)S(1)} %get-tuple-element.28), channel_id=1, source_target_pairs={{1,2},{3,4},{5,6},{7,8},{9,10},{11,12},{13,14},{15,16},{17,18},{19... | collective-permute-start | bytes 196616 | tf_op jit(solution)/shard_map/ppermute | solution.py:405
  74.3 15.4 %collective-permute-start.6 = (f32[128,128]{1,0:T(8,128)S(1)}, f32[128,128]{1,0:T(8,128)S(1)}, u32[]{:S(2)}, u32[]{:S(2)}) collective-permute-start(f32[128,128]{1,0:T(8,128)S(1)} %get-tuple-element.29), channel_id=1, source_target_pairs={{0,1},{1,0},{2,3},{3,2},{4,5},{5,4},{6,7},{7,6},{8,9},{9,8},{10,11... | collective-permute-start | bytes 196616 | tf_op jit(solution)/shard_map/ppermute | solution.py:409
  83.3 19.3 %all-to-all-start.2 = ((bf16[16,40,128]{2,1,0:T(8,128)(2,1)}), bf16[16,40,128]{2,1,0:T(8,128)(2,1)S(1)}, u32[]{:S(2)}, u32[]{:S(2)}) async-start(bf16[16,40,128]{2,1,0:T(8,128)(2,1)} %shard_map.170.refs_11_), calls=%async_computation.2 | async-start | bytes 327680 | tf_op jit(solution)/shard_map/all_to_all | solution.py:413
  96.4 18.2 %collective-permute-start.7 = (bf16[128,1024]{1,0:T(8,128)(2,1)}, bf16[128,1024]{1,0:T(8,128)(2,1)S(1)}, u32[]{:S(2)}, u32[]{:S(2)}) collective-permute-start(bf16[128,1024]{1,0:T(8,128)(2,1)} %get-tuple-element.35), channel_id=1, source_target_pairs={{1,2},{3,4},{5,6},{7,8},{9,10},{11,12},{13,14},{15,16},{17,18},{19... | collective-permute-start | bytes 786440 | tf_op jit(solution)/shard_map/ppermute | solution.py:405
  100.5 14.1 %copy-start.15 = (f32[128,1024]{1,0:T(8,128)S(1)}, f32[128,1024]{1,0:T(8,128)}, u32[]{:S(2)}) copy-start(f32[128,1024]{1,0:T(8,128)} %get-tuple-element.34.refs_0_) | copy-start | bytes 1572868
  100.5 14.1 %collective-permute-start.8 = (bf16[128,1024]{1,0:T(8,128)(2,1)}, bf16[128,1024]{1,0:T(8,128)(2,1)S(1)}, u32[]{:S(2)}, u32[]{:S(2)}) collective-permute-start(bf16[128,1024]{1,0:T(8,128)(2,1)} %get-tuple-element.36), channel_id=1, source_target_pairs={{0,1},{1,0},{2,3},{3,2},{4,5},{5,4},{6,7},{7,6},{8,9},{9,8},{10,11... | collective-permute-start | bytes 786440 | tf_op jit(solution)/shard_map/ppermute | solution.py:409
  103.4 20.8 %all-to-all-start.3 = ((bf16[32,40,128]{2,1,0:T(8,128)(2,1)}), bf16[32,40,128]{2,1,0:T(8,128)(2,1)S(1)}, u32[]{:S(2)}, u32[]{:S(2)}) async-start(bf16[32,40,128]{2,1,0:T(8,128)(2,1)} %shard_map.173), calls=%async_computation.3 | async-start | bytes 655360 | tf_op jit(solution)/shard_map/all_to_all | solution.py:413
  (8 other events, 37.6 us)

commit v9 on v8

--- a/solution.py
+++ b/solution.py
@@ -251,7 +251,7 @@
         out_ref[i] = sent.astype(BF16)
 
 
-def sum_body(in_ref, out_ref):
+def sum_body(in_ref, after_ref, out_ref):
     total = total_of(in_ref).astype(BF16)
     for i in range(NEAR_SIZE):
         out_ref[i] = total
@@ -539,8 +539,8 @@
     far_sums = call(
         sum_body,
         shape((NEAR_SIZE, SENT, VARS_LANE), BF16),
-        "v",
-        (along,),
+        "va",
+        (along, grad_query),
         cost=LONG,
     )
     everything = exchange(far_sums, NEAR)
@@ -550,7 +550,6 @@
         (shape((1, NODES, ATT), BF16), shape((1, NODES, ATT), BF16), flag),
         "lll",
         (kv_own, far_term, mate_term),
-        cost=LONG,
     )
     grad_wo, grad_dec = call(
         final_body,

time: 126 us -> 130 us (1.032)
  the two profiles are of different devices: /device:TPU:1 before, /device:TPU:2 now
where the time goes in v9:
time: 130 us; the launch traced here: 129 us
  starting transfers between devices  73.2 us (56%)
  waiting for transfers between devices  27.6 us (21%)
  Pallas kernels  23.8 us (18%)
  local copies, waits for them, and re-layouts  3.07 us (2%)
    all_to_all x4, starting transfers between devices, exchange(): return lax.all_to_all(x, axes, split_axis=0, concat_axis=0, tiled=True)  26.1 us
    pallas_call x12, Pallas kernels, call(): pl.pallas_call(kernel, out_shape=out_shape, in_specs=specs, scratch_shape...  23.8 us
    ppermute x4, starting transfers between devices, swap_far(): lax.ppermute(x, SPACE, pairs + [(target, source) for source, target in pa...  23.6 us
    ppermute x4, waiting for transfers between devices, swap_far(): lax.ppermute(x, SPACE, pairs + [(target, source) for source, target in pa...  19.2 us
    ppermute x1, starting transfers between devices, per_device(): other = lax.ppermute(proj, 'zh', [(0, 1), (1, 0)])  15.7 us
    all_to_all x4, waiting for transfers between devices, exchange(): return lax.all_to_all(x, axes, split_axis=0, concat_axis=0, tiled=True)  8.44 us
    ppermute x4, starting transfers between devices, swap_mate(): return lax.ppermute(x, 'c', [(0, 1), (1, 0)])  7.68 us
    unnamed x45, local copies, waits for them, and re-layouts  3.07 us
  transfers between devices with their start and end apart: 13, of which 5 were waited for; matrix products, arithmetic and copies ran while one was open for 0% of the time, Pallas kernels for 12%

profile of v9, /device:TPU:2, one launch (start us, length us, event | category | flops | bytes accessed | tf_op | source)
XLA Modules:
  0.0 128.7 jit_solution(2818439116262264872)
XLA Ops:
  0.6 1.9 %shard_map.163.refs_0_.refs_3_ = bf16[112,128]{1,0:T(8,128)(2,1)} custom-call(bf16[1,128,1024]{2,1,0:T(8,128)(2,1)} %refs_8_.1, bf16[100,1024]{1,0:T(8,128)(2,1)} %refs_2_.9), custom_call_target="tpu_custom_call" | custom-call | flops 100000000 | bytes 1000000 | tf_op jit(solution)/shard_map/pallas_call | solution.py:98
  2.5 15.7 %collective-permute-start = (bf16[112,128]{1,0:T(8,128)(2,1)}, bf16[112,128]{1,0:T(8,128)(2,1)S(1)}, u32[]{:S(2)}, u32[]{:S(2)}) collective-permute-start(bf16[112,128]{1,0:T(8,128)(2,1)} %shard_map.163.refs_0_.refs_3_), channel_id=1, source_target_pairs={{0,256},{256,0},{1,257},{257,1},{2,258},{258,2},{3,259},{259,3},{4... | collective-permute-start | bytes 86024 | tf_op jit(solution)/shard_map/ppermute | solution.py:440
  18.3 1.9 %shard_map.165 = bf16[128,2048]{1,0:T(8,128)(2,1)} custom-call(bf16[1,128,1024]{2,1,0:T(8,128)(2,1)} %refs_8_.1, bf16[1,128,512]{2,1,0:T(8,128)(2,1)} %refs_6_.3, bf16[1,128,512]{2,1,0:T(8,128)(2,1)} %refs_7_.1, bf16[112,128]{1,0:T(8,128)(2,1)} %shard_map.163.refs_0_.refs_3_), custom_call_target="tpu_custom_call" | custom-call | flops 100000000 | bytes 1000000 | tf_op jit(solution)/shard_map/pallas_call | solution.py:98
  20.2 4.9 %collective-permute-start.2 = (bf16[128,2048]{1,0:T(8,128)(2,1)}, bf16[128,2048]{1,0:T(8,128)(2,1)S(1)}, u32[]{:S(2)}, u32[]{:S(2)}) collective-permute-start(bf16[128,2048]{1,0:T(8,128)(2,1)} %shard_map.165), channel_id=1, source_target_pairs={{1,2},{3,4},{5,6},{7,8},{9,10},{11,12},{13,14},{15,16},{17,18},{19... | collective-permute-start | bytes 1572872 | tf_op jit(solution)/shard_map/ppermute | solution.py:405
  25.2 1.9 %collective-permute-start.1 = (bf16[128,2048]{1,0:T(8,128)(2,1)}, bf16[128,2048]{1,0:T(8,128)(2,1)S(1)}, u32[]{:S(2)}, u32[]{:S(2)}) collective-permute-start(bf16[128,2048]{1,0:T(8,128)(2,1)} %shard_map.165), channel_id=1, source_target_pairs={{0,1},{1,0},{2,3},{3,2},{4,5},{5,4},{6,7},{7,6},{8,9},{9,8},{10,11... | collective-permute-start | bytes 1572872 | tf_op jit(solution)/shard_map/ppermute | solution.py:409
  28.6 4.5 %all-to-all-start = ((bf16[4,224,128]{2,1,0:T(8,128)(2,1)}), bf16[4,224,128]{2,1,0:T(8,128)(2,1)S(1)}, u32[]{:S(2)}, u32[]{:S(2)}) async-start(bf16[4,224,128]{2,1,0:T(8,128)(2,1)} %shard_map.164), calls=%async_computation | async-start | bytes 458752 | tf_op jit(solution)/shard_map/all_to_all | solution.py:413
  34.0 5.2 %collective-permute-done.2.refs_6_.refs_5_.refs_10_.refs_8_ = bf16[128,2048]{1,0:T(8,128)(2,1)S(1)} collective-permute-done((bf16[128,2048]{1,0:T(8,128)(2,1)}, bf16[128,2048]{1,0:T(8,128)(2,1)S(1)}, u32[]{:S(2)}, u32[]{:S(2)}) %collective-permute-start.2) | collective-permute-done | bytes 524320 | tf_op jit(solution)/shard_map/ppermute | solution.py:405
  39.2 2.9 %shard_map.166.refs_7_ = bf16[4,128,128]{2,1,0:T(8,128)(2,1)S(1)} custom-call(s32[1]{0:T(128)} %bitcast.2.refs_0_, s32[2,1]{1,0:T(2,128)S(1)} %copy.18.refs_1_, bf16[1,128,512]{2,1,0:T(8,128)(2,1)S(1)} %copy-done.8, bf16[1,128,512]{2,1,0:T(8,128)(2,1)S(1)} %copy-done.4, bf16[1,128,512]{2,1,0:T(8,128)(2,1)S(1)} %copy-done.5, ...), custom_call_target="tpu_custom_call" | custom-call | flops 100000000 | bytes 1000000 | tf_op jit(solution)/shard_map/pallas_call | solution.py:98
  42.2 7.6 %collective-permute-start.4 = (bf16[1408,128]{1,0:T(8,128)(2,1)S(1)}, bf16[1408,128]{1,0:T(8,128)(2,1)S(1)}, u32[]{:S(2)}, u32[]{:S(2)}) collective-permute-start(bf16[1408,128]{1,0:T(8,128)(2,1)S(1)} %pad_maximum_fusion.refs_6_), channel_id=1, source_target_pairs={{1,2},{3,4},{5,6},{7,8},{9,10},{11,12},{13,14},{15,16},{17,18},{19... | collective-permute-start | bytes 1081352 | tf_op jit(solution)/shard_map/ppermute | solution.py:405
  49.7 1.9 %collective-permute-start.3 = (bf16[1408,128]{1,0:T(8,128)(2,1)S(1)}, bf16[1408,128]{1,0:T(8,128)(2,1)S(1)}, u32[]{:S(2)}, u32[]{:S(2)}) collective-permute-start(bf16[1408,128]{1,0:T(8,128)(2,1)S(1)} %pad_maximum_fusion.refs_6_), channel_id=1, source_target_pairs={{0,1},{1,0},{2,3},{3,2},{4,5},{5,4},{6,7},{7,6},{8,9},{9,8},{10,11... | collective-permute-start | bytes 1081352 | tf_op jit(solution)/shard_map/ppermute | solution.py:409
  51.7 1.7 %shard_map.168 = (f32[8,128,384]{2,1,0:T(8,128)S(1)}, f32[8,128]{1,0:T(8,128)S(1)}) custom-call(s32[1]{0:T(128)} %bitcast.2.refs_0_, s32[2,1]{1,0:T(2,128)S(1)} %copy.18.refs_1_, bf16[1,128,512]{2,1,0:T(8,128)(2,1)S(1)} %copy-done.8, bf16[1,128,512]{2,1,0:T(8,128)(2,1)S(1)} %copy-done.4, ...), custom_call_target="tpu_custom_call" | custom-call | flops 20000000000 | bytes 1000000 | tf_op jit(solution)/shard_map/pallas_call | solution.py:98
  53.4 5.2 %collective-permute-done.4.refs_3_ = bf16[1408,128]{1,0:T(8,128)(2,1)S(1)} collective-permute-done((bf16[1408,128]{1,0:T(8,128)(2,1)S(1)}, bf16[1408,128]{1,0:T(8,128)(2,1)S(1)}, u32[]{:S(2)}, u32[]{:S(2)}) %collective-permute-start.4) | collective-permute-done | bytes 360480 | tf_op jit(solution)/shard_map/ppermute | solution.py:405
  58.6 4.6 %shard_map.169 = (bf16[32,48,128]{2,1,0:T(8,128)(2,1)}, f32[128,128]{1,0:T(8,128)S(1)}, f32[128,128]{1,0:T(8,128)S(1)}, f32[128,128]{1,0:T(8,128)S(1)}) custom-call(s32[1]{0:T(128)} %bitcast.refs_0_, bf16[1408,128]{1,0:T(8,128)(2,1)S(1)} %collective-permute-done.3.refs_1_, bf16[4,224,128]{2,1,0:T(8,128)(2,1)S(1)} %all-to-all-done.refs_2_, ...), custom_call_target="tpu_custom_call" | custom-call | flops 100000000 | bytes 1000000 | tf_op jit(solution)/shard_map/pallas_call | solution.py:98
  63.8 7.7 %all-to-all-start.1 = ((bf16[32,48,128]{2,1,0:T(8,128)(2,1)}), bf16[32,48,128]{2,1,0:T(8,128)(2,1)S(1)}, u32[]{:S(2)}, u32[]{:S(2)}) async-start(bf16[32,48,128]{2,1,0:T(8,128)(2,1)} %get-tuple-element.31), calls=%async_computation.1 | async-start | bytes 786432 | tf_op jit(solution)/shard_map/all_to_all | solution.py:413
  71.5 6.7 %collective-permute-start.5 = (f32[128,128]{1,0:T(8,128)S(1)}, f32[128,128]{1,0:T(8,128)S(1)}, u32[]{:S(2)}, u32[]{:S(2)}) collective-permute-start(f32[128,128]{1,0:T(8,128)S(1)} %get-tuple-element.28), channel_id=1, source_target_pairs={{1,2},{3,4},{5,6},{7,8},{9,10},{11,12},{13,14},{15,16},{17,18},{19... | collective-permute-start | bytes 196616 | tf_op jit(solution)/shard_map/ppermute | solution.py:405
  78.2 1.9 %collective-permute-start.6 = (f32[128,128]{1,0:T(8,128)S(1)}, f32[128,128]{1,0:T(8,128)S(1)}, u32[]{:S(2)}, u32[]{:S(2)}) collective-permute-start(f32[128,128]{1,0:T(8,128)S(1)} %get-tuple-element.29), channel_id=1, source_target_pairs={{0,1},{1,0},{2,3},{3,2},{4,5},{5,4},{6,7},{7,6},{8,9},{9,8},{10,11... | collective-permute-start | bytes 196616 | tf_op jit(solution)/shard_map/ppermute | solution.py:409
  81.3 6.6 %all-to-all-start.2 = ((bf16[16,40,128]{2,1,0:T(8,128)(2,1)}), bf16[16,40,128]{2,1,0:T(8,128)(2,1)S(1)}, u32[]{:S(2)}, u32[]{:S(2)}) async-start(bf16[16,40,128]{2,1,0:T(8,128)(2,1)} %shard_map.170.refs_11_), calls=%async_computation.2 | async-start | bytes 327680 | tf_op jit(solution)/shard_map/all_to_all | solution.py:413
  88.6 6.1 %shard_map.171 = (bf16[1,128,1024]{2,1,0:T(8,128)(2,1)}, bf16[1,128,512]{2,1,0:T(8,128)(2,1)}, bf16[128,1024]{1,0:T(8,128)(2,1)}, f32[128,1024]{1,0:T(8,128)}, bf16[128,1024]{1,0:T(8,128)(2,1)}) custom-call(f32[128,128]{1,0:T(8,128)} %copy-done.10, f32[128,128]{1,0:T(8,128)} %copy-done.19, f32[128,128]{1,0:T(8,128)} %copy-done.20, ...), custom_call_target="tpu_custom_call" | custom-call | flops 20000000000 | bytes 1000000 | tf_op jit(solution)/shard_map/pallas_call | solution.py:98
  94.7 8.0 %all-to-all-done.2.refs_0_ = bf16[16,40,128]{2,1,0:T(8,128)(2,1)S(1)} async-done(((bf16[16,40,128]{2,1,0:T(8,128)(2,1)}), bf16[16,40,128]{2,1,0:T(8,128)(2,1)S(1)}, u32[]{:S(2)}, u32[]{:S(2)}) %all-to-all-start.2) | async-done | bytes 163872 | tf_op jit(solution)/shard_map/all_to_all | solution.py:413
  104.4 7.4 %all-to-all-start.3 = ((bf16[32,40,128]{2,1,0:T(8,128)(2,1)}), bf16[32,40,128]{2,1,0:T(8,128)(2,1)S(1)}, u32[]{:S(2)}, u32[]{:S(2)}) async-start(bf16[32,40,128]{2,1,0:T(8,128)(2,1)} %shard_map.173), calls=%async_computation.3 | async-start | bytes 655360 | tf_op jit(solution)/shard_map/all_to_all | solution.py:413
  111.8 4.4 %collective-permute-start.7 = (bf16[128,1024]{1,0:T(8,128)(2,1)S(1)}, bf16[128,1024]{1,0:T(8,128)(2,1)S(1)}, u32[]{:S(2)}, u32[]{:S(2)}) collective-permute-start(bf16[128,1024]{1,0:T(8,128)(2,1)S(1)} %copy-done.18), channel_id=1, source_target_pairs={{1,2},{3,4},{5,6},{7,8},{9,10},{11,12},{13,14},{15,16},{17,18},{19... | collective-permute-start | bytes 786440 | tf_op jit(solution)/shard_map/ppermute | solution.py:405
  116.2 1.9 %collective-permute-start.8 = (bf16[128,1024]{1,0:T(8,128)(2,1)S(1)}, bf16[128,1024]{1,0:T(8,128)(2,1)S(1)}, u32[]{:S(2)}, u32[]{:S(2)}) collective-permute-start(bf16[128,1024]{1,0:T(8,128)(2,1)S(1)} %copy-done.17), channel_id=1, source_target_pairs={{0,1},{1,0},{2,3},{3,2},{4,5},{5,4},{6,7},{7,6},{8,9},{9,8},{10,11... | collective-permute-start | bytes 786440 | tf_op jit(solution)/shard_map/ppermute | solution.py:409
  118.1 8.8 %collective-permute-done.7.refs_1_ = bf16[128,1024]{1,0:T(8,128)(2,1)S(1)} collective-permute-done((bf16[128,1024]{1,0:T(8,128)(2,1)S(1)}, bf16[128,1024]{1,0:T(8,128)(2,1)S(1)}, u32[]{:S(2)}, u32[]{:S(2)}) %collective-permute-start.7) | collective-permute-done | bytes 262176 | tf_op jit(solution)/shard_map/ppermute | solution.py:405
  127.8 0.9 shard_map.174
  (60 shorter events, 7.4 us)
Async XLA Ops:
  2.5 24.6 %collective-permute-start = (bf16[112,128]{1,0:T(8,128)(2,1)}, bf16[112,128]{1,0:T(8,128)(2,1)S(1)}, u32[]{:S(2)}, u32[]{:S(2)}) collective-permute-start(bf16[112,128]{1,0:T(8,128)(2,1)} %shard_map.163.refs_0_.refs_3_), channel_id=1, source_target_pairs={{0,256},{256,0},{1,257},{257,1},{2,258},{258,2},{3,259},{259,3},{4... | collective-permute-start | bytes 86024 | tf_op jit(solution)/shard_map/ppermute | solution.py:440
  18.3 15.0 %copy-start.11 = (s32[3,1024]{1,0:T(4,128)S(1)}, s32[3,1024]{1,0:T(4,128)}, u32[]{:S(2)}) copy-start(s32[3,1024]{1,0:T(4,128)} %refs_1_.7) | copy-start | bytes 36868
  18.3 14.9 %copy-start.12 = (f32[3,1024]{1,0:T(4,128)S(1)}, f32[3,1024]{1,0:T(4,128)}, u32[]{:S(2)}) copy-start(f32[3,1024]{1,0:T(4,128)} %refs_2_.7) | copy-start | bytes 36868
  20.2 18.9 %copy-start.4 = (bf16[1,128,512]{2,1,0:T(8,128)(2,1)S(1)}, bf16[1,128,512]{2,1,0:T(8,128)(2,1)}, u32[]{:S(2)}) copy-start(bf16[1,128,512]{2,1,0:T(8,128)(2,1)} %refs_6_.3) | copy-start | bytes 393220
  20.2 18.9 %copy-start.5 = (bf16[1,128,512]{2,1,0:T(8,128)(2,1)S(1)}, bf16[1,128,512]{2,1,0:T(8,128)(2,1)}, u32[]{:S(2)}) copy-start(bf16[1,128,512]{2,1,0:T(8,128)(2,1)} %refs_7_.1) | copy-start | bytes 393220
  20.2 18.9 %copy-start.8 = (bf16[1,128,512]{2,1,0:T(8,128)(2,1)S(1)}, bf16[1,128,512]{2,1,0:T(8,128)(2,1)}, u32[]{:S(2)}) copy-start(bf16[1,128,512]{2,1,0:T(8,128)(2,1)} %refs_5_.1) | copy-start | bytes 393220
  20.2 18.9 %collective-permute-start.2 = (bf16[128,2048]{1,0:T(8,128)(2,1)}, bf16[128,2048]{1,0:T(8,128)(2,1)S(1)}, u32[]{:S(2)}, u32[]{:S(2)}) collective-permute-start(bf16[128,2048]{1,0:T(8,128)(2,1)} %shard_map.165), channel_id=1, source_target_pairs={{1,2},{3,4},{5,6},{7,8},{9,10},{11,12},{13,14},{15,16},{17,18},{19... | collective-permute-start | bytes 1572872 | tf_op jit(solution)/shard_map/ppermute | solution.py:405
  25.2 14.0 %collective-permute-start.1 = (bf16[128,2048]{1,0:T(8,128)(2,1)}, bf16[128,2048]{1,0:T(8,128)(2,1)S(1)}, u32[]{:S(2)}, u32[]{:S(2)}) collective-permute-start(bf16[128,2048]{1,0:T(8,128)(2,1)} %shard_map.165), channel_id=1, source_target_pairs={{0,1},{1,0},{2,3},{3,2},{4,5},{5,4},{6,7},{7,6},{8,9},{9,8},{10,11... | collective-permute-start | bytes 1572872 | tf_op jit(solution)/shard_map/ppermute | solution.py:409
  28.6 13.5 %all-to-all-start = ((bf16[4,224,128]{2,1,0:T(8,128)(2,1)}), bf16[4,224,128]{2,1,0:T(8,128)(2,1)S(1)}, u32[]{:S(2)}, u32[]{:S(2)}) async-start(bf16[4,224,128]{2,1,0:T(8,128)(2,1)} %shard_map.164), calls=%async_computation | async-start | bytes 458752 | tf_op jit(solution)/shard_map/all_to_all | solution.py:413
  39.1 19.4 %copy-start.1 = (bf16[128,2048]{1,0:T(8,128)(2,1)}, bf16[128,2048]{1,0:T(8,128)(2,1)S(1)}, u32[]{:S(2)}) copy-start(bf16[128,2048]{1,0:T(8,128)(2,1)S(1)} %collective-permute-done.2.refs_6_.refs_5_.refs_10_.refs_8_) | copy-start | bytes 1572868
  39.2 19.4 %copy-start.2 = (bf16[128,2048]{1,0:T(8,128)(2,1)}, bf16[128,2048]{1,0:T(8,128)(2,1)S(1)}, u32[]{:S(2)}) copy-start(bf16[128,2048]{1,0:T(8,128)(2,1)S(1)} %collective-permute-done.1.refs_5_.refs_4_.refs_9_) | copy-start | bytes 1572868
  42.1 16.4 %copy-start = (bf16[1,128,1024]{2,1,0:T(8,128)(2,1)S(1)}, bf16[1,128,1024]{2,1,0:T(8,128)(2,1)}, u32[]{:S(2)}) copy-start(bf16[1,128,1024]{2,1,0:T(8,128)(2,1)} %refs_8_.1) | copy-start | bytes 786436
  42.2 16.4 %copy-start.7 = (f32[100,1024]{1,0:T(8,128)S(1)}, f32[100,1024]{1,0:T(8,128)}, u32[]{:S(2)}) copy-start(f32[100,1024]{1,0:T(8,128)} %refs_6_.2) | copy-start | bytes 1228804
  42.2 16.4 %collective-permute-start.4 = (bf16[1408,128]{1,0:T(8,128)(2,1)S(1)}, bf16[1408,128]{1,0:T(8,128)(2,1)S(1)}, u32[]{:S(2)}, u32[]{:S(2)}) collective-permute-start(bf16[1408,128]{1,0:T(8,128)(2,1)S(1)} %pad_maximum_fusion.refs_6_), channel_id=1, source_target_pairs={{1,2},{3,4},{5,6},{7,8},{9,10},{11,12},{13,14},{15,16},{17,18},{19... | collective-permute-start | bytes 1081352 | tf_op jit(solution)/shard_map/ppermute | solution.py:405
  49.7 8.8 %collective-permute-start.3 = (bf16[1408,128]{1,0:T(8,128)(2,1)S(1)}, bf16[1408,128]{1,0:T(8,128)(2,1)S(1)}, u32[]{:S(2)}, u32[]{:S(2)}) collective-permute-start(bf16[1408,128]{1,0:T(8,128)(2,1)S(1)} %pad_maximum_fusion.refs_6_), channel_id=1, source_target_pairs={{0,1},{1,0},{2,3},{3,2},{4,5},{5,4},{6,7},{7,6},{8,9},{9,8},{10,11... | collective-permute-start | bytes 1081352 | tf_op jit(solution)/shard_map/ppermute | solution.py:409
  63.8 16.7 %all-to-all-start.1 = ((bf16[32,48,128]{2,1,0:T(8,128)(2,1)}), bf16[32,48,128]{2,1,0:T(8,128)(2,1)S(1)}, u32[]{:S(2)}, u32[]{:S(2)}) async-start(bf16[32,48,128]{2,1,0:T(8,128)(2,1)} %get-tuple-element.31), calls=%async_computation.1 | async-start | bytes 786432 | tf_op jit(solution)/shard_map/all_to_all | solution.py:413
  71.5 16.5 %collective-permute-start.5 = (f32[128,128]{1,0:T(8,128)S(1)}, f32[128,128]{1,0:T(8,128)S(1)}, u32[]{:S(2)}, u32[]{:S(2)}) collective-permute-start(f32[128,128]{1,0:T(8,128)S(1)} %get-tuple-element.28), channel_id=1, source_target_pairs={{1,2},{3,4},{5,6},{7,8},{9,10},{11,12},{13,14},{15,16},{17,18},{19... | collective-permute-start | bytes 196616 | tf_op jit(solution)/shard_map/ppermute | solution.py:405
  78.2 9.8 %collective-permute-start.6 = (f32[128,128]{1,0:T(8,128)S(1)}, f32[128,128]{1,0:T(8,128)S(1)}, u32[]{:S(2)}, u32[]{:S(2)}) collective-permute-start(f32[128,128]{1,0:T(8,128)S(1)} %get-tuple-element.29), channel_id=1, source_target_pairs={{0,1},{1,0},{2,3},{3,2},{4,5},{5,4},{6,7},{7,6},{8,9},{9,8},{10,11... | collective-permute-start | bytes 196616 | tf_op jit(solution)/shard_map/ppermute | solution.py:409
  81.3 21.4 %all-to-all-start.2 = ((bf16[16,40,128]{2,1,0:T(8,128)(2,1)}), bf16[16,40,128]{2,1,0:T(8,128)(2,1)S(1)}, u32[]{:S(2)}, u32[]{:S(2)}) async-start(bf16[16,40,128]{2,1,0:T(8,128)(2,1)} %shard_map.170.refs_11_), calls=%async_computation.2 | async-start | bytes 327680 | tf_op jit(solution)/shard_map/all_to_all | solution.py:413
  103.6 23.4 %copy-start.6 = (f32[128,1024]{1,0:T(8,128)S(1)}, f32[128,1024]{1,0:T(8,128)}, u32[]{:S(2)}) copy-start(f32[128,1024]{1,0:T(8,128)} %get-tuple-element.34.refs_0_) | copy-start | bytes 1572868
  104.4 23.5 %copy-start.3 = (bf16[100,1024]{1,0:T(8,128)(2,1)S(1)}, bf16[100,1024]{1,0:T(8,128)(2,1)}, u32[]{:S(2)}) copy-start(bf16[100,1024]{1,0:T(8,128)(2,1)} %refs_2_.9) | copy-start | bytes 614404
  104.4 23.5 %all-to-all-start.3 = ((bf16[32,40,128]{2,1,0:T(8,128)(2,1)}), bf16[32,40,128]{2,1,0:T(8,128)(2,1)S(1)}, u32[]{:S(2)}, u32[]{:S(2)}) async-start(bf16[32,40,128]{2,1,0:T(8,128)(2,1)} %shard_map.173), calls=%async_computation.3 | async-start | bytes 655360 | tf_op jit(solution)/shard_map/all_to_all | solution.py:413
  111.8 15.2 %collective-permute-start.7 = (bf16[128,1024]{1,0:T(8,128)(2,1)S(1)}, bf16[128,1024]{1,0:T(8,128)(2,1)S(1)}, u32[]{:S(2)}, u32[]{:S(2)}) collective-permute-start(bf16[128,1024]{1,0:T(8,128)(2,1)S(1)} %copy-done.18), channel_id=1, source_target_pairs={{1,2},{3,4},{5,6},{7,8},{9,10},{11,12},{13,14},{15,16},{17,18},{19... | collective-permute-start | bytes 786440 | tf_op jit(solution)/shard_map/ppermute | solution.py:405
  116.2 10.8 %collective-permute-start.8 = (bf16[128,1024]{1,0:T(8,128)(2,1)S(1)}, bf16[128,1024]{1,0:T(8,128)(2,1)S(1)}, u32[]{:S(2)}, u32[]{:S(2)}) collective-permute-start(bf16[128,1024]{1,0:T(8,128)(2,1)S(1)} %copy-done.17), channel_id=1, source_target_pairs={{0,1},{1,0},{2,3},{3,2},{4,5},{5,4},{6,7},{7,6},{8,9},{9,8},{10,11... | collective-permute-start | bytes 786440 | tf_op jit(solution)/shard_map/ppermute | solution.py:409
  (11 other events, 78.8 us)
